TPU v7x, 128 devices: a whole 4x4x4 slice. The times are simulated.
128 devices in a mesh: ctx: 16 (over y, z_hi, core), fsdp: 8 (over z_lo, x).
Axes of the slice: x: 4, y: 4, z: 4 (z_hi: 2, z_lo: 2; z = z_hi * 2 + z_lo), core: 2. Of those that a mesh axis runs over, the one named last changes fastest.
Arguments:
- decoder_in: bfloat16 [8, 2048, 768], P('fsdp', 'ctx'), may hold values from -6 to 6
- encoder_states: bfloat16 [8, 1024, 768], P('fsdp', 'ctx'), may hold values from -6 to 6
- out_grad: bfloat16 [8, 2048, 768], P('fsdp', 'ctx'), may hold values from -6 to 6
- block_pairs: int32 [16], replicated, may hold values from 0 to 15, each once
- bucket_table: int32 [128], replicated, may hold values from 0 to 31, as said below
- gain_self: bfloat16 [768], P('fsdp'), may hold values from 0.25 to 1.75
- self_query: bfloat16 [768, 768], P('fsdp'), may hold values from -0.078125 to 0.078125
- self_key: bfloat16 [768, 768], P('fsdp'), may hold values from -0.078125 to 0.078125
- self_value: bfloat16 [768, 768], P('fsdp'), may hold values from -0.21875 to 0.21875
- self_out: bfloat16 [768, 768], P('fsdp'), may hold values from -2.5 to 2.5
- position_bias: bfloat16 [32, 12], P('fsdp'), may hold values from -4 to 4
- gain_cross: bfloat16 [768], P('fsdp'), may hold values from 0.25 to 1.75
- cross_query: bfloat16 [768, 768], P('fsdp'), may hold values from -0.078125 to 0.078125
- cross_key: bfloat16 [768, 768], P('fsdp'), may hold values from -0.078125 to 0.078125
- cross_value: bfloat16 [768, 768], P('fsdp'), may hold values from -0.21875 to 0.21875
- cross_out: bfloat16 [768, 768], P('fsdp'), may hold values from -3.5 to 3.5
- gain_feed: bfloat16 [768], P('fsdp'), may hold values from 0.25 to 1.75
- feed_gate: bfloat16 [768, 2048], P('fsdp'), may hold values from -0.21875 to 0.21875
- feed_up: bfloat16 [768, 2048], P('fsdp'), may hold values from -0.21875 to 0.21875
- feed_down: bfloat16 [2048, 768], P('fsdp'), may hold values from -0.125 to 0.125
Outputs:
- block_out: float32 [8, 2048, 768], P('fsdp', 'ctx')
- grad_decoder: float32 [8, 2048, 768], P('fsdp', 'ctx')
- grad_encoder: float32 [8, 1024, 768], P('fsdp', 'ctx')
- grad_gain_self: float32 [768], P('fsdp')
- grad_self_query: float32 [768, 768], P('fsdp')
- grad_self_key: float32 [768, 768], P('fsdp')
- grad_self_value: float32 [768, 768], P('fsdp')
- grad_self_out: float32 [768, 768], P('fsdp')
- grad_position_bias: float32 [32, 12], P('fsdp')
- grad_gain_cross: float32 [768], P('fsdp')
- grad_cross_query: float32 [768, 768], P('fsdp')
- grad_cross_key: float32 [768, 768], P('fsdp')
- grad_cross_value: float32 [768, 768], P('fsdp')
- grad_cross_out: float32 [768, 768], P('fsdp')
- grad_gain_feed: float32 [768], P('fsdp')
- grad_feed_gate: float32 [768, 2048], P('fsdp')
- grad_feed_up: float32 [768, 2048], P('fsdp')
- grad_feed_down: float32 [2048, 768], P('fsdp')
Inputs may be any that keep to these rules, and one draw needn't show every extreme that they name: block_pairs is a permutation of 0 to 15. `bucket_table`: entry n is the bucket of distance n (distances of 127 and more use the last entry); it never falls along n, is 0 at n = 0 and 31 at n = 127.
All inputs are finite; a program needn't handle non-finite values.
Results may differ from a plain program's by a relative error of at most 0.03.
Values may be sent and summed in bfloat16 or wider, within the bound.
A program may use at most 192 MiB of HBM per device.

v0:
```python
import functools

import jax
import jax.numpy as jnp
from jax import lax
from jax.experimental import pallas as pl
from jax.experimental.pallas import tpu as pltpu
from jax.sharding import PartitionSpec as P

D = 768
FF = 2048
HEADS = 12
HEAD_DIM = 64
PAIRS = HEADS // 2
N_CTX = 16
TOK = 128
ENC = 64
HALF = 64
REACH = 128
BF = jnp.bfloat16
F32 = jnp.float32
MIB = 1024 * 1024


def ctx_place():
    me = lax.axis_index("ctx")
    core = me % 2
    high = (me // 2) % 2
    y = me // 4
    return me, core, high, y


def slot_of(y, shift, high, core):
    return ((y + shift) % 4) * 4 + 2 * high + core


def greet(devices):
    barrier = pltpu.get_barrier_semaphore()
    for device in devices:
        pl.semaphore_signal(barrier, inc=1, device_id={"ctx": device})
    pl.semaphore_wait(barrier, len(devices))


def remote(src, dst, send_sem, recv_sem, device):
    return pltpu.make_async_remote_copy(
        src_ref=src, dst_ref=dst, send_sem=send_sem, recv_sem=recv_sem, device_id={"ctx": device}
    )


def gather_kernel(x_ref, out_ref, send_sem, recv_sem, local_sem):
    me, core, high, y = ctx_place()
    sibling = slot_of(y, 0, high, 1 - core)
    across = slot_of(y, 0, 1 - high, core)
    rows = [slot_of(y, shift, high, core) for shift in (1, 2, 3)]
    greet([sibling, across] + rows)
    sends = []

    def send(src, slot, device):
        copy = remote(src, out_ref.at[slot], send_sem.at[len(sends)], recv_sem.at[slot], device)
        copy.start()
        sends.append(copy)

    def arrived(slot):
        remote(x_ref, out_ref.at[slot], send_sem.at[0], recv_sem.at[slot], sibling).wait_recv()

    send(x_ref, me, across)
    for device in rows:
        send(x_ref, me, device)
    send(x_ref, me, sibling)
    own = pltpu.make_async_copy(x_ref, out_ref.at[me], local_sem)
    own.start()
    arrived(across)
    for device in rows:
        send(out_ref.at[across], across, device)
    send(out_ref.at[across], across, sibling)
    for shift in (1, 3, 2):
        slot = slot_of(y, shift, high, core)
        arrived(slot)
        send(out_ref.at[slot], slot, sibling)
    for shift in (1, 3, 2):
        slot = slot_of(y, shift, 1 - high, core)
        arrived(slot)
        send(out_ref.at[slot], slot, sibling)
    for shift in range(4):
        for other in range(2):
            arrived(slot_of(y, shift, other, 1 - core))
    own.wait()
    for copy in sends:
        copy.wait_send()


def ctx_gather(x, collective_id):
    return pl.pallas_call(
        gather_kernel,
        out_shape=jax.ShapeDtypeStruct((N_CTX,) + x.shape, x.dtype),
        in_specs=[pl.BlockSpec(memory_space=pl.ANY)],
        out_specs=pl.BlockSpec(memory_space=pl.ANY),
        scratch_shapes=[
            pltpu.SemaphoreType.DMA((15,)),
            pltpu.SemaphoreType.DMA((N_CTX,)),
            pltpu.SemaphoreType.DMA,
        ],
        compiler_params=pltpu.CompilerParams(collective_id=collective_id, has_side_effects=True),
        name="ctx_gather",
    )(x)


def scatter_kernel(
    x_ref, out_ref, from_core, kept, from_row, stage, from_high,
    send_a, recv_a, send_b, recv_b, send_c, recv_c,
):
    me, core, high, y = ctx_place()
    sibling = slot_of(y, 0, high, 1 - core)
    across = slot_of(y, 0, 1 - high, core)
    rows = [slot_of(y, shift, high, core) for shift in (1, 2, 3)]
    greet([sibling, across] + rows)
    order = [(shift, half) for shift in (2, 1, 3, 0) for half in range(2)]
    first = []
    for index, (shift, half) in enumerate(order):
        copy = remote(
            x_ref.at[slot_of(y, shift, half, 1 - core)],
            from_core.at[index],
            send_a.at[index],
            recv_a.at[index],
            sibling,
        )
        copy.start()
        first.append(copy)
    second = []
    for index, (shift, half) in enumerate(order):
        first[index].wait_recv()
        mine = x_ref[slot_of(y, shift, half, core)].astype(F32)
        kept[index] = (mine + from_core[index].astype(F32)).astype(BF)
        if half == 1 and shift:
            spot = index // 2
            copy = remote(
                kept.at[pl.ds(index - 1, 2)],
                from_row.at[spot],
                send_b.at[spot],
                recv_b.at[spot],
                rows[shift - 1],
            )
            copy.start()
            second.append(copy)
    for copy in second:
        copy.wait_recv()

    def total(half):
        result = kept[6 + half].astype(F32)
        for spot in range(3):
            result = result + from_row[spot, half].astype(F32)
        return result

    stage[...] = total(1 - high).astype(BF)
    last = remote(stage, from_high, send_c, recv_c, across)
    last.start()
    mine = total(high)
    last.wait_recv()
    out_ref[...] = (mine + from_high[...].astype(F32)).astype(BF)
    last.wait_send()
    for copy in first + second:
        copy.wait_send()


def ctx_scatter(x, collective_id):
    block = x.shape[1:]
    return pl.pallas_call(
        scatter_kernel,
        out_shape=jax.ShapeDtypeStruct(block, x.dtype),
        in_specs=[pl.BlockSpec(memory_space=pltpu.VMEM)],
        out_specs=pl.BlockSpec(memory_space=pltpu.VMEM),
        scratch_shapes=[
            pltpu.VMEM((8,) + block, BF),
            pltpu.VMEM((8,) + block, BF),
            pltpu.VMEM((3, 2) + block, BF),
            pltpu.VMEM(block, BF),
            pltpu.VMEM(block, BF),
            pltpu.SemaphoreType.DMA((8,)),
            pltpu.SemaphoreType.DMA((8,)),
            pltpu.SemaphoreType.DMA((3,)),
            pltpu.SemaphoreType.DMA((3,)),
            pltpu.SemaphoreType.DMA,
            pltpu.SemaphoreType.DMA,
        ],
        compiler_params=pltpu.CompilerParams(
            collective_id=collective_id, has_side_effects=True, vmem_limit_bytes=40 * MIB
        ),
        name="ctx_scatter",
    )(x)


def torus_place():
    me, core, high, y = ctx_place()
    shard = lax.axis_index("fsdp")
    return me, core, high, y, shard // 4, shard % 4


def hop(src, dst, send_sem, recv_sem, ctx, fsdp):
    return pltpu.make_async_remote_copy(
        src_ref=src,
        dst_ref=dst,
        send_sem=send_sem,
        recv_sem=recv_sem,
        device_id={"ctx": ctx, "fsdp": fsdp},
    )


def greet_all(devices):
    barrier = pltpu.get_barrier_semaphore()
    for ctx, fsdp in devices:
        pl.semaphore_signal(barrier, inc=1, device_id={"ctx": ctx, "fsdp": fsdp})
    pl.semaphore_wait(barrier, len(devices))


def weights_kernel(count, *refs):
    sources = refs[:count]
    targets = refs[count : 2 * count]
    send_sem, x_sem, z_sem, core_sem, local_sem = refs[2 * count :]
    me, core, high, y, low, x = torus_place()
    shard = low * 4 + x
    sibling = (slot_of(y, 0, high, 1 - core), shard)
    inside = (me, (1 - low) * 4 + x)
    outside = (slot_of(y, 0, 1 - high, core), (1 - low) * 4 + x)
    others = [low * 4 + (x + shift) % 4 for shift in (1, 2, 3)]
    greet_all([sibling, inside, outside] + [(me, other) for other in others])

    def part(index, owner, whose, side=None):
        ref = targets[index]
        rows = ref.shape[1] // 2
        start = pl.multiple_of(whose * rows, 16)
        if side is None:
            return ref.at[owner, pl.ds(start, rows), :]
        width = ref.shape[2] // 2
        return ref.at[owner, pl.ds(start, rows), pl.ds(side * width, width)]

    def mine(index, side=None):
        ref = sources[index]
        rows = ref.shape[0] // 2
        start = pl.multiple_of(core * rows, 16)
        if side is None:
            return ref.at[pl.ds(start, rows), :]
        width = ref.shape[1] // 2
        return ref.at[pl.ds(start, rows), pl.ds(side * width, width)]

    sends = []

    def send(index, src, dst, recv_sem, device):
        copy = hop(src, dst, send_sem.at[len(sends)], recv_sem, *device)
        copy.start()
        sends.append(copy)

    def arrived(index, ref, recv_sem):
        hop(ref, ref, send_sem.at[0], recv_sem, *sibling).wait_recv()

    for index in range(count):
        for spot in (1, 0, 2):
            send(index, mine(index), part(index, shard, core), x_sem.at[index, spot], (me, others[spot]))
        for side, device in enumerate((inside, outside)):
            send(
                index, mine(index, side), part(index, shard, core, side), z_sem.at[index, 3, side], device
            )
    own = []
    for index in range(count):
        copy = pltpu.make_async_copy(sources[index], targets[index].at[shard], local_sem.at[index])
        copy.start()
        own.append(copy)
    for index in range(count):
        for spot in (0, 2, 1):
            owner = low * 4 + (x + 3 - spot) % 4
            block = part(index, owner, core)
            arrived(index, block, x_sem.at[index, spot])
            for side, device in enumerate((inside, outside)):
                piece = part(index, owner, core, side)
                send(index, piece, piece, z_sem.at[index, spot, side], device)
            send(index, block, block, core_sem.at[index, spot], sibling)
        for spot in (3, 0, 2, 1):
            owner = (1 - low) * 4 + (x + 3 - spot) % 4
            for side in range(2):
                piece = part(index, owner, core, side)
                arrived(index, piece, z_sem.at[index, spot, side])
                send(index, piece, piece, core_sem.at[index, 3 + 2 * spot + side], sibling)
    for index in range(count):
        for spot in range(3):
            owner = low * 4 + (x + 3 - spot) % 4
            arrived(index, part(index, owner, 1 - core), core_sem.at[index, spot])
        for spot in range(4):
            owner = (1 - low) * 4 + (x + 3 - spot) % 4
            for side in range(2):
                piece = part(index, owner, 1 - core, side)
                arrived(index, piece, core_sem.at[index, 3 + 2 * spot + side])
    for copy in own:
        copy.wait()
    for copy in sends:
        copy.wait_send()


def gather_weights(packs, collective_id):
    count = len(packs)
    return pl.pallas_call(
        functools.partial(weights_kernel, count),
        out_shape=[jax.ShapeDtypeStruct((8,) + pack.shape, pack.dtype) for pack in packs],
        in_specs=[pl.BlockSpec(memory_space=pl.ANY)] * count,
        out_specs=[pl.BlockSpec(memory_space=pl.ANY)] * count,
        scratch_shapes=[
            pltpu.SemaphoreType.DMA((22 * count,)),
            pltpu.SemaphoreType.DMA((count, 3)),
            pltpu.SemaphoreType.DMA((count, 4, 2)),
            pltpu.SemaphoreType.DMA((count, 11)),
            pltpu.SemaphoreType.DMA((count,)),
        ],
        compiler_params=pltpu.CompilerParams(collective_id=collective_id, has_side_effects=True),
        name="gather_weights",
    )(*packs)


PIECE = 48
ROOM = D + FF // 4 + FF // 8 + 128


def reduce_kernel(widths, *refs):
    count = len(widths)
    parts = refs[:count]
    wide_ref, down_ref, out_ref = refs[count : count + 3]
    (
        from_core, kept, from_z, held, from_x, wide_in, down_in, packed, from_ctx, total_ref,
        core_send, core_recv, z_send, z_recv, x_send, x_recv,
        ctx_send, ctx_recv, out_send, out_recv, pass_send, pass_recv, local_sem,
    ) = refs[count + 3 :]
    me, core, high, y, low, x = torus_place()
    shard = low * 4 + x
    rank = y * 2 + high
    sibling = (slot_of(y, 0, high, 1 - core), shard)
    inside = (me, (1 - low) * 4 + x)
    outside = (slot_of(y, 0, 1 - high, core), (1 - low) * 4 + x)
    others = [low * 4 + (x + shift) % 4 for shift in (1, 2, 3)]
    shifts = [(dy, dz) for dy in range(4) for dz in range(2)][1:]
    mates = [((y + dy) % 4) * 2 + (high + dz) % 2 for dy, dz in shifts]
    greet_all(
        [sibling, inside, outside]
        + [(me, other) for other in others]
        + [(mate * 2 + core, shard) for mate in mates]
    )
    mine = pl.ds(pl.multiple_of(core * PIECE, 16), PIECE)
    theirs = pl.ds(pl.multiple_of((1 - core) * PIECE, 16), PIECE)
    mine_down = pl.ds(pl.multiple_of(core * 128, 16), 128)
    theirs_down = pl.ds(pl.multiple_of((1 - core) * 128, 16), 128)
    starts = [sum(widths[:k]) for k in range(count)]
    cuts = [pl.ds(starts[k], widths[k]) for k in range(count)]
    sends = []

    def go(src, dst, send_sem, recv_sem, device):
        copy = hop(src, dst, send_sem, recv_sem, *device)
        copy.start()
        sends.append(copy)
        return copy

    over_core = [
        go(
            parts[k].at[:, theirs, :],
            from_core.at[:, :, cuts[k]],
            core_send.at[k],
            core_recv.at[k],
            sibling,
        )
        for k in range(count)
    ]
    wide_copy = go(wide_ref.at[theirs, :], wide_in, core_send.at[count], core_recv.at[count], sibling)
    down_copy = go(
        down_ref.at[theirs_down, :], down_in, core_send.at[count + 1], core_recv.at[count + 1], sibling
    )
    over_z = [None] * count
    over_x = [None] * count

    def step_core(k):
        over_core[k].wait_recv()
        half = widths[k] // 2
        away = pl.ds(4 * (1 - low), 4)
        for owner in range(8):
            kept[owner, :, cuts[k]] = (
                parts[k][owner, mine, :].astype(F32) + from_core[owner, :, cuts[k]].astype(F32)
            ).astype(BF)
        over_z[k] = [
            go(
                kept.at[away, :, pl.ds(starts[k] + side * half, half)],
                from_z.at[:, :, pl.ds(starts[k] + side * half, half)],
                z_send.at[k, side],
                z_recv.at[k, side],
                device,
            )
            for side, device in enumerate((inside, outside))
        ]

    def step_z(k):
        for copy in over_z[k]:
            copy.wait_recv()
        for column in range(4):
            held[column, :, cuts[k]] = (
                kept[4 * low + column, :, cuts[k]].astype(F32) + from_z[column, :, cuts[k]].astype(F32)
            ).astype(BF)
        over_x[k] = [
            go(
                held.at[(x + spot + 1) % 4, :, cuts[k]],
                from_x.at[spot, :, cuts[k]],
                x_send.at[k, spot],
                x_recv.at[k, spot],
                (me, others[spot]),
            )
            for spot in (1, 0, 2)
        ]

    def step_x(k):
        for copy in over_x[k]:
            copy.wait_recv()
        total = held[x, :, cuts[k]].astype(F32)
        for spot in range(3):
            total = total + from_x[spot, :, cuts[k]].astype(F32)
        total = total.astype(BF)
        if widths[k] % D:
            packed[0, :, ROOM - 128 :] = total[:, :128]
            for piece in range(1, 8):
                packed[piece, :, ROOM - 128 :] = jnp.zeros((PIECE, 128), BF)
            return
        for piece in range(widths[k] // D):
            packed[starts[k] // D + piece, :, :D] = total[:, piece * D : (piece + 1) * D]

    for k in range(count + 2):
        if k < count:
            step_core(k)
        if 0 <= k - 1 < count:
            step_z(k - 1)
        if k - 2 >= 0:
            step_x(k - 2)
        if k == 1:
            wide_copy.wait_recv()
            for piece in range(8):
                cut = slice(piece * 512, piece * 512 + 512)
                packed[piece, :, D : D + 512] = (
                    wide_ref[mine, cut].astype(F32) + wide_in[:, cut].astype(F32)
                ).astype(BF)
            down_copy.wait_recv()
            total = (down_ref[mine_down, :].astype(F32) + down_in[...].astype(F32)).astype(BF)
            for piece in range(8):
                for part in range(3):
                    packed[piece, part * 16 : part * 16 + 16, D + 512 : D + 768] = total[
                        piece * 16 : piece * 16 + 16, part * 256 : part * 256 + 256
                    ]

    over_ctx = [
        go(
            packed.at[mate],
            from_ctx.at[spot],
            ctx_send.at[spot],
            ctx_recv.at[spot],
            (mate * 2 + core, shard),
        )
        for spot, mate in enumerate(mates)
    ]
    total = packed[rank].astype(F32)
    for spot in range(7):
        over_ctx[spot].wait_recv()
        total = total + from_ctx[spot].astype(F32)
    total_ref[...] = total.astype(BF)
    for spot, mate in enumerate(mates):
        go(
            total_ref,
            out_ref.at[rank, mine, :],
            out_send.at[spot],
            out_recv.at[rank],
            (mate * 2 + core, shard),
        )
    go(total_ref, out_ref.at[rank, mine, :], pass_send.at[7], pass_recv.at[rank], sibling)
    own = pltpu.make_async_copy(total_ref, out_ref.at[rank, mine, :], local_sem)
    own.start()

    def landed(ref, recv_sem):
        hop(ref, ref, pass_send.at[0], recv_sem, *sibling).wait_recv()

    for spot, mate in enumerate(mates):
        block = out_ref.at[mate, mine, :]
        landed(block, out_recv.at[mate])
        go(block, block, pass_send.at[spot], pass_recv.at[mate], sibling)
    for mate in [rank] + mates:
        landed(out_ref.at[mate, theirs, :], pass_recv.at[mate])
    own.wait()
    for copy in sends:
        copy.wait_send()


def reduce_gradients(parts, wide, down, collective_id):
    widths = [part.shape[2] for part in parts]
    count = len(parts)
    span = sum(widths)
    dma = pltpu.SemaphoreType.DMA
    return pl.pallas_call(
        functools.partial(reduce_kernel, widths),
        out_shape=jax.ShapeDtypeStruct((8, 2 * PIECE, ROOM), BF),
        in_specs=[pl.BlockSpec(memory_space=pltpu.VMEM)] * (count + 2),
        out_specs=pl.BlockSpec(memory_space=pl.ANY),
        scratch_shapes=[
            pltpu.VMEM((8, PIECE, span), BF),
            pltpu.VMEM((8, PIECE, span), BF),
            pltpu.VMEM((4, PIECE, span), BF),
            pltpu.VMEM((4, PIECE, span), BF),
            pltpu.VMEM((3, PIECE, span), BF),
            pltpu.VMEM((PIECE, wide.shape[1]), BF),
            pltpu.VMEM((128, down.shape[1]), BF),
            pltpu.VMEM((8, PIECE, ROOM), BF),
            pltpu.VMEM((7, PIECE, ROOM), BF),
            pltpu.VMEM((PIECE, ROOM), BF),
            dma((count + 2,)),
            dma((count + 2,)),
            dma((count, 2)),
            dma((count, 2)),
            dma((count, 3)),
            dma((count, 3)),
            dma((7,)),
            dma((7,)),
            dma((7,)),
            dma((8,)),
            dma((8,)),
            dma((8,)),
            dma,
        ],
        compiler_params=pltpu.CompilerParams(
            collective_id=collective_id, has_side_effects=True, vmem_limit_bytes=56 * MIB
        ),
        name="reduce_gradients",
    )(*parts, wide, down)


def split_heads(block):
    lane = lax.broadcasted_iota(jnp.int32, block.shape, 1)
    nothing = jnp.zeros_like(block)
    return jnp.concatenate(
        [jnp.where(lane < HEAD_DIM, block, nothing), jnp.where(lane < HEAD_DIM, nothing, block)],
        axis=0,
    )


def join_heads(transposed):
    row = lax.broadcasted_iota(jnp.int32, (2 * HEAD_DIM, TOK), 0)
    return jnp.where(row < HEAD_DIM, transposed[:, :TOK], transposed[:, TOK:]).T


def contract(left, right, dims):
    return lax.dot_general(left, right, (dims, ((), ())), preferred_element_type=F32)


def key_chunk(ref, j):
    if ref.shape[2] == 2 * HALF:
        return ref[j, 0]
    return ref[pl.ds(2 * j, 2), 0].reshape(2 * HALF, 2 * HEAD_DIM)


def bias_chunk(class_ref, tile_ref, j):
    lane = lax.broadcasted_iota(jnp.int32, (HALF, TOK), 1)
    rows = []
    for half in range(2):
        spot = 2 * j + half
        near = class_ref[0, spot]
        far = class_ref[1, spot]
        rows.append(
            jnp.concatenate(
                [
                    jnp.where(lane < HALF, tile_ref[head, near], tile_ref[head, far])
                    for head in range(2)
                ],
                axis=1,
            )
        )
    return jnp.concatenate(rows, axis=0)


def fold(values, join):
    return join(values.reshape(-1, 8, values.shape[-1]), axis=0)


def forward_kernel(biased, *refs):
    if biased:
        class_ref, q_ref, k_ref, v_ref, tile_ref, out_ref, total_ref, score_ref, share_ref = refs
    else:
        q_ref, k_ref, v_ref, out_ref, total_ref, score_ref, share_ref = refs
    chunks = score_ref.shape[0]
    queries = split_heads(q_ref[...])
    highest = None
    for j in range(chunks):
        scores = contract(key_chunk(k_ref, j), queries, ((1,), (1,)))
        if biased:
            scores = scores + bias_chunk(class_ref, tile_ref, j)
        score_ref[j] = scores
        top = fold(scores, jnp.max)
        highest = top if highest is None else jnp.maximum(highest, top)
    highest = jnp.max(highest, axis=0, keepdims=True)
    summed = jnp.zeros((8, 2 * TOK), F32)
    for j in range(chunks):
        raised = jnp.exp(score_ref[j] - highest)
        summed = summed + fold(raised, jnp.sum)
        share_ref[j] = raised.astype(BF)
    summed = jnp.sum(summed, axis=0, keepdims=True)
    values = jnp.concatenate([key_chunk(v_ref, j) for j in range(chunks)], axis=0)
    mixed = contract(values, share_ref[...].reshape(-1, 2 * TOK), ((0,), (0,)))
    out_ref[...] = join_heads(mixed / summed).astype(BF)
    total_ref[0] = jnp.broadcast_to(highest + jnp.log(summed), (8, 2 * TOK))


def backward_kernel(biased, *refs):
    if biased:
        class_ref, near_ref, q_ref, k_ref, v_ref, g_ref, total_ref, tile_ref = refs[:8]
        dq_ref, dkv_ref, strip_ref, share_ref, slope_ref, share_low, slope_low = refs[8:]
    else:
        q_ref, k_ref, v_ref, g_ref, total_ref = refs[:5]
        dq_ref, dkv_ref, share_ref, slope_ref, share_low, slope_low = refs[5:]
    chunks = share_ref.shape[0]
    queries = split_heads(q_ref[...])
    grads = split_heads(g_ref[...])
    totals = total_ref[0, 0:1]
    inner = jnp.zeros((8, 2 * TOK), F32)
    for j in range(chunks):
        scores = contract(key_chunk(k_ref, j), queries, ((1,), (1,)))
        if biased:
            scores = scores + bias_chunk(class_ref, tile_ref, j)
        shares = jnp.exp(scores - totals)
        slopes = contract(key_chunk(v_ref, j), grads, ((1,), (1,)))
        inner = inner + fold(shares * slopes, jnp.sum)
        share_ref[j] = shares
        slope_ref[j] = slopes
        share_low[j] = shares.astype(BF)
    inner = jnp.sum(inner, axis=0, keepdims=True)
    for j in range(chunks):
        grad = share_ref[j] * (slope_ref[j] - inner)
        if biased:
            slope_ref[j] = grad
        slope_low[j] = grad.astype(BF)
    keys = jnp.concatenate([key_chunk(k_ref, j) for j in range(chunks)], axis=0)
    low = slope_low[...].reshape(-1, 2 * TOK)
    dq_ref[...] = join_heads(contract(keys, low, ((0,), (0,)))).astype(BF)
    shape = dkv_ref.shape
    block = (shape[0], shape[2], shape[3])
    dkv_ref[:, 0] = contract(low, queries, ((1,), (0,))).astype(BF).reshape(block)
    dkv_ref[:, 1] = (
        contract(share_low[...].reshape(-1, 2 * TOK), grads, ((1,), (0,))).astype(BF).reshape(block)
    )
    if biased:
        lane = lax.broadcasted_iota(jnp.int32, (HALF, TOK), 1)
        for gap in range(3):
            pieces = []
            for half in range(2):
                spot = near_ref[half, gap]
                held = slope_ref[jnp.maximum(spot, 0) // 2, pl.ds(
                    pl.multiple_of((jnp.maximum(spot, 0) % 2) * HALF, HALF), HALF)]
                pieces.append(jnp.where(spot >= 0, held, jnp.zeros_like(held)))
            for head in range(2):
                cut = slice(head * TOK, (head + 1) * TOK)
                strip_ref[head, gap] = jnp.where(lane < HALF, pieces[0][:, cut], pieces[1][:, cut])


def pair_columns(pair):
    return (0, pair)


def kv_spec(rows, row_block, part):
    return pl.BlockSpec(
        (N_CTX, 1, rows, 2 * HEAD_DIM), lambda pair: (0, part, row_block, pair)
    )


SMEM_SPEC = pl.BlockSpec(memory_space=pltpu.SMEM)
TILE_SPEC = pl.BlockSpec((2, 5, HALF, TOK), lambda pair: (pair, 0, 0, 0))
TOTAL_SPEC = pl.BlockSpec((1, 8, 2 * TOK), lambda pair: (pair, 0, 0))
ROW_SPEC = pl.BlockSpec((TOK, 2 * HEAD_DIM), pair_columns)
LOCAL = pltpu.CompilerParams(vmem_limit_bytes=48 * MIB)


def attend(queries, gathered, rows, row_block, classes=None, tiles=None):
    biased = classes is not None
    chunks = N_CTX * rows // TOK
    specs = [ROW_SPEC, kv_spec(rows, row_block, 0), kv_spec(rows, row_block, 1)]
    operands = [queries, gathered, gathered]
    if biased:
        specs = [SMEM_SPEC] + specs + [TILE_SPEC]
        operands = [classes] + operands + [tiles]
    return pl.pallas_call(
        functools.partial(forward_kernel, biased),
        grid=(PAIRS,),
        in_specs=specs,
        out_specs=[ROW_SPEC, TOTAL_SPEC],
        out_shape=[
            jax.ShapeDtypeStruct((TOK, D), BF),
            jax.ShapeDtypeStruct((PAIRS, 8, 2 * TOK), F32),
        ],
        scratch_shapes=[
            pltpu.VMEM((chunks, TOK, 2 * TOK), F32),
            pltpu.VMEM((chunks, TOK, 2 * TOK), BF),
        ],
        compiler_params=LOCAL,
        cost_estimate=pl.CostEstimate(flops=10**9, bytes_accessed=10**7, transcendentals=10**6),
        name="attend_self" if biased else "attend_cross",
    )(*operands)


def attend_back(queries, gathered, grads, totals, rows, row_block, classes=None, near=None, tiles=None):
    biased = classes is not None
    chunks = N_CTX * rows // TOK
    specs = [ROW_SPEC, kv_spec(rows, row_block, 0), kv_spec(rows, row_block, 1), ROW_SPEC, TOTAL_SPEC]
    operands = [queries, gathered, gathered, grads, totals]
    out_specs = [
        ROW_SPEC,
        pl.BlockSpec((N_CTX, 2, rows, 2 * HEAD_DIM), lambda pair: (0, 0, 0, pair)),
    ]
    out_shape = [
        jax.ShapeDtypeStruct((TOK, D), BF),
        jax.ShapeDtypeStruct((N_CTX, 2, rows, D), BF),
    ]
    if biased:
        specs = [SMEM_SPEC, SMEM_SPEC] + specs + [TILE_SPEC]
        operands = [classes, near] + operands + [tiles]
        out_specs.append(pl.BlockSpec((2, 3, HALF, TOK), lambda pair: (pair, 0, 0, 0)))
        out_shape.append(jax.ShapeDtypeStruct((HEADS, 3, HALF, TOK), F32))
    return pl.pallas_call(
        functools.partial(backward_kernel, biased),
        grid=(PAIRS,),
        in_specs=specs,
        out_specs=out_specs,
        out_shape=out_shape,
        scratch_shapes=[
            pltpu.VMEM((chunks, TOK, 2 * TOK), F32),
            pltpu.VMEM((chunks, TOK, 2 * TOK), F32),
            pltpu.VMEM((chunks, TOK, 2 * TOK), BF),
            pltpu.VMEM((chunks, TOK, 2 * TOK), BF),
        ],
        compiler_params=LOCAL,
        cost_estimate=pl.CostEstimate(flops=3 * 10**9, bytes_accessed=10**7, transcendentals=10**6),
        name="attend_self_back" if biased else "attend_cross_back",
    )(*operands)


def matmul(left, right):
    return jnp.dot(left, right, preferred_element_type=F32)


def transposed_left(left, right):
    return contract(left, right, ((0,), (0,)))


def transposed_right(left, right):
    return contract(left, right, ((1,), (1,)))


def rms_scaled(values, gain):
    inverse = lax.rsqrt(jnp.mean(values * values, axis=-1, keepdims=True) + 1e-06)
    return (values * inverse * gain).astype(BF)


def rms_back(values, gain, grad):
    inverse = lax.rsqrt(jnp.mean(values * values, axis=-1, keepdims=True) + 1e-06)
    scaled = gain * grad
    mixed = jnp.mean(values * scaled, axis=-1, keepdims=True)
    grad_values = inverse * scaled - values * (inverse * inverse * inverse * mixed)
    return grad_values, jnp.sum(values * inverse * grad, axis=0)


def gelu_product(gate_part, up_part):
    return jax.nn.gelu(gate_part, approximate=True) * up_part


def near_hot():
    shape = (REACH, 3 * HALF * HALF)
    spot = lax.broadcasted_iota(jnp.int32, shape, 1)
    gap = spot // (HALF * HALF)
    key = (spot // HALF) % HALF
    row = spot % HALF
    distance = jnp.clip(HALF * gap + row - key, 0, REACH - 1)
    return (distance == lax.broadcasted_iota(jnp.int32, shape, 0)).astype(BF)


def bias_tiles(bias_rows):
    near = matmul(bias_rows.astype(BF), near_hot()).reshape(HEADS, 3, HALF, HALF)
    key = jnp.arange(HALF, dtype=jnp.int32)[:, None]
    row = jnp.arange(HALF, dtype=jnp.int32)[None, :]
    barred = (jnp.arange(3) == 0)[None, :, None, None] & (key > row)[None, None]
    near = jnp.where(barred, -1e30, near)
    far = jnp.broadcast_to(bias_rows[:, -1][:, None, None, None], (HEADS, 1, HALF, HALF))
    none = jnp.full((HEADS, 1, HALF, HALF), -1e30, F32)
    tiles = jnp.concatenate([near, far, none], axis=1)
    return jnp.concatenate([tiles, tiles], axis=-1)


def bias_sums(strips):
    tiles = (strips[..., :HALF] + strips[..., HALF:]).reshape(HEADS, -1)
    high = tiles.astype(BF)
    low = (tiles - high.astype(F32)).astype(BF)
    hot = near_hot()
    sums = transposed_right(high, hot) + transposed_right(low, hot)
    far = -jnp.sum(sums[:, :-1], axis=1, keepdims=True)
    return jnp.concatenate([sums[:, :-1], far], axis=1)


def owned_rows(grad):
    return lax.psum_scatter(grad, "fsdp", scatter_dimension=0, tiled=True)


def body(
    decoder_in,
    encoder_states,
    out_grad,
    block_pairs,
    bucket_table,
    gain_self,
    self_query,
    self_key,
    self_value,
    self_out,
    position_bias,
    gain_cross,
    cross_query,
    cross_key,
    cross_value,
    cross_out,
    gain_feed,
    feed_gate,
    feed_up,
    feed_down,
):
    me = lax.axis_index("ctx")
    rows = self_query.shape[0]
    extra = jnp.concatenate(
        [
            gain_self[:, None],
            gain_cross[:, None],
            gain_feed[:, None],
            jnp.zeros((rows, 5), BF),
            jnp.pad(position_bias, ((0, rows - position_bias.shape[0]), (0, 0))),
            jnp.zeros((rows, 236), BF),
        ],
        axis=1,
    )
    early, late, down = gather_weights(
        [
            jnp.concatenate([self_query, self_key, self_value, cross_key, cross_value, extra], axis=1),
            jnp.concatenate([self_out, cross_query, cross_out, feed_gate, feed_up], axis=1),
            feed_down,
        ],
        5,
    )
    early = early.reshape(D, -1)
    late = late.reshape(D, -1)
    down = down.reshape(FF, D)
    qkv_one = early[:, : 3 * D]
    kv_two = early[:, 3 * D : 5 * D]
    gains = early[:, 5 * D : 5 * D + 3].astype(F32).T
    norm_one, norm_two, norm_three = gains[0:1], gains[1:2], gains[2:3]
    table = early.reshape(8, rows, -1)[:, :4, 5 * D + 8 : 5 * D + 20].reshape(32, HEADS)
    out_one = late[:, :D]
    query_two = late[:, D : 2 * D]
    out_two = late[:, 2 * D : 3 * D]
    gate_up = late[:, 3 * D :]

    bucket_hot = (bucket_table[:, None] == jnp.arange(32, dtype=jnp.int32)[None, :]).astype(BF)
    bias_rows = transposed_right(table.T, bucket_hot)
    tiles = bias_tiles(bias_rows)
    pair = block_pairs[me]
    query_blocks = jnp.stack([pair, 31 - pair])
    key_blocks = jnp.stack([block_pairs, 31 - block_pairs], axis=1).reshape(-1)
    gaps = query_blocks[:, None] - key_blocks[None, :]
    classes = jnp.where(gaps < 0, 4, jnp.minimum(gaps, 3)).astype(jnp.int32)
    wanted = query_blocks[:, None] - jnp.arange(3, dtype=jnp.int32)[None, :]
    near = jnp.max(
        jnp.where(
            wanted[:, :, None] == key_blocks[None, None, :],
            jnp.arange(32, dtype=jnp.int32)[None, None, :],
            -1,
        ),
        axis=-1,
    )

    tokens = decoder_in[0].astype(F32)
    states = encoder_states[0]
    upstream = out_grad[0]
    normed_one = rms_scaled(tokens, norm_one)
    qkv = matmul(normed_one, qkv_one).astype(BF)
    cross_kv = matmul(states, kv_two).astype(BF)
    queries = qkv[:, :D]
    local = jnp.stack(
        [
            jnp.concatenate([qkv[:, D : 2 * D], cross_kv[:, :D]], axis=0),
            jnp.concatenate([qkv[:, 2 * D :], cross_kv[:, D:]], axis=0),
        ]
    )
    gathered = ctx_gather(local, 0)
    attended, self_totals = attend(queries, gathered, TOK, 0, classes, tiles)
    mid_one = tokens + matmul(attended, out_one)
    normed_two = rms_scaled(mid_one, norm_two)
    cross_queries = matmul(normed_two, query_two).astype(BF)
    cross_attended, cross_totals = attend(cross_queries, gathered, ENC, 2)
    mid_two = mid_one + matmul(cross_attended, out_two)
    normed_three = rms_scaled(mid_two, norm_three)
    gate_up_values = matmul(normed_three, gate_up).astype(BF).astype(F32)
    gate_values, up_values = gate_up_values[:, :FF], gate_up_values[:, FF:]
    hidden, pull_feed = jax.vjp(gelu_product, gate_values, up_values)
    hidden = hidden.astype(BF)
    block_out = mid_two + matmul(hidden, down)

    d_hidden = transposed_right(upstream, down)
    d_gate_up = jnp.concatenate(pull_feed(d_hidden), axis=1).astype(BF)
    grad_down = owned_rows(transposed_left(hidden, upstream).astype(BF))
    grad_gate_up = owned_rows(transposed_left(normed_three, d_gate_up).astype(BF))
    d_normed_three = transposed_right(d_gate_up, gate_up)
    part_three, grad_norm_three = rms_back(mid_two, norm_three, d_normed_three)
    d_mid_two = upstream.astype(F32) + part_three
    cross_branch = d_mid_two.astype(BF)
    d_cross_attended = transposed_right(cross_branch, out_two).astype(BF)
    d_cross_queries, d_cross_kv_all = attend_back(
        cross_queries, gathered, d_cross_attended, cross_totals, ENC, 2
    )
    d_cross_kv = ctx_scatter(d_cross_kv_all, 1)
    d_cross_kv = jnp.concatenate([d_cross_kv[0], d_cross_kv[1]], axis=1)
    grad_encoder = transposed_right(d_cross_kv, kv_two)
    grad_out_two = transposed_left(cross_attended, cross_branch).astype(BF)
    grad_query_two = transposed_left(normed_two, d_cross_queries).astype(BF)
    grad_kv_two = transposed_left(states, d_cross_kv).astype(BF)
    d_normed_two = transposed_right(d_cross_queries, query_two)
    part_two, grad_norm_two = rms_back(mid_one, norm_two, d_normed_two)
    d_mid_one = d_mid_two + part_two
    self_branch = d_mid_one.astype(BF)
    d_attended = transposed_right(self_branch, out_one).astype(BF)
    d_queries, d_kv_all, strips = attend_back(
        queries, gathered, d_attended, self_totals, TOK, 0, classes, near, tiles
    )
    d_kv = ctx_scatter(d_kv_all, 2)
    d_qkv = jnp.concatenate([d_queries, d_kv[0], d_kv[1]], axis=1)
    d_normed_one = transposed_right(d_qkv, qkv_one)
    part_one, grad_norm_one = rms_back(tokens, norm_one, d_normed_one)
    grad_decoder = d_mid_one + part_one
    grad_table = matmul(bias_sums(strips), bucket_hot.astype(F32)).T.reshape(8, 4, HEADS)
    grad_extra = jnp.concatenate(
        [
            grad_norm_one[:, None],
            grad_norm_two[:, None],
            grad_norm_three[:, None],
            jnp.zeros((D, 5), F32),
            jnp.pad(grad_table, ((0, 0), (0, rows - 4), (0, 0))).reshape(D, HEADS),
            jnp.zeros((D, 236), F32),
        ],
        axis=1,
    )
    grad_out_one = transposed_left(attended, self_branch).astype(BF)
    grad_qkv_one = transposed_left(normed_one, d_qkv).astype(BF)
    summed = reduce_gradients(
        [
            part.astype(BF).reshape(8, rows, -1)
            for part in (
                grad_out_two, grad_query_two, grad_kv_two, grad_out_one, grad_qkv_one, grad_extra,
            )
        ],
        grad_gate_up,
        grad_down,
        3,
    )
    owned = summed[:, :, :D].astype(F32)
    wide = summed[:, :, D : D + 512].astype(F32)
    wide = jnp.transpose(wide, (1, 0, 2)).reshape(rows, 2 * FF)
    tall = summed[:, :, D + 512 : D + 768].astype(F32).reshape(8, 2, 3, 16, 256)
    tall = jnp.transpose(tall, (1, 0, 3, 2, 4)).reshape(256, D)
    extras = summed[0, :, D + 768 :].astype(F32)
    return (
        block_out[None],
        grad_decoder[None],
        grad_encoder[None],
        extras[:, 0],
        owned[5],
        owned[6],
        owned[7],
        owned[4],
        extras[:4, 8:20],
        extras[:, 1],
        owned[1],
        owned[2],
        owned[3],
        owned[0],
        extras[:, 2],
        wide[:, :FF],
        wide[:, FF:],
        tall,
    )


def solution(mesh):
    tokens = P("fsdp", "ctx", None)
    matrix = P("fsdp", None)
    vector = P("fsdp")
    weights = (
        (vector,) + (matrix,) * 5 + (vector,) + (matrix,) * 4 + (vector,) + (matrix,) * 3
    )
    return jax.shard_map(
        body,
        mesh=mesh,
        in_specs=(tokens,) * 3 + (P(), P()) + weights,
        out_specs=(tokens,) * 3 + weights,
        check_vma=False,
    )
```

profile of v0, /device:TPU:1, one launch (start us, length us, event | category | flops | bytes accessed | tf_op | source)
XLA Modules:
  0.0 499.4 jit_solution(7922627454438444119)
XLA Ops:
  19.9 84.7 %gather_weights.1 = (bf16[8,96,4096]{2,1,0:T(8,128)(2,1)}, bf16[8,96,6400]{2,1,0:T(8,128)(2,1)}, bf16[8,256,768]{2,1,0:T(8,128)(2,1)}) custom-call(bf16[96,4096]{1,0:T(8,128)(2,1)} %concatenate.42.refs_0_, bf16[96,6400]{1,0:T(8,128)(2,1)} %copy-done.29, bf16[256,768]{1,0:T(8,128)(2,1)} %refs_2_.1), custom_call_target="tpu_custom_call" | custom-call | tf_op jit(solution)/shard_map/gather_weights/pallas_call | solution.py:299
  106.7 2.7 convolution_convert_fusion.2
  109.4 2.2 fusion.17
  112.6 59.8 %ctx_gather.1.refs_2_.refs_3_.refs_1_.refs_4_ = bf16[16,2,192,768]{3,2,1,0:T(8,128)(2,1)} custom-call(bf16[2,192,768]{2,1,0:T(8,128)(2,1)} %pad_maximum_fusion.3.x_ref), custom_call_target="tpu_custom_call" | custom-call | tf_op jit(solution)/shard_map/ctx_gather/pallas_call | solution.py:93
  174.1 1.7 fusion.76
  175.8 1.6 reshape.230
  178.5 10.2 %attend_self.1 = (bf16[128,768]{1,0:T(8,128)(2,1)S(1)}, f32[6,8,256]{2,1,0:T(8,128)S(1)}) custom-call(s32[2,32]{1,0:T(2,128)S(1)} %compare_select_fusion.1.refs_0_, bf16[128,768]{1,0:T(8,128)(2,1)S(1)} %get-tuple-element.71.refs_1_.refs_2_, bf16[16,2,192,768]{3,2,1,0:T(8,128)(2,1)} %ctx_gather.1.refs_2_.refs_3_.refs_1_.refs_4_, ...), custom_call_target="tpu_custom_call" | custom-call | flops 1000000000 | bytes 10000000 | tf_op jit(solution)/shard_map/attend_self/pallas_call | solution.py:682
  189.7 6.8 %attend_cross.1 = (bf16[128,768]{1,0:T(8,128)(2,1)S(1)}, f32[6,8,256]{2,1,0:T(8,128)S(1)}) custom-call(bf16[128,768]{1,0:T(8,128)(2,1)S(1)} %convolution_convert_fusion.11.refs_0_, bf16[16,2,192,768]{3,2,1,0:T(8,128)(2,1)} %ctx_gather.1.refs_2_.refs_3_.refs_1_.refs_4_, bf16[16,2,192,768]{3,2,1,0:T(8,128)(2,1)} %ctx_gather.1.refs_2_.refs_3_.refs_1_.refs_4_), custom_call_target="tpu_custom_call" | custom-call | flops 1000000000 | bytes 10000000 | tf_op jit(solution)/shard_map/attend_cross/pallas_call | solution.py:682
  199.0 2.3 fusion.31
  202.2 2.7 convolution_convert_fusion.4
  205.2 5.6 %convolution_convert_fusion = bf16[768,4096]{1,0:T(8,128)(2,1)} fusion(bf16[128,2048]{1,0:T(8,128)(2,1)} %get-tuple-element.57, bf16[128,2048]{1,0:T(8,128)(2,1)S(1)} %get-tuple-element.56, f32[128,768]{1,0:T(8,128)S(1)} %get-tuple-element.81, f32[768]{0:T(1024)S(1)} %get-tuple-element.51, f32[128]{0:T(128)S(1)} %add_rsqrt_fusion), kind=kOutput, calls=%fused_computation.5 | convolution fusion | flops 810844160 | bytes 7736832 | tf_op jit(solution)/shard_map/dot_general | solution.py:546
  211.1 5.6 %multiply_reduce_fusion = (bf16[768]{0:T(1024)(128)(2,1)S(1)}, f32[128]{0:T(128)S(1)}, f32[128,768]{1,0:T(8,128)S(1)}) fusion(f32[128,768]{1,0:T(8,128)S(1)} %get-tuple-element.81, f32[128]{0:T(128)S(1)} %add_rsqrt_fusion, f32[768]{0:T(1024)S(1)} %get-tuple-element.51, bf16[768,6400]{1,0:T(8,128)(2,1)} %bitcast.112, ...), kind=kOutput, calls=%fused_computation.83 | convolution fusion | flops 807992448 | bytes 8132096 | tf_op jit(solution)/shard_map/dot_general | solution.py:546
  216.9 2.0 convolution_convert_fusion.10.refs_3_
  218.9 8.3 %attend_cross_back.1 = (bf16[128,768]{1,0:T(8,128)(2,1)S(1)}, bf16[16,2,64,768]{3,2,1,0:T(8,128)(2,1)S(1)}) custom-call(bf16[128,768]{1,0:T(8,128)(2,1)S(1)} %convolution_convert_fusion.11.refs_0_, bf16[16,2,192,768]{3,2,1,0:T(8,128)(2,1)} %ctx_gather.1.refs_2_.refs_3_.refs_1_.refs_4_, bf16[16,2,192,768]{3,2,1,0:T(8,128)(2,1)} %ctx_gather.1.refs_2_.refs_3_.refs_1_.refs_4_, ...), custom_call_target="tpu_custom_call" | custom-call | flops 3000000000 | bytes 10000000 | tf_op jit(solution)/shard_map/attend_cross_back/pallas_call | solution.py:719
  227.2 2.0 multiply_reduce_fusion.1
  229.4 2.1 convolution_convert_fusion.9.refs_5_
  231.5 13.8 %attend_self_back.1 = (bf16[128,768]{1,0:T(8,128)(2,1)S(1)}, bf16[16,2,128,768]{3,2,1,0:T(8,128)(2,1)}, f32[12,3,64,128]{3,2,1,0:T(8,128)S(1)}) custom-call(s32[2,32]{1,0:T(2,128)S(1)} %compare_select_fusion.1.refs_0_, s32[2,3]{1,0:T(2,128)S(1)} %copy.65.refs_1_, bf16[128,768]{1,0:T(8,128)(2,1)S(1)} %get-tuple-element.71.refs_1_.refs_2_, ...), custom_call_target="tpu_custom_call" | custom-call | flops 3000000000 | bytes 10000000 | tf_op jit(solution)/shard_map/attend_self_back/pallas_call | solution.py:719
  245.3 2.9 copy-done.1
  248.2 85.4 %ctx_scatter.2 = bf16[2,128,768]{2,1,0:T(8,128)(2,1)S(1)} custom-call(bf16[16,2,128,768]{3,2,1,0:T(8,128)(2,1)S(1)} %copy-done.1), custom_call_target="tpu_custom_call" | custom-call | tf_op jit(solution)/shard_map/ctx_scatter/pallas_call | solution.py:167
  333.7 31.1 %ctx_scatter.3 = bf16[2,64,768]{2,1,0:T(8,128)(2,1)S(1)} custom-call(bf16[16,2,64,768]{3,2,1,0:T(8,128)(2,1)S(1)} %get-tuple-element.40.x_ref), custom_call_target="tpu_custom_call" | custom-call | tf_op jit(solution)/shard_map/ctx_scatter/pallas_call | solution.py:167
  364.9 2.1 fusion.42
  370.1 1.4 slice_add_fusion
  371.5 1.8 reshape.238
  377.2 3.3 fusion.22
  381.4 1.5 convolution_convert_fusion.8
  383.0 1.5 convolution_convert_fusion.6
  384.5 1.7 convolution_convert_fusion.7
  386.2 2.2 convolution_convert_fusion.3
  389.8 2.9 convolution_convert_fusion.1
  392.8 91.7 %reduce_gradients.1 = bf16[8,96,1664]{2,1,0:T(8,128)(2,1)} custom-call(bf16[8,96,768]{2,1,0:T(8,128)(2,1)} %bitcast.125, bf16[8,96,768]{2,1,0:T(8,128)(2,1)} %bitcast.127, bf16[8,96,1536]{2,1,0:T(8,128)(2,1)} %bitcast.123, bf16[8,96,768]{2,1,0:T(8,128)(2,1)} %bitcast.126, bf16[8,96,2304]{2,1,0:T(8,128)(2,1)} %bitcast.111, ...), custom_call_target="tpu_custom_call" | custom-call | tf_op jit(solution)/shard_map/reduce_gradients/pallas_call | solution.py:494
  485.3 1.5 slice_convert_fusion
  488.4 1.4 slice_bitcast_fusion
  (197 shorter events, 37.1 us)
Async XLA Ops:
  7.2 102.2 %copy-start = (bf16[1,64,768]{2,1,0:T(8,128)(2,1)S(1)}, bf16[1,64,768]{2,1,0:T(8,128)(2,1)}, u32[]{:S(2)}) copy-start(bf16[1,64,768]{2,1,0:T(8,128)(2,1)} %param.21) | copy-start | bytes 294916
  7.2 11.3 %copy-start.39 = (bf16[96,2048]{1,0:T(8,128)(2,1)S(1)}, bf16[96,2048]{1,0:T(8,128)(2,1)}, u32[]{:S(2)}) copy-start(bf16[96,2048]{1,0:T(8,128)(2,1)} %param.38) | copy-start | bytes 1179652
  7.2 11.4 %copy-start.41 = (bf16[96,768]{1,0:T(8,128)(2,1)S(1)}, bf16[96,768]{1,0:T(8,128)(2,1)}, u32[]{:S(2)}) copy-start(bf16[96,768]{1,0:T(8,128)(2,1)} %param.26) | copy-start | bytes 442372
  7.2 11.4 %copy-start.42 = (bf16[96,768]{1,0:T(8,128)(2,1)S(1)}, bf16[96,768]{1,0:T(8,128)(2,1)}, u32[]{:S(2)}) copy-start(bf16[96,768]{1,0:T(8,128)(2,1)} %param.27) | copy-start | bytes 442372
  7.2 11.4 %copy-start.43 = (bf16[96,768]{1,0:T(8,128)(2,1)S(1)}, bf16[96,768]{1,0:T(8,128)(2,1)}, u32[]{:S(2)}) copy-start(bf16[96,768]{1,0:T(8,128)(2,1)} %param.28) | copy-start | bytes 442372
  7.2 11.4 %copy-start.44 = (bf16[96,768]{1,0:T(8,128)(2,1)S(1)}, bf16[96,768]{1,0:T(8,128)(2,1)}, u32[]{:S(2)}) copy-start(bf16[96,768]{1,0:T(8,128)(2,1)} %param.33) | copy-start | bytes 442372
  7.3 11.4 %copy-start.45 = (bf16[96,768]{1,0:T(8,128)(2,1)S(1)}, bf16[96,768]{1,0:T(8,128)(2,1)}, u32[]{:S(2)}) copy-start(bf16[96,768]{1,0:T(8,128)(2,1)} %param.34) | copy-start | bytes 442372
  7.3 385.5 %reduce-scatter.5.cloned.1.call-start = ((), (), s32[]{:S(2)}) async-start(), calls=%async_computation.3 | async-start | bytes 3538944 | tf_op jit(solution)/shard_map/reduce_scatter | solution.py:799
  19.9 86.7 %copy-start.24 = (bf16[1,128,768]{2,1,0:T(8,128)(2,1)S(1)}, bf16[1,128,768]{2,1,0:T(8,128)(2,1)}, u32[]{:S(2)}) copy-start(bf16[1,128,768]{2,1,0:T(8,128)(2,1)} %param.20) | copy-start | bytes 589828
  112.6 59.8 %copy-start.46 = (s32[128]{0:T(128)S(1)}, s32[128]{0:T(128)}, u32[]{:S(2)}) copy-start(s32[128]{0:T(128)} %param.24) | copy-start | bytes 1540
  177.9 10.8 %slice-start = ((s8[9830400]{0:T(1024)(128)(4,1)}), s8[4194304]{0:T(1024)(128)(4,1)S(1)}, s32[]{:S(2)}) async-start(s8[9830400]{0:T(1024)(128)(4,1)} %bitcast.116), calls=%async_computation.4 | async-start | bytes 8388608
  178.4 10.2 %slice-start.1 = ((s8[9830400]{0:T(1024)(128)(4,1)}), s8[4194304]{0:T(1024)(128)(4,1)S(1)}, s32[]{:S(2)}) async-start(s8[9830400]{0:T(1024)(128)(4,1)} %bitcast.116), calls=%async_computation.5 | async-start | bytes 8388608
  178.5 10.2 %slice-start.2 = ((s8[9830400]{0:T(1024)(128)(4,1)}), s8[1441792]{0:T(1024)(128)(4,1)S(1)}, s32[]{:S(2)}) async-start(s8[9830400]{0:T(1024)(128)(4,1)} %bitcast.116), calls=%async_computation.6 | async-start | bytes 2883584
  189.1 7.4 %copy-start.19 = (f32[128,768]{1,0:T(8,128)}, f32[128,768]{1,0:T(8,128)S(1)}, u32[]{:S(2)}) copy-start(f32[128,768]{1,0:T(8,128)S(1)} %get-tuple-element.79) | copy-start | bytes 1179652
  197.0 19.8 %copy-start.12 = (f32[128,768]{1,0:T(8,128)}, f32[128,768]{1,0:T(8,128)S(1)}, u32[]{:S(2)}) copy-start(f32[128,768]{1,0:T(8,128)S(1)} %get-tuple-element.81) | copy-start | bytes 1179652
  204.9 187.8 %reduce-scatter.3.cloned.1.call-start = ((), (), s32[]{:S(2)}) async-start(), calls=%async_computation.2 | async-start | bytes 7077888 | tf_op jit(solution)/shard_map/reduce_scatter | solution.py:799
  211.1 5.6 %copy-start.38 = (bf16[1,128,768]{2,1,0:T(8,128)(2,1)S(1)}, bf16[1,128,768]{2,1,0:T(8,128)(2,1)}, u32[]{:S(2)}) copy-start(bf16[1,128,768]{2,1,0:T(8,128)(2,1)} %param.22) | copy-start | bytes 589828
  216.9 12.3 %copy-start.15 = (f32[128,768]{1,0:T(8,128)}, f32[128,768]{1,0:T(8,128)S(1)}, u32[]{:S(2)}) copy-start(f32[128,768]{1,0:T(8,128)S(1)} %subtract_add_fusion.1) | copy-start | bytes 1179652
  218.9 8.3 %copy-start.20 = (f32[128,768]{1,0:T(8,128)S(1)}, f32[128,768]{1,0:T(8,128)}, u32[]{:S(2)}) copy-start(f32[128,768]{1,0:T(8,128)} %copy-done.19) | copy-start | bytes 1179652
  227.2 4.3 copy-start.8
  229.2 135.6 %slice-start.4 = ((s8[6291456]{0:T(1024)(128)(4,1)}), s8[2097152]{0:T(1024)(128)(4,1)S(1)}, s32[]{:S(2)}) async-start(s8[6291456]{0:T(1024)(128)(4,1)} %bitcast.139), calls=%async_computation.8 | async-start | bytes 4194304
  229.4 15.9 %copy-start.17 = (f32[128,768]{1,0:T(8,128)}, f32[128,768]{1,0:T(8,128)S(1)}, u32[]{:S(2)}) copy-start(f32[128,768]{1,0:T(8,128)S(1)} %subtract_add_fusion) | copy-start | bytes 1179652
  231.5 133.4 %slice-start.5 = ((s8[6291456]{0:T(1024)(128)(4,1)}), s8[4194304]{0:T(1024)(128)(4,1)S(1)}, s32[]{:S(2)}) async-start(s8[6291456]{0:T(1024)(128)(4,1)} %bitcast.139), calls=%async_computation.9 | async-start | bytes 8388608
  245.3 119.5 %copy-start.4 = (bf16[128,768]{1,0:T(8,128)(2,1)}, bf16[128,768]{1,0:T(8,128)(2,1)S(1)}, u32[]{:S(2)}) copy-start(bf16[128,768]{1,0:T(8,128)(2,1)S(1)} %get-tuple-element.38) | copy-start | bytes 589828
  333.6 31.2 %copy-start.25 = (bf16[1,128,768]{2,1,0:T(8,128)(2,1)S(1)}, bf16[1,128,768]{2,1,0:T(8,128)(2,1)}, u32[]{:S(2)}) copy-start(bf16[1,128,768]{2,1,0:T(8,128)(2,1)} %param.20) | copy-start | bytes 589828
  377.2 3.3 copy-start.40
  377.2 4.2 copy-start.3
  377.2 4.2 copy-start.16
  384.5 3.9 copy-start.13
  384.5 3.9 copy-start.23
  384.5 3.9 copy-start.28
  484.4 3.8 copy-start.14
  (23 other events, 46.2 us)
Sparse Core Ops, SparseCore 0:
  205.0 40.9 reduce-scatter.4
  248.5 75.8 reduce-scatter.2
where the time goes:
time: 500 us; the launch traced here: 499 us
  Pallas kernels  392 us (78%)
  matrix products  50 us (10%)
  local copies, waits for them, and re-layouts  29.6 us (6%)
  between operations  15.7 us (3%)
  other arithmetic  11.9 us (2%)
    pallas_call x2, Pallas kernels, ctx_scatter(): pl.pallas_call(scatter_kernel, out_shape=jax.ShapeDtypeStruct(block, x.dt...  117 us
    pallas_call x1, Pallas kernels, reduce_gradients(): pl.pallas_call(functools.partial(reduce_kernel, widths), out_shape=jax.Sh...  91.7 us
    pallas_call x1, Pallas kernels, gather_weights(): pl.pallas_call(functools.partial(weights_kernel, count), out_shape=[jax.S...  84.7 us
    pallas_call x1, Pallas kernels, ctx_gather(): pl.pallas_call(gather_kernel, out_shape=jax.ShapeDtypeStruct((N_CTX,) + x...  59.8 us
    dot_general x17, matrix products, contract(): lax.dot_general(left, right, (dims, ((), ())), preferred_element_type=F32)  39.6 us
    pallas_call x2, Pallas kernels, attend_back(): pl.pallas_call(functools.partial(backward_kernel, biased), grid=(PAIRS,),...  22.1 us
    pallas_call x2, Pallas kernels, attend(): pl.pallas_call(functools.partial(forward_kernel, biased), grid=(PAIRS,),...  17 us
    dot_general x9, matrix products, matmul(): return jnp.dot(left, right, preferred_element_type=F32)  10.4 us
  transfers between devices with their start and end apart: 2, of which 0 were waited for; matrix products, arithmetic and copies ran while one was open for 9% of the time, Pallas kernels for 28%

commit v1 on v0

--- a/solution.py
+++ b/solution.py
@@ -102,90 +102,6 @@
         ],
         compiler_params=pltpu.CompilerParams(collective_id=collective_id, has_side_effects=True),
         name="ctx_gather",
-    )(x)
-
-
-def scatter_kernel(
-    x_ref, out_ref, from_core, kept, from_row, stage, from_high,
-    send_a, recv_a, send_b, recv_b, send_c, recv_c,
-):
-    me, core, high, y = ctx_place()
-    sibling = slot_of(y, 0, high, 1 - core)
-    across = slot_of(y, 0, 1 - high, core)
-    rows = [slot_of(y, shift, high, core) for shift in (1, 2, 3)]
-    greet([sibling, across] + rows)
-    order = [(shift, half) for shift in (2, 1, 3, 0) for half in range(2)]
-    first = []
-    for index, (shift, half) in enumerate(order):
-        copy = remote(
-            x_ref.at[slot_of(y, shift, half, 1 - core)],
-            from_core.at[index],
-            send_a.at[index],
-            recv_a.at[index],
-            sibling,
-        )
-        copy.start()
-        first.append(copy)
-    second = []
-    for index, (shift, half) in enumerate(order):
-        first[index].wait_recv()
-        mine = x_ref[slot_of(y, shift, half, core)].astype(F32)
-        kept[index] = (mine + from_core[index].astype(F32)).astype(BF)
-        if half == 1 and shift:
-            spot = index // 2
-            copy = remote(
-                kept.at[pl.ds(index - 1, 2)],
-                from_row.at[spot],
-                send_b.at[spot],
-                recv_b.at[spot],
-                rows[shift - 1],
-            )
-            copy.start()
-            second.append(copy)
-    for copy in second:
-        copy.wait_recv()
-
-    def total(half):
-        result = kept[6 + half].astype(F32)
-        for spot in range(3):
-            result = result + from_row[spot, half].astype(F32)
-        return result
-
-    stage[...] = total(1 - high).astype(BF)
-    last = remote(stage, from_high, send_c, recv_c, across)
-    last.start()
-    mine = total(high)
-    last.wait_recv()
-    out_ref[...] = (mine + from_high[...].astype(F32)).astype(BF)
-    last.wait_send()
-    for copy in first + second:
-        copy.wait_send()
-
-
-def ctx_scatter(x, collective_id):
-    block = x.shape[1:]
-    return pl.pallas_call(
-        scatter_kernel,
-        out_shape=jax.ShapeDtypeStruct(block, x.dtype),
-        in_specs=[pl.BlockSpec(memory_space=pltpu.VMEM)],
-        out_specs=pl.BlockSpec(memory_space=pltpu.VMEM),
-        scratch_shapes=[
-            pltpu.VMEM((8,) + block, BF),
-            pltpu.VMEM((8,) + block, BF),
-            pltpu.VMEM((3, 2) + block, BF),
-            pltpu.VMEM(block, BF),
-            pltpu.VMEM(block, BF),
-            pltpu.SemaphoreType.DMA((8,)),
-            pltpu.SemaphoreType.DMA((8,)),
-            pltpu.SemaphoreType.DMA((3,)),
-            pltpu.SemaphoreType.DMA((3,)),
-            pltpu.SemaphoreType.DMA,
-            pltpu.SemaphoreType.DMA,
-        ],
-        compiler_params=pltpu.CompilerParams(
-            collective_id=collective_id, has_side_effects=True, vmem_limit_bytes=40 * MIB
-        ),
-        name="ctx_scatter",
     )(x)
 
 
@@ -315,23 +231,30 @@
 
 PIECE = 48
 ROOM = D + FF // 4 + FF // 8 + 128
-
-
-def reduce_kernel(widths, *refs):
-    count = len(widths)
-    parts = refs[:count]
-    wide_ref, down_ref, out_ref = refs[count : count + 3]
+EARLY = (2 * FF, D, D, D, D)
+WIDTHS = EARLY + (2 * D, 2 * D, 256)
+SPAN = sum(WIDTHS)
+DOWN = len(WIDTHS)
+
+
+def finish_kernel(*refs):
     (
-        from_core, kept, from_z, held, from_x, wide_in, down_in, packed, from_ctx, total_ref,
-        core_send, core_recv, z_send, z_recv, x_send, x_recv,
-        ctx_send, ctx_recv, out_send, out_recv, pass_send, pass_recv, local_sem,
-    ) = refs[count + 3 :]
+        dckv_ref, dkv_ref, wide_ref, two_out_ref, two_query_ref, one_out_ref, one_query_ref, down_ref,
+        normed_ref, states_ref, kv_ref, ckv_ref, dn_ref, dmid_ref, token_ref, gain_ref, extra_ref,
+        out_ref, decoder_ref, encoder_ref,
+        kept, from_core, from_z, from_x, d_kept, d_core, d_z, d_x,
+        s_kept, s_core, s_row, s_stage, s_high, c_kept, c_core, c_row, c_stage, c_high,
+        to_core, gain_cols, packed, from_ctx, total_ref,
+        s_sem, c_sem, local_sem, core_send, core_recv, z_send, z_recv, x_send, x_recv,
+        ctx_send, ctx_recv, out_send, out_recv, pass_send, pass_recv, own_sem,
+    ) = refs
     me, core, high, y, low, x = torus_place()
     shard = low * 4 + x
     rank = y * 2 + high
     sibling = (slot_of(y, 0, high, 1 - core), shard)
     inside = (me, (1 - low) * 4 + x)
     outside = (slot_of(y, 0, 1 - high, core), (1 - low) * 4 + x)
+    across = (slot_of(y, 0, 1 - high, core), shard)
     others = [low * 4 + (x + shift) % 4 for shift in (1, 2, 3)]
     shifts = [(dy, dz) for dy in range(4) for dz in range(2)][1:]
     mates = [((y + dy) % 4) * 2 + (high + dz) % 2 for dy, dz in shifts]
@@ -344,8 +267,6 @@
     theirs = pl.ds(pl.multiple_of((1 - core) * PIECE, 16), PIECE)
     mine_down = pl.ds(pl.multiple_of(core * 128, 16), 128)
     theirs_down = pl.ds(pl.multiple_of((1 - core) * 128, 16), 128)
-    starts = [sum(widths[:k]) for k in range(count)]
-    cuts = [pl.ds(starts[k], widths[k]) for k in range(count)]
     sends = []
 
     def go(src, dst, send_sem, recv_sem, device):
@@ -354,53 +275,131 @@
         sends.append(copy)
         return copy
 
-    over_core = [
-        go(
-            parts[k].at[:, theirs, :],
-            from_core.at[:, :, cuts[k]],
+    def bring(src, dst, sem):
+        copy = pltpu.make_async_copy(src, dst, sem)
+        copy.start()
+        return copy
+
+
+    def rows_start(source, held, arrived, sem, base):
+        over = []
+        local = []
+        for spot, shift in enumerate((2, 1, 3, 0)):
+            pair = pl.ds(((y + shift) % 4) * 2, 2)
+            block = pl.ds(2 * spot, 2)
+            over.append(
+                go(
+                    source.at[pair, 1 - core], arrived.at[block],
+                    sem.at[0, spot], sem.at[1, spot], sibling,
+                )
+            )
+            local.append(bring(source.at[pair, core], held.at[block], local_sem.at[base + spot]))
+        return over, local
+
+    def rows_send(copies, held, arrived, row, sem):
+        over, local = copies
+        onward = []
+        for spot, shift in enumerate((2, 1, 3, 0)):
+            local[spot].wait()
+            over[spot].wait_recv()
+            for block in (2 * spot, 2 * spot + 1):
+                for part in range(2):
+                    held[block, part] = held[block, part] + arrived[block, part]
+            if shift:
+                onward.append(
+                    go(
+                        held.at[pl.ds(2 * spot, 2)], row.at[spot],
+                        sem.at[2, spot], sem.at[3, spot], (others_ctx[shift - 1], shard),
+                    )
+                )
+        return onward
+
+    others_ctx = [slot_of(y, shift, high, core) for shift in (1, 2, 3)]
+
+    def rows_total(held, row, half, part):
+        result = held[6 + half, part].astype(F32)
+        for spot in range(3):
+            result = result + row[spot, half, part].astype(F32)
+        return result
+
+    def rows_across(onward, held, row, stage, landing, sem):
+        for copy in onward:
+            copy.wait_recv()
+        for part in range(2):
+            stage[part] = rows_total(held, row, 1 - high, part).astype(BF)
+        return go(stage, landing, sem.at[2, 3], sem.at[3, 3], across)
+
+    def rows_sum(last, held, row, landing):
+        totals = [rows_total(held, row, high, part) for part in range(2)]
+        last.wait_recv()
+        return jnp.concatenate(
+            [(totals[part] + landing[part].astype(F32)).astype(BF) for part in range(2)], axis=1
+        )
+
+
+    starts = [sum(WIDTHS[:k]) for k in range(len(WIDTHS))]
+
+    def buffers(k):
+        if k == DOWN:
+            return d_kept, d_core, d_z, d_x, 0, D
+        return kept, from_core, from_z, from_x, starts[k], WIDTHS[k]
+
+    over_core, over_z, over_x, brought = {}, {}, {}, {}
+
+    def chunk_start(k, source):
+        held, arrived, _, _, start, width = buffers(k)
+        cut = pl.ds(start, width)
+        rows, far_rows = (mine_down, theirs_down) if k == DOWN else (mine, theirs)
+        over_core[k] = go(
+            source.at[:, far_rows, :], arrived.at[:, :, cut], core_send.at[k], core_recv.at[k], sibling
+        )
+        brought[k] = bring(source.at[:, rows, :], held.at[:, :, cut], local_sem.at[8 + k])
+
+    def chunk_send(k, offset):
+        width = WIDTHS[k]
+        over_core[k] = go(
+            to_core.at[:, :, pl.ds(offset, width)],
+            from_core.at[:, :, pl.ds(starts[k], width)],
             core_send.at[k],
             core_recv.at[k],
             sibling,
         )
-        for k in range(count)
-    ]
-    wide_copy = go(wide_ref.at[theirs, :], wide_in, core_send.at[count], core_recv.at[count], sibling)
-    down_copy = go(
-        down_ref.at[theirs_down, :], down_in, core_send.at[count + 1], core_recv.at[count + 1], sibling
-    )
-    over_z = [None] * count
-    over_x = [None] * count
 
     def step_core(k):
+        held, arrived, landing, _, start, width = buffers(k)
+        cut = pl.ds(start, width)
+        if k in brought:
+            brought[k].wait()
         over_core[k].wait_recv()
-        half = widths[k] // 2
-        away = pl.ds(4 * (1 - low), 4)
-        for owner in range(8):
-            kept[owner, :, cuts[k]] = (
-                parts[k][owner, mine, :].astype(F32) + from_core[owner, :, cuts[k]].astype(F32)
-            ).astype(BF)
+        for column in range(4):
+            owner = 4 * (1 - low) + column
+            held[owner, :, cut] = held[owner, :, cut] + arrived[owner, :, cut]
+        half = width // 2
         over_z[k] = [
             go(
-                kept.at[away, :, pl.ds(starts[k] + side * half, half)],
-                from_z.at[:, :, pl.ds(starts[k] + side * half, half)],
+                held.at[pl.ds(4 * (1 - low), 4), :, pl.ds(start + side * half, half)],
+                landing.at[:, :, pl.ds(start + side * half, half)],
                 z_send.at[k, side],
                 z_recv.at[k, side],
                 device,
             )
             for side, device in enumerate((inside, outside))
         ]
+        for column in range(4):
+            owner = 4 * low + column
+            held[owner, :, cut] = held[owner, :, cut] + arrived[owner, :, cut]
 
     def step_z(k):
+        held, _, landing, spread, start, width = buffers(k)
+        cut = pl.ds(start, width)
         for copy in over_z[k]:
             copy.wait_recv()
         for column in range(4):
-            held[column, :, cuts[k]] = (
-                kept[4 * low + column, :, cuts[k]].astype(F32) + from_z[column, :, cuts[k]].astype(F32)
-            ).astype(BF)
+            landing[column, :, cut] = landing[column, :, cut] + held[4 * low + column, :, cut]
         over_x[k] = [
             go(
-                held.at[(x + spot + 1) % 4, :, cuts[k]],
-                from_x.at[spot, :, cuts[k]],
+                landing.at[(x + spot + 1) % 4, :, cut],
+                spread.at[spot, :, cut],
                 x_send.at[k, spot],
                 x_recv.at[k, spot],
                 (me, others[spot]),
@@ -408,42 +407,96 @@
             for spot in (1, 0, 2)
         ]
 
-    def step_x(k):
+    def step_x(k, first=None):
+        _, _, landing, spread, start, width = buffers(k)
+        cut = pl.ds(start, width)
         for copy in over_x[k]:
             copy.wait_recv()
-        total = held[x, :, cuts[k]].astype(F32)
+        total = landing[x, :, cut].astype(F32)
         for spot in range(3):
-            total = total + from_x[spot, :, cuts[k]].astype(F32)
+            total = total + spread[spot, :, cut].astype(F32)
         total = total.astype(BF)
-        if widths[k] % D:
-            packed[0, :, ROOM - 128 :] = total[:, :128]
-            for piece in range(1, 8):
-                packed[piece, :, ROOM - 128 :] = jnp.zeros((PIECE, 128), BF)
-            return
-        for piece in range(widths[k] // D):
-            packed[starts[k] // D + piece, :, :D] = total[:, piece * D : (piece + 1) * D]
-
-    for k in range(count + 2):
-        if k < count:
-            step_core(k)
-        if 0 <= k - 1 < count:
-            step_z(k - 1)
-        if k - 2 >= 0:
-            step_x(k - 2)
-        if k == 1:
-            wide_copy.wait_recv()
+        if k == 0:
             for piece in range(8):
-                cut = slice(piece * 512, piece * 512 + 512)
-                packed[piece, :, D : D + 512] = (
-                    wide_ref[mine, cut].astype(F32) + wide_in[:, cut].astype(F32)
-                ).astype(BF)
-            down_copy.wait_recv()
-            total = (down_ref[mine_down, :].astype(F32) + down_in[...].astype(F32)).astype(BF)
+                packed[piece, :, D : D + 512] = total[:, piece * 512 : piece * 512 + 512]
+        elif k == DOWN:
             for piece in range(8):
                 for part in range(3):
                     packed[piece, part * 16 : part * 16 + 16, D + 512 : D + 768] = total[
                         piece * 16 : piece * 16 + 16, part * 256 : part * 256 + 256
                     ]
+        elif k == len(WIDTHS) - 1:
+            packed[0, :, ROOM - 128 :] = total[:, :128]
+            for piece in range(1, 8):
+                packed[piece, :, ROOM - 128 :] = jnp.zeros((PIECE, 128), BF)
+        else:
+            for piece in range(width // D):
+                packed[first + piece, :, :D] = total[:, piece * D : (piece + 1) * D]
+
+    def outer(left_ref, rows, right):
+        left = left_ref[:, rows, :]
+        return contract(left.reshape(8 * PIECE, left.shape[-1]), right, ((1,), (0,))).astype(BF).reshape(
+            8, PIECE, right.shape[-1]
+        )
+
+    c_copies = rows_start(dckv_ref, c_kept, c_core, c_sem, 0)
+    s_copies = rows_start(dkv_ref, s_kept, s_core, s_sem, 4)
+    for k, source in enumerate((wide_ref, two_out_ref, two_query_ref, one_out_ref, one_query_ref)):
+        chunk_start(k, source)
+        if k == 0:
+            chunk_start(DOWN, down_ref)
+    c_onward = rows_send(c_copies, c_kept, c_core, c_row, c_sem)
+    s_onward = rows_send(s_copies, s_kept, s_core, s_row, s_sem)
+    for k in (0, DOWN, 1, 2, 3, 4):
+        step_core(k)
+    step_z(0)
+    c_last = rows_across(c_onward, c_kept, c_row, c_stage, c_high, c_sem)
+    step_z(DOWN)
+    d_ckv = rows_sum(c_last, c_kept, c_row, c_high)
+    to_core[:, :, : 2 * D] = outer(states_ref, theirs, d_ckv)
+    chunk_send(5, 0)
+    kept[:, :, starts[5] : starts[5] + 2 * D] = outer(states_ref, mine, d_ckv)
+    encoder_ref[...] = contract(d_ckv, ckv_ref[...], ((1,), (1,)))
+    for k in (1, 2, 3, 4):
+        step_z(k)
+    step_core(5)
+    step_x(0)
+    step_x(DOWN)
+    s_last = rows_across(s_onward, s_kept, s_row, s_stage, s_high, s_sem)
+    step_z(5)
+    for k in (1, 2, 3, 4):
+        step_x(k, k - 1)
+    d_kv = rows_sum(s_last, s_kept, s_row, s_high)
+    over_core[5].wait_send()
+    to_core[:, :, : 2 * D] = outer(normed_ref, theirs, d_kv)
+    chunk_send(6, 0)
+    kept[:, :, starts[6] : starts[6] + 2 * D] = outer(normed_ref, mine, d_kv)
+    tokens = token_ref[...].astype(F32)
+    grad = dn_ref[...] + contract(d_kv, kv_ref[...], ((1,), (1,)))
+    inverse = lax.rsqrt(jnp.mean(tokens * tokens, axis=-1, keepdims=True) + 1e-06)
+    columns = contract(
+        (tokens * inverse * grad).astype(BF), jnp.ones((TOK, 128), BF), ((0,), (0,))
+    )
+    lane = lax.broadcasted_iota(jnp.int32, (D, 128), 1)
+    gain_cols[...] = jnp.where(lane == 0, columns, 0.0).astype(BF).reshape(8, 2 * PIECE, 128)
+    to_core[:, :, 2 * D : 2 * D + 128] = gain_cols[:, theirs, :] + extra_ref[:, theirs, :128]
+    to_core[:, :, 2 * D + 128 :] = extra_ref[:, theirs, 128:]
+    chunk_send(7, 2 * D)
+    kept[:, :, starts[7] : starts[7] + 128] = gain_cols[:, mine, :] + extra_ref[:, mine, :128]
+    kept[:, :, starts[7] + 128 :] = extra_ref[:, mine, 128:]
+    step_core(6)
+    step_core(7)
+    step_x(5, 4)
+    step_z(6)
+    step_z(7)
+    scaled = gain_ref[...] * grad
+    mixed = jnp.mean(tokens * scaled, axis=-1, keepdims=True)
+    decoder_ref[...] = (
+        dmid_ref[...] + inverse * scaled - tokens * (inverse * inverse * inverse * mixed)
+    )
+    step_x(6, 6)
+    step_x(7)
+
 
     over_ctx = [
         go(
@@ -469,8 +522,7 @@
             (mate * 2 + core, shard),
         )
     go(total_ref, out_ref.at[rank, mine, :], pass_send.at[7], pass_recv.at[rank], sibling)
-    own = pltpu.make_async_copy(total_ref, out_ref.at[rank, mine, :], local_sem)
-    own.start()
+    own = bring(total_ref, out_ref.at[rank, mine, :], own_sem)
 
     def landed(ref, recv_sem):
         hop(ref, ref, pass_send.at[0], recv_sem, *sibling).wait_recv()
@@ -483,36 +535,64 @@
         landed(out_ref.at[mate, theirs, :], pass_recv.at[mate])
     own.wait()
     for copy in sends:
-        copy.wait_send()
-
-
-def reduce_gradients(parts, wide, down, collective_id):
-    widths = [part.shape[2] for part in parts]
-    count = len(parts)
-    span = sum(widths)
+        if copy is not over_core[5]:
+            copy.wait_send()
+
+
+def finish(far, near, collective_id):
     dma = pltpu.SemaphoreType.DMA
+    chunks = len(WIDTHS) + 1
+
+    def rows(count):
+        return [
+            pltpu.VMEM((8, 2, count, D), BF),
+            pltpu.VMEM((8, 2, count, D), BF),
+            pltpu.VMEM((3, 2, 2, count, D), BF),
+            pltpu.VMEM((2, count, D), BF),
+            pltpu.VMEM((2, count, D), BF),
+        ]
+
     return pl.pallas_call(
-        functools.partial(reduce_kernel, widths),
-        out_shape=jax.ShapeDtypeStruct((8, 2 * PIECE, ROOM), BF),
-        in_specs=[pl.BlockSpec(memory_space=pltpu.VMEM)] * (count + 2),
-        out_specs=pl.BlockSpec(memory_space=pl.ANY),
+        finish_kernel,
+        out_shape=[
+            jax.ShapeDtypeStruct((8, 2 * PIECE, ROOM), BF),
+            jax.ShapeDtypeStruct((TOK, D), F32),
+            jax.ShapeDtypeStruct((ENC, D), F32),
+        ],
+        in_specs=[pl.BlockSpec(memory_space=pl.ANY)] * len(far)
+        + [pl.BlockSpec(memory_space=pltpu.VMEM)] * len(near),
+        out_specs=[
+            pl.BlockSpec(memory_space=pl.ANY),
+            pl.BlockSpec(memory_space=pltpu.VMEM),
+            pl.BlockSpec(memory_space=pltpu.VMEM),
+        ],
         scratch_shapes=[
-            pltpu.VMEM((8, PIECE, span), BF),
-            pltpu.VMEM((8, PIECE, span), BF),
-            pltpu.VMEM((4, PIECE, span), BF),
-            pltpu.VMEM((4, PIECE, span), BF),
-            pltpu.VMEM((3, PIECE, span), BF),
-            pltpu.VMEM((PIECE, wide.shape[1]), BF),
-            pltpu.VMEM((128, down.shape[1]), BF),
+            pltpu.VMEM((8, PIECE, SPAN), BF),
+            pltpu.VMEM((8, PIECE, SPAN), BF),
+            pltpu.VMEM((4, PIECE, SPAN), BF),
+            pltpu.VMEM((3, PIECE, SPAN), BF),
+            pltpu.VMEM((8, 128, D), BF),
+            pltpu.VMEM((8, 128, D), BF),
+            pltpu.VMEM((4, 128, D), BF),
+            pltpu.VMEM((3, 128, D), BF),
+        ]
+        + rows(TOK)
+        + rows(ENC)
+        + [
+            pltpu.VMEM((8, PIECE, 2 * D + 256), BF),
+            pltpu.VMEM((8, 2 * PIECE, 128), BF),
             pltpu.VMEM((8, PIECE, ROOM), BF),
             pltpu.VMEM((7, PIECE, ROOM), BF),
             pltpu.VMEM((PIECE, ROOM), BF),
-            dma((count + 2,)),
-            dma((count + 2,)),
-            dma((count, 2)),
-            dma((count, 2)),
-            dma((count, 3)),
-            dma((count, 3)),
+            dma((4, 4)),
+            dma((4, 4)),
+            dma((8 + chunks,)),
+            dma((chunks,)),
+            dma((chunks,)),
+            dma((chunks, 2)),
+            dma((chunks, 2)),
+            dma((chunks, 3)),
+            dma((chunks, 3)),
             dma((7,)),
             dma((7,)),
             dma((7,)),
@@ -522,10 +602,10 @@
             dma,
         ],
         compiler_params=pltpu.CompilerParams(
-            collective_id=collective_id, has_side_effects=True, vmem_limit_bytes=56 * MIB
+            collective_id=collective_id, has_side_effects=True, vmem_limit_bytes=60 * MIB
         ),
-        name="reduce_gradients",
-    )(*parts, wide, down)
+        name="finish_gradients",
+    )(*far, *near)
 
 
 def split_heads(block):
@@ -795,10 +875,6 @@
     return jnp.concatenate([sums[:, :-1], far], axis=1)
 
 
-def owned_rows(grad):
-    return lax.psum_scatter(grad, "fsdp", scatter_dimension=0, tiled=True)
-
-
 def body(
     decoder_in,
     encoder_states,
@@ -902,8 +978,8 @@
 
     d_hidden = transposed_right(upstream, down)
     d_gate_up = jnp.concatenate(pull_feed(d_hidden), axis=1).astype(BF)
-    grad_down = owned_rows(transposed_left(hidden, upstream).astype(BF))
-    grad_gate_up = owned_rows(transposed_left(normed_three, d_gate_up).astype(BF))
+    grad_down = transposed_left(hidden, upstream).astype(BF)
+    grad_gate_up = transposed_left(normed_three, d_gate_up).astype(BF)
     d_normed_three = transposed_right(d_gate_up, gate_up)
     part_three, grad_norm_three = rms_back(mid_two, norm_three, d_normed_three)
     d_mid_two = upstream.astype(F32) + part_three
@@ -912,12 +988,8 @@
     d_cross_queries, d_cross_kv_all = attend_back(
         cross_queries, gathered, d_cross_attended, cross_totals, ENC, 2
     )
-    d_cross_kv = ctx_scatter(d_cross_kv_all, 1)
-    d_cross_kv = jnp.concatenate([d_cross_kv[0], d_cross_kv[1]], axis=1)
-    grad_encoder = transposed_right(d_cross_kv, kv_two)
     grad_out_two = transposed_left(cross_attended, cross_branch).astype(BF)
     grad_query_two = transposed_left(normed_two, d_cross_queries).astype(BF)
-    grad_kv_two = transposed_left(states, d_cross_kv).astype(BF)
     d_normed_two = transposed_right(d_cross_queries, query_two)
     part_two, grad_norm_two = rms_back(mid_one, norm_two, d_normed_two)
     d_mid_one = d_mid_two + part_two
@@ -926,15 +998,10 @@
     d_queries, d_kv_all, strips = attend_back(
         queries, gathered, d_attended, self_totals, TOK, 0, classes, near, tiles
     )
-    d_kv = ctx_scatter(d_kv_all, 2)
-    d_qkv = jnp.concatenate([d_queries, d_kv[0], d_kv[1]], axis=1)
-    d_normed_one = transposed_right(d_qkv, qkv_one)
-    part_one, grad_norm_one = rms_back(tokens, norm_one, d_normed_one)
-    grad_decoder = d_mid_one + part_one
     grad_table = matmul(bias_sums(strips), bucket_hot.astype(F32)).T.reshape(8, 4, HEADS)
     grad_extra = jnp.concatenate(
         [
-            grad_norm_one[:, None],
+            jnp.zeros((D, 1), F32),
             grad_norm_two[:, None],
             grad_norm_three[:, None],
             jnp.zeros((D, 5), F32),
@@ -944,16 +1011,29 @@
         axis=1,
     )
     grad_out_one = transposed_left(attended, self_branch).astype(BF)
-    grad_qkv_one = transposed_left(normed_one, d_qkv).astype(BF)
-    summed = reduce_gradients(
+    grad_query_one = transposed_left(normed_one, d_queries).astype(BF)
+    summed, grad_decoder, grad_encoder = finish(
         [
-            part.astype(BF).reshape(8, rows, -1)
-            for part in (
-                grad_out_two, grad_query_two, grad_kv_two, grad_out_one, grad_qkv_one, grad_extra,
-            )
-        ],
-        grad_gate_up,
-        grad_down,
+            d_cross_kv_all.reshape(8, 2, 2, ENC, D),
+            d_kv_all.reshape(8, 2, 2, TOK, D),
+            grad_gate_up.reshape(8, rows, -1),
+            grad_out_two.reshape(8, rows, D),
+            grad_query_two.reshape(8, rows, D),
+            grad_out_one.reshape(8, rows, D),
+            grad_query_one.reshape(8, rows, D),
+            grad_down.reshape(8, -1, D),
+        ],
+        [
+            normed_one.T.reshape(8, rows, TOK),
+            states.T.reshape(8, rows, ENC),
+            qkv_one[:, D:],
+            kv_two,
+            transposed_right(d_queries, qkv_one[:, :D]),
+            d_mid_one,
+            decoder_in[0],
+            norm_one,
+            grad_extra.astype(BF).reshape(8, rows, 256),
+        ],
         3,
     )
     owned = summed[:, :, :D].astype(F32)
@@ -967,15 +1047,15 @@
         grad_decoder[None],
         grad_encoder[None],
         extras[:, 0],
-        owned[5],
+        owned[3],
         owned[6],
         owned[7],
-        owned[4],
+        owned[2],
         extras[:4, 8:20],
         extras[:, 1],
         owned[1],
-        owned[2],
-        owned[3],
+        owned[4],
+        owned[5],
         owned[0],
         extras[:, 2],
         wide[:, :FF],

time: 500 us -> 423 us (0.85)
  Pallas kernels: 392 us -> 330 us
  between operations: 15.7 us -> 2.24 us
  matrix products: 50 us -> 37 us
  local copies, waits for them, and re-layouts: 29.6 us -> 37.1 us
    pallas_call x3 -> x1, Pallas kernels: 208 us -> 147 us  [finish(): pl.pallas_call(finish_kernel, out_shape=[jax.ShapeDtypeStruct((8, 2 * PIE...]
    dot_general x17 -> x15, matrix products: 39.6 us -> 27.4 us  [contract(): lax.dot_general(left, right, (dims, ((), ())), preferred_element_type=F32)]
    unnamed x110 -> x130, local copies, waits for them, and re-layouts: 9.99 us -> 10.2 us
  transfers between devices with their start and end apart: 2 -> 0, of which waited for: 0 -> 0; matrix products, arithmetic and copies ran while one was open for 9% -> 0% of each run, Pallas kernels for 28% -> 0%
where the time goes in v1:
time: 423 us; the launch traced here: 421 us
  Pallas kernels  330 us (78%)
  local copies, waits for them, and re-layouts  37.1 us (9%)
  matrix products  37 us (9%)
  other arithmetic  14.6 us (3%)
    pallas_call x1, Pallas kernels, finish(): pl.pallas_call(finish_kernel, out_shape=[jax.ShapeDtypeStruct((8, 2 * PIE...  147 us
    pallas_call x1, Pallas kernels, gather_weights(): pl.pallas_call(functools.partial(weights_kernel, count), out_shape=[jax.S...  84.7 us
    pallas_call x1, Pallas kernels, ctx_gather(): pl.pallas_call(gather_kernel, out_shape=jax.ShapeDtypeStruct((N_CTX,) + x...  59.8 us
    dot_general x15, matrix products, contract(): lax.dot_general(left, right, (dims, ((), ())), preferred_element_type=F32)  27.4 us
    pallas_call x2, Pallas kernels, attend_back(): pl.pallas_call(functools.partial(backward_kernel, biased), grid=(PAIRS,),...  22 us
    pallas_call x2, Pallas kernels, attend(): pl.pallas_call(functools.partial(forward_kernel, biased), grid=(PAIRS,),...  17.2 us
    unnamed x130, local copies, waits for them, and re-layouts  10.2 us
    dot_general x9, matrix products, matmul(): return jnp.dot(left, right, preferred_element_type=F32)  9.57 us

profile of v1, /device:TPU:1, one launch (start us, length us, event | category | flops | bytes accessed | tf_op | source)
XLA Modules:
  0.0 421.2 jit_solution(6856028242714387339)
XLA Ops:
  8.0 2.1 concatenate.34.refs_0_
  12.2 84.7 %gather_weights.1 = (bf16[8,96,4096]{2,1,0:T(8,128)(2,1)}, bf16[8,96,6400]{2,1,0:T(8,128)(2,1)}, bf16[8,256,768]{2,1,0:T(8,128)(2,1)}) custom-call(bf16[96,4096]{1,0:T(8,128)(2,1)} %concatenate.34.refs_0_, bf16[96,6400]{1,0:T(8,128)(2,1)} %copy-done.23, bf16[256,768]{1,0:T(8,128)(2,1)} %refs_2_.1), custom_call_target="tpu_custom_call" | custom-call | tf_op jit(solution)/shard_map/gather_weights/pallas_call | solution.py:215
  99.3 2.7 convolution_convert_fusion.1
  102.1 2.2 fusion.15
  105.3 59.8 %ctx_gather.1.refs_2_.refs_3_.refs_1_.refs_4_ = bf16[16,2,192,768]{3,2,1,0:T(8,128)(2,1)} custom-call(bf16[2,192,768]{2,1,0:T(8,128)(2,1)} %pad_maximum_fusion.3.x_ref), custom_call_target="tpu_custom_call" | custom-call | tf_op jit(solution)/shard_map/ctx_gather/pallas_call | solution.py:93
  166.5 1.3 fusion.2
  171.2 10.2 %attend_self.1 = (bf16[128,768]{1,0:T(8,128)(2,1)S(1)}, f32[6,8,256]{2,1,0:T(8,128)S(1)}) custom-call(s32[2,32]{1,0:T(2,128)S(1)} %compare_select_fusion.1.refs_0_, bf16[128,768]{1,0:T(8,128)(2,1)S(1)} %get-tuple-element.77.refs_1_.refs_2_, bf16[16,2,192,768]{3,2,1,0:T(8,128)(2,1)} %ctx_gather.1.refs_2_.refs_3_.refs_1_.refs_4_, ...), custom_call_target="tpu_custom_call" | custom-call | flops 1000000000 | bytes 10000000 | tf_op jit(solution)/shard_map/attend_self/pallas_call | solution.py:762
  183.3 7.0 %attend_cross.1 = (bf16[128,768]{1,0:T(8,128)(2,1)S(1)}, f32[6,8,256]{2,1,0:T(8,128)S(1)}) custom-call(bf16[128,768]{1,0:T(8,128)(2,1)S(1)} %convolution_convert_fusion.10.refs_0_, bf16[16,2,192,768]{3,2,1,0:T(8,128)(2,1)} %ctx_gather.1.refs_2_.refs_3_.refs_1_.refs_4_, bf16[16,2,192,768]{3,2,1,0:T(8,128)(2,1)} %ctx_gather.1.refs_2_.refs_3_.refs_1_.refs_4_), custom_call_target="tpu_custom_call" | custom-call | flops 1000000000 | bytes 10000000 | tf_op jit(solution)/shard_map/attend_cross/pallas_call | solution.py:762
  192.7 1.6 fusion.25
  194.3 1.4 fusion.16
  195.7 2.7 multiply_reduce_fusion
  199.2 8.2 %attend_cross_back.1 = (bf16[128,768]{1,0:T(8,128)(2,1)S(1)}, bf16[16,2,64,768]{3,2,1,0:T(8,128)(2,1)S(1)}) custom-call(bf16[128,768]{1,0:T(8,128)(2,1)S(1)} %convolution_convert_fusion.10.refs_0_, bf16[16,2,192,768]{3,2,1,0:T(8,128)(2,1)} %ctx_gather.1.refs_2_.refs_3_.refs_1_.refs_4_, bf16[16,2,192,768]{3,2,1,0:T(8,128)(2,1)} %ctx_gather.1.refs_2_.refs_3_.refs_1_.refs_4_, ...), custom_call_target="tpu_custom_call" | custom-call | flops 3000000000 | bytes 10000000 | tf_op jit(solution)/shard_map/attend_cross_back/pallas_call | solution.py:799
  207.4 1.7 copy-done
  210.7 2.5 multiply_reduce_fusion.1
  213.9 1.5 subtract_add_fusion
  215.4 2.0 convolution_convert_fusion.8.refs_5_
  217.4 13.8 %attend_self_back.1 = (bf16[128,768]{1,0:T(8,128)(2,1)S(1)}, bf16[16,2,128,768]{3,2,1,0:T(8,128)(2,1)}, f32[12,3,64,128]{3,2,1,0:T(8,128)S(1)}) custom-call(s32[2,32]{1,0:T(2,128)S(1)} %compare_select_fusion.1.refs_0_, s32[2,3]{1,0:T(2,128)S(1)} %copy.71.refs_1_, bf16[128,768]{1,0:T(8,128)(2,1)S(1)} %get-tuple-element.77.refs_1_.refs_2_, ...), custom_call_target="tpu_custom_call" | custom-call | flops 3000000000 | bytes 10000000 | tf_op jit(solution)/shard_map/attend_self_back/pallas_call | solution.py:799
  231.3 4.5 %convolution_convert_fusion = bf16[768,4096]{1,0:T(8,128)(2,1)} fusion(bf16[128,2048]{1,0:T(8,128)(2,1)S(1)} %copy-done.32, bf16[128,2048]{1,0:T(8,128)(2,1)S(1)} %copy-done.30, f32[128,768]{1,0:T(8,128)S(1)} %copy-done.12, f32[768]{0:T(1024)S(1)} %get-tuple-element.55, f32[128]{0:T(128)S(1)} %copy-done.44), kind=kOutput, calls=%fused_computation.5 | convolution fusion | flops 810844160 | bytes 7736832 | tf_op jit(solution)/shard_map/dot_general | solution.py:626
  235.9 1.6 convolution_convert_fusion.7
  237.5 1.6 convolution_convert_fusion.6
  239.1 1.5 convolution_convert_fusion.5
  240.7 1.6 convolution_convert_fusion.4
  242.3 2.7 convolution_convert_fusion.2
  246.6 4.8 %fusion.74 = (bf16[768,1536]{1,0:T(8,128)(2,1)}, bf16[768,1536]{1,0:T(8,128)(2,1)}) fusion(bf16[768,4096]{1,0:T(8,128)(2,1)} %bitcast.124), kind=kLoop, calls=%fused_computation.163 | loop fusion | bytes 9437184 | tf_op jit(solution)/shard_map/slice | solution.py:925
  251.4 2.6 fusion.17.refs_12_
  256.0 1.4 slice_add_fusion
  257.4 1.7 reshape.242
  261.7 1.3 concatenate.44.refs_16_
  263.0 146.6 %finish_gradients.1 = (bf16[8,96,1664]{2,1,0:T(8,128)(2,1)}, f32[128,768]{1,0:T(8,128)}, f32[64,768]{1,0:T(8,128)}) custom-call(bf16[8,2,2,64,768]{4,3,2,1,0:T(8,128)(2,1)} %bitcast.106, bf16[8,2,2,128,768]{4,3,2,1,0:T(8,128)(2,1)} %bitcast.120, bf16[8,96,4096]{2,1,0:T(8,128)(2,1)} %bitcast.107, bf16[8,96,768]{2,1,0:T(8,128)(2,1)} %bitcast.126, ...), custom_call_target="tpu_custom_call" | custom-call | tf_op jit(solution)/shard_map/finish_gradients/pallas_call | solution.py:555
  411.1 1.5 slice_convert_fusion
  412.6 1.4 slice_bitcast_fusion
  414.6 1.3 convert_bitcast_fusion
  (209 shorter events, 37.5 us)
Async XLA Ops:
  0.7 10.4 %copy-start.37 = (bf16[96,768]{1,0:T(8,128)(2,1)S(1)}, bf16[96,768]{1,0:T(8,128)(2,1)}, u32[]{:S(2)}) copy-start(bf16[96,768]{1,0:T(8,128)(2,1)} %param.32) | copy-start | bytes 442372
  0.7 10.4 %copy-start.38 = (bf16[96,768]{1,0:T(8,128)(2,1)S(1)}, bf16[96,768]{1,0:T(8,128)(2,1)}, u32[]{:S(2)}) copy-start(bf16[96,768]{1,0:T(8,128)(2,1)} %param.35) | copy-start | bytes 442372
  0.7 10.4 %copy-start.33 = (bf16[96,2048]{1,0:T(8,128)(2,1)S(1)}, bf16[96,2048]{1,0:T(8,128)(2,1)}, u32[]{:S(2)}) copy-start(bf16[96,2048]{1,0:T(8,128)(2,1)} %param.37) | copy-start | bytes 1179652
  0.7 10.4 %copy-start.34 = (bf16[96,2048]{1,0:T(8,128)(2,1)S(1)}, bf16[96,2048]{1,0:T(8,128)(2,1)}, u32[]{:S(2)}) copy-start(bf16[96,2048]{1,0:T(8,128)(2,1)} %param.38) | copy-start | bytes 1179652
  2.3 5.7 %copy-start.45 = (s32[32]{0:T(128)}, s32[32]{0:T(128)S(1)}, u32[]{:S(2)}) copy-start(s32[32]{0:T(128)S(1)} %sub.86) | copy-start | bytes 388
  11.1 87.5 %copy-start.18 = (bf16[1,128,768]{2,1,0:T(8,128)(2,1)S(1)}, bf16[1,128,768]{2,1,0:T(8,128)(2,1)}, u32[]{:S(2)}) copy-start(bf16[1,128,768]{2,1,0:T(8,128)(2,1)} %param.20) | copy-start | bytes 589828
  98.7 83.4 %copy-start.41 = (f32[768]{0:T(1024)}, f32[768]{0:T(1024)S(1)}, u32[]{:S(2)}) copy-start(f32[768]{0:T(1024)S(1)} %get-tuple-element.57) | copy-start | bytes 9220
  105.3 60.6 %copy-start.55 = (s32[128]{0:T(128)S(1)}, s32[128]{0:T(128)}, u32[]{:S(2)}) copy-start(s32[128]{0:T(128)} %param.24) | copy-start | bytes 1540
  170.5 10.8 %slice-start = ((s8[9830400]{0:T(1024)(128)(4,1)}), s8[4194304]{0:T(1024)(128)(4,1)S(1)}, s32[]{:S(2)}) async-start(s8[9830400]{0:T(1024)(128)(4,1)} %bitcast.111), calls=%async_computation | async-start | bytes 8388608
  171.1 10.3 %slice-start.1 = ((s8[9830400]{0:T(1024)(128)(4,1)}), s8[4194304]{0:T(1024)(128)(4,1)S(1)}, s32[]{:S(2)}) async-start(s8[9830400]{0:T(1024)(128)(4,1)} %bitcast.111), calls=%async_computation.1 | async-start | bytes 8388608
  171.1 10.3 %slice-start.2 = ((s8[9830400]{0:T(1024)(128)(4,1)}), s8[1441792]{0:T(1024)(128)(4,1)S(1)}, s32[]{:S(2)}) async-start(s8[9830400]{0:T(1024)(128)(4,1)} %bitcast.111), calls=%async_computation.2 | async-start | bytes 2883584
  181.4 8.9 %copy-start.7 = (f32[6,8,256]{2,1,0:T(8,128)}, f32[6,8,256]{2,1,0:T(8,128)S(1)}, u32[]{:S(2)}) copy-start(f32[6,8,256]{2,1,0:T(8,128)S(1)} %get-tuple-element.41.refs_6_) | copy-start | bytes 147460
  181.8 32.1 %copy-start.16 = (f32[128,768]{1,0:T(8,128)}, f32[128,768]{1,0:T(8,128)S(1)}, u32[]{:S(2)}) copy-start(f32[128,768]{1,0:T(8,128)S(1)} %get-tuple-element.82) | copy-start | bytes 1179652
  190.7 7.8 %copy-start.11 = (f32[128,768]{1,0:T(8,128)}, f32[128,768]{1,0:T(8,128)S(1)}, u32[]{:S(2)}) copy-start(f32[128,768]{1,0:T(8,128)S(1)} %get-tuple-element.84) | copy-start | bytes 1179652
  190.7 7.7 %copy-start.43 = (f32[128]{0:T(128)}, f32[128]{0:T(128)S(1)}, u32[]{:S(2)}) copy-start(f32[128]{0:T(128)S(1)} %add_rsqrt_fusion) | copy-start | bytes 1540
  198.6 15.3 %copy-start.14 = (f32[128,768]{1,0:T(8,128)}, f32[128,768]{1,0:T(8,128)S(1)}, u32[]{:S(2)}) copy-start(f32[128,768]{1,0:T(8,128)S(1)} %subtract_add_fusion.1) | copy-start | bytes 1179652
  199.2 10.0 %copy-start.50 = (s32[2]{0:T(128)S(1)}, s32[2]{0:T(128)}, u32[]{:S(2)}) copy-start(s32[2]{0:T(128)} %copy-done.49) | copy-start | bytes 28
  199.2 10.0 %copy-start.46 = (s32[32]{0:T(128)S(1)}, s32[32]{0:T(128)}, u32[]{:S(2)}) copy-start(s32[32]{0:T(128)} %copy-done.45) | copy-start | bytes 388
  209.1 6.3 %copy-start.5 = (bf16[128,768]{1,0:T(8,128)(2,1)}, bf16[128,768]{1,0:T(8,128)(2,1)S(1)}, u32[]{:S(2)}) copy-start(bf16[128,768]{1,0:T(8,128)(2,1)S(1)} %get-tuple-element.40) | copy-start | bytes 589828
  215.4 23.7 %copy-start.13 = (f32[128,768]{1,0:T(8,128)}, f32[128,768]{1,0:T(8,128)S(1)}, u32[]{:S(2)}) copy-start(f32[128,768]{1,0:T(8,128)S(1)} %get-tuple-element.87.refs_13_) | copy-start | bytes 1179652
  217.4 13.9 %copy-start.12 = (f32[128,768]{1,0:T(8,128)S(1)}, f32[128,768]{1,0:T(8,128)}, u32[]{:S(2)}) copy-start(f32[128,768]{1,0:T(8,128)} %copy-done.11) | copy-start | bytes 1179652
  217.4 13.9 %copy-start.30 = (bf16[128,2048]{1,0:T(8,128)(2,1)S(1)}, bf16[128,2048]{1,0:T(8,128)(2,1)}, u32[]{:S(2)}) copy-start(bf16[128,2048]{1,0:T(8,128)(2,1)} %copy-done.29) | copy-start | bytes 1572868
  217.4 13.9 %copy-start.32 = (bf16[128,2048]{1,0:T(8,128)(2,1)S(1)}, bf16[128,2048]{1,0:T(8,128)(2,1)}, u32[]{:S(2)}) copy-start(bf16[128,2048]{1,0:T(8,128)(2,1)} %copy-done.31) | copy-start | bytes 1572868
  217.4 13.9 %copy-start.44 = (f32[128]{0:T(128)S(1)}, f32[128]{0:T(128)}, u32[]{:S(2)}) copy-start(f32[128]{0:T(128)} %copy-done.43) | copy-start | bytes 1540
  231.3 9.4 %copy-start.1 = (bf16[128,768]{1,0:T(8,128)(2,1)}, bf16[128,768]{1,0:T(8,128)(2,1)S(1)}, u32[]{:S(2)}) copy-start(bf16[128,768]{1,0:T(8,128)(2,1)S(1)} %get-tuple-element.43) | copy-start | bytes 589828
  231.3 6.2 %copy-start.6 = (bf16[128,768]{1,0:T(8,128)(2,1)S(1)}, bf16[128,768]{1,0:T(8,128)(2,1)}, u32[]{:S(2)}) copy-start(bf16[128,768]{1,0:T(8,128)(2,1)} %copy-done.5) | copy-start | bytes 589828
  231.3 6.2 %copy-start.17 = (f32[128,768]{1,0:T(8,128)S(1)}, f32[128,768]{1,0:T(8,128)}, u32[]{:S(2)}) copy-start(f32[128,768]{1,0:T(8,128)} %copy-done.16) | copy-start | bytes 1179652
  231.3 6.2 %copy-start.42 = (f32[768]{0:T(1024)S(1)}, f32[768]{0:T(1024)}, u32[]{:S(2)}) copy-start(f32[768]{0:T(1024)} %copy-done.41) | copy-start | bytes 9220
  231.3 6.2 %copy-start.54 = (f32[128]{0:T(128)S(1)}, f32[128]{0:T(128)}, u32[]{:S(2)}) copy-start(f32[128]{0:T(128)} %copy-done.53) | copy-start | bytes 1540
  246.6 4.8 %copy-start.2 = (bf16[128,768]{1,0:T(8,128)(2,1)S(1)}, bf16[128,768]{1,0:T(8,128)(2,1)}, u32[]{:S(2)}) copy-start(bf16[128,768]{1,0:T(8,128)(2,1)} %copy-done.1) | copy-start | bytes 589828
  246.6 7.4 %copy-start.48 = (bf16[768]{0:T(1024)(128)(2,1)S(1)}, bf16[768]{0:T(1024)(128)(2,1)}, u32[]{:S(2)}) copy-start(bf16[768]{0:T(1024)(128)(2,1)} %get-tuple-element.50) | copy-start | bytes 4612
  246.6 8.4 %copy-start.47 = (bf16[768]{0:T(1024)(128)(2,1)S(1)}, bf16[768]{0:T(1024)(128)(2,1)}, u32[]{:S(2)}) copy-start(bf16[768]{0:T(1024)(128)(2,1)} %get-tuple-element.48) | copy-start | bytes 4612
  (29 other events, 63.9 us)

commit v2 on v1

--- a/solution.py
+++ b/solution.py
@@ -34,77 +34,6 @@
     return ((y + shift) % 4) * 4 + 2 * high + core
 
 
-def greet(devices):
-    barrier = pltpu.get_barrier_semaphore()
-    for device in devices:
-        pl.semaphore_signal(barrier, inc=1, device_id={"ctx": device})
-    pl.semaphore_wait(barrier, len(devices))
-
-
-def remote(src, dst, send_sem, recv_sem, device):
-    return pltpu.make_async_remote_copy(
-        src_ref=src, dst_ref=dst, send_sem=send_sem, recv_sem=recv_sem, device_id={"ctx": device}
-    )
-
-
-def gather_kernel(x_ref, out_ref, send_sem, recv_sem, local_sem):
-    me, core, high, y = ctx_place()
-    sibling = slot_of(y, 0, high, 1 - core)
-    across = slot_of(y, 0, 1 - high, core)
-    rows = [slot_of(y, shift, high, core) for shift in (1, 2, 3)]
-    greet([sibling, across] + rows)
-    sends = []
-
-    def send(src, slot, device):
-        copy = remote(src, out_ref.at[slot], send_sem.at[len(sends)], recv_sem.at[slot], device)
-        copy.start()
-        sends.append(copy)
-
-    def arrived(slot):
-        remote(x_ref, out_ref.at[slot], send_sem.at[0], recv_sem.at[slot], sibling).wait_recv()
-
-    send(x_ref, me, across)
-    for device in rows:
-        send(x_ref, me, device)
-    send(x_ref, me, sibling)
-    own = pltpu.make_async_copy(x_ref, out_ref.at[me], local_sem)
-    own.start()
-    arrived(across)
-    for device in rows:
-        send(out_ref.at[across], across, device)
-    send(out_ref.at[across], across, sibling)
-    for shift in (1, 3, 2):
-        slot = slot_of(y, shift, high, core)
-        arrived(slot)
-        send(out_ref.at[slot], slot, sibling)
-    for shift in (1, 3, 2):
-        slot = slot_of(y, shift, 1 - high, core)
-        arrived(slot)
-        send(out_ref.at[slot], slot, sibling)
-    for shift in range(4):
-        for other in range(2):
-            arrived(slot_of(y, shift, other, 1 - core))
-    own.wait()
-    for copy in sends:
-        copy.wait_send()
-
-
-def ctx_gather(x, collective_id):
-    return pl.pallas_call(
-        gather_kernel,
-        out_shape=jax.ShapeDtypeStruct((N_CTX,) + x.shape, x.dtype),
-        in_specs=[pl.BlockSpec(memory_space=pl.ANY)],
-        out_specs=pl.BlockSpec(memory_space=pl.ANY),
-        scratch_shapes=[
-            pltpu.SemaphoreType.DMA((15,)),
-            pltpu.SemaphoreType.DMA((N_CTX,)),
-            pltpu.SemaphoreType.DMA,
-        ],
-        compiler_params=pltpu.CompilerParams(collective_id=collective_id, has_side_effects=True),
-        name="ctx_gather",
-    )(x)
-
-
 def torus_place():
     me, core, high, y = ctx_place()
     shard = lax.axis_index("fsdp")
@@ -128,105 +57,237 @@
     pl.semaphore_wait(barrier, len(devices))
 
 
-def weights_kernel(count, *refs):
-    sources = refs[:count]
-    targets = refs[count : 2 * count]
-    send_sem, x_sem, z_sem, core_sem, local_sem = refs[2 * count :]
+PACKS = ((0, 1), (2, 3), (4, 5, 6, 7), (8, 9), (10,))
+
+
+def front_kernel(*refs):
+    sources = refs[:11]
+    small_ref, token_ref, state_ref = refs[11:14]
+    targets = refs[14:19]
+    small_out, normed_out, query_out, self_out_ref, cross_out_ref = refs[19:24]
+    (
+        landing, weight_ref, self_ref, cross_ref, send_sem, x_sem, z_sem, core_sem, fill_sem,
+        small_sem, self_sem, cross_sem, local_sem,
+    ) = refs[24:]
     me, core, high, y, low, x = torus_place()
     shard = low * 4 + x
     sibling = (slot_of(y, 0, high, 1 - core), shard)
     inside = (me, (1 - low) * 4 + x)
     outside = (slot_of(y, 0, 1 - high, core), (1 - low) * 4 + x)
+    across = slot_of(y, 0, 1 - high, core)
+    rows = [slot_of(y, shift, high, core) for shift in (1, 2, 3)]
     others = [low * 4 + (x + shift) % 4 for shift in (1, 2, 3)]
-    greet_all([sibling, inside, outside] + [(me, other) for other in others])
-
-    def part(index, owner, whose, side=None):
-        ref = targets[index]
-        rows = ref.shape[1] // 2
-        start = pl.multiple_of(whose * rows, 16)
-        if side is None:
-            return ref.at[owner, pl.ds(start, rows), :]
-        width = ref.shape[2] // 2
-        return ref.at[owner, pl.ds(start, rows), pl.ds(side * width, width)]
-
-    def mine(index, side=None):
-        ref = sources[index]
-        rows = ref.shape[0] // 2
-        start = pl.multiple_of(core * rows, 16)
-        if side is None:
-            return ref.at[pl.ds(start, rows), :]
-        width = ref.shape[1] // 2
-        return ref.at[pl.ds(start, rows), pl.ds(side * width, width)]
-
+    peers = [(shard + shift) % 8 for shift in range(1, 8)]
+    greet_all(
+        [sibling, outside, (across, shard)]
+        + [(me, peer) for peer in peers]
+        + [(row, shard) for row in rows]
+    )
     sends = []
 
-    def send(index, src, dst, recv_sem, device):
+    def send(src, dst, recv_sem, device):
         copy = hop(src, dst, send_sem.at[len(sends)], recv_sem, *device)
         copy.start()
         sends.append(copy)
 
-    def arrived(index, ref, recv_sem):
+    def arrived(ref, recv_sem):
         hop(ref, ref, send_sem.at[0], recv_sem, *sibling).wait_recv()
 
-    for index in range(count):
+    def bring(src, dst, sem):
+        copy = pltpu.make_async_copy(src, dst, sem)
+        copy.start()
+        return copy
+
+
+    def part(k, owner, whose, side=None):
+        ref = targets[k]
+        count = ref.shape[1] // 2
+        start = pl.multiple_of(whose * count, 16)
+        if side is None:
+            return ref.at[owner, pl.ds(start, count), :]
+        width = ref.shape[2] // 2
+        return ref.at[owner, pl.ds(start, count), pl.ds(side * width, width)]
+
+    def fill(k):
+        copies = []
+        start = 0
+        for source in PACKS[k]:
+            width = sources[source].shape[1]
+            copies.append(
+                bring(
+                    sources[source],
+                    targets[k].at[shard, :, pl.ds(start, width)],
+                    fill_sem.at[source],
+                )
+            )
+            start += width
+        return copies
+
+    def send_own(k):
+        for copy in fills[k]:
+            copy.wait()
         for spot in (1, 0, 2):
-            send(index, mine(index), part(index, shard, core), x_sem.at[index, spot], (me, others[spot]))
+            block = part(k, shard, core)
+            send(block, block, x_sem.at[k, spot], (me, others[spot]))
         for side, device in enumerate((inside, outside)):
-            send(
-                index, mine(index, side), part(index, shard, core, side), z_sem.at[index, 3, side], device
-            )
-    own = []
-    for index in range(count):
-        copy = pltpu.make_async_copy(sources[index], targets[index].at[shard], local_sem.at[index])
-        copy.start()
-        own.append(copy)
-    for index in range(count):
+            piece = part(k, shard, core, side)
+            send(piece, piece, z_sem.at[k, 3, side], device)
+
+
+    def pass_x(k):
         for spot in (0, 2, 1):
             owner = low * 4 + (x + 3 - spot) % 4
-            block = part(index, owner, core)
-            arrived(index, block, x_sem.at[index, spot])
+            block = part(k, owner, core)
+            arrived(block, x_sem.at[k, spot])
             for side, device in enumerate((inside, outside)):
-                piece = part(index, owner, core, side)
-                send(index, piece, piece, z_sem.at[index, spot, side], device)
-            send(index, block, block, core_sem.at[index, spot], sibling)
+                piece = part(k, owner, core, side)
+                send(piece, piece, z_sem.at[k, spot, side], device)
+            send(block, block, core_sem.at[k, spot], sibling)
+
+    def pass_z(k):
         for spot in (3, 0, 2, 1):
             owner = (1 - low) * 4 + (x + 3 - spot) % 4
             for side in range(2):
-                piece = part(index, owner, core, side)
-                arrived(index, piece, z_sem.at[index, spot, side])
-                send(index, piece, piece, core_sem.at[index, 3 + 2 * spot + side], sibling)
-    for index in range(count):
+                piece = part(k, owner, core, side)
+                arrived(piece, z_sem.at[k, spot, side])
+                send(piece, piece, core_sem.at[k, 3 + 2 * spot + side], sibling)
+
+    def complete(k):
         for spot in range(3):
             owner = low * 4 + (x + 3 - spot) % 4
-            arrived(index, part(index, owner, 1 - core), core_sem.at[index, spot])
+            arrived(part(k, owner, 1 - core), core_sem.at[k, spot])
         for spot in range(4):
             owner = (1 - low) * 4 + (x + 3 - spot) % 4
             for side in range(2):
-                piece = part(index, owner, 1 - core, side)
-                arrived(index, piece, core_sem.at[index, 3 + 2 * spot + side])
-    for copy in own:
-        copy.wait()
+                arrived(part(k, owner, 1 - core, side), core_sem.at[k, 3 + 2 * spot + side])
+
+
+    def kv_start(src, out, sems):
+        send(src, out.at[me], sems.at[me], (across, shard))
+        for row in rows:
+            send(src, out.at[me], sems.at[me], (row, shard))
+        send(src, out.at[me], sems.at[me], sibling)
+
+    def kv_across(out, sems):
+        block = out.at[across]
+        arrived(block, sems.at[across])
+        for row in rows:
+            send(block, block, sems.at[across], (row, shard))
+        send(block, block, sems.at[across], sibling)
+
+    def kv_rows(out, sems, flip):
+        for shift in (1, 3, 2):
+            slot = slot_of(y, shift, 1 - high if flip else high, core)
+            block = out.at[slot]
+            arrived(block, sems.at[slot])
+            send(block, block, sems.at[slot], sibling)
+
+    def kv_complete(out, sems):
+        for shift in range(4):
+            for half in range(2):
+                slot = slot_of(y, shift, half, 1 - core)
+                arrived(out.at[slot], sems.at[slot])
+
+    fills = [fill(k) for k in range(5)]
+    own_small = bring(small_ref, landing.at[shard], local_sem.at[0])
+    for spot, peer in enumerate(peers):
+        send(small_ref, landing.at[shard], small_sem.at[spot], (me, peer))
+    send_own(0)
+    send_own(1)
+    own_small.wait()
+    for spot in range(7):
+        arrived(landing.at[(shard + 7 - spot) % 8], small_sem.at[spot])
+    small = landing[...]
+    small_out[...] = small
+    gains = small.astype(F32)
+    gain = jnp.concatenate([gains[owner, 0:1, :96] for owner in range(8)], axis=1)
+    normed = rms_scaled(token_ref[...].astype(F32), gain)
+    normed_out[...] = normed
+    pass_x(0)
+    send_own(2)
+    pass_z(0)
+    pass_x(1)
+    send_own(3)
+    complete(0)
+    bring(targets[0], weight_ref, local_sem.at[1]).wait()
+    for half in range(2):
+        weight = weight_ref[:, :, half * D : half * D + D].reshape(D, D)
+        self_ref[half] = matmul(normed, weight).astype(BF)
+    kv_start(self_ref, self_out_ref, self_sem)
+    own_self = bring(self_ref, self_out_ref.at[me], local_sem.at[2])
+    pass_z(1)
+    complete(1)
+    bring(targets[1], weight_ref, local_sem.at[1]).wait()
+    for half in range(2):
+        weight = weight_ref[:, :, half * D : half * D + D].reshape(D, D)
+        cross_ref[half] = matmul(state_ref[...], weight).astype(BF)
+    kv_start(cross_ref, cross_out_ref, cross_sem)
+    own_cross = bring(cross_ref, cross_out_ref.at[me], local_sem.at[3])
+    pass_x(2)
+    send_own(4)
+    kv_across(self_out_ref, self_sem)
+    pass_z(2)
+    kv_across(cross_out_ref, cross_sem)
+    pass_x(3)
+    kv_rows(self_out_ref, self_sem, False)
+    pass_z(3)
+    pass_x(4)
+    kv_rows(self_out_ref, self_sem, True)
+    kv_rows(cross_out_ref, cross_sem, False)
+    pass_z(4)
+    kv_rows(cross_out_ref, cross_sem, True)
+    complete(2)
+    bring(targets[2].at[:, :, pl.ds(0, D)], weight_ref.at[:, :, pl.ds(0, D)], local_sem.at[1]).wait()
+    query_out[...] = matmul(normed, weight_ref[:, :, :D].reshape(D, D)).astype(BF)
+    complete(3)
+    complete(4)
+    kv_complete(self_out_ref, self_sem)
+    kv_complete(cross_out_ref, cross_sem)
+    own_self.wait()
+    own_cross.wait()
     for copy in sends:
         copy.wait_send()
 
 
-def gather_weights(packs, collective_id):
-    count = len(packs)
+def front(weights, small, tokens, states, collective_id):
+    dma = pltpu.SemaphoreType.DMA
+    packs = [
+        (8, weights[group[0]].shape[0], sum(weights[k].shape[1] for k in group)) for group in PACKS
+    ]
+    anywhere = pl.BlockSpec(memory_space=pl.ANY)
+    inside = pl.BlockSpec(memory_space=pltpu.VMEM)
     return pl.pallas_call(
-        functools.partial(weights_kernel, count),
-        out_shape=[jax.ShapeDtypeStruct((8,) + pack.shape, pack.dtype) for pack in packs],
-        in_specs=[pl.BlockSpec(memory_space=pl.ANY)] * count,
-        out_specs=[pl.BlockSpec(memory_space=pl.ANY)] * count,
+        front_kernel,
+        out_shape=[jax.ShapeDtypeStruct(pack, BF) for pack in packs]
+        + [
+            jax.ShapeDtypeStruct((8, 16, 128), BF),
+            jax.ShapeDtypeStruct((TOK, D), BF),
+            jax.ShapeDtypeStruct((TOK, D), BF),
+            jax.ShapeDtypeStruct((N_CTX, 2, TOK, D), BF),
+            jax.ShapeDtypeStruct((N_CTX, 2, ENC, D), BF),
+        ],
+        in_specs=[anywhere] * 12 + [inside] * 2,
+        out_specs=[anywhere] * 5 + [inside] * 3 + [anywhere] * 2,
         scratch_shapes=[
-            pltpu.SemaphoreType.DMA((22 * count,)),
-            pltpu.SemaphoreType.DMA((count, 3)),
-            pltpu.SemaphoreType.DMA((count, 4, 2)),
-            pltpu.SemaphoreType.DMA((count, 11)),
-            pltpu.SemaphoreType.DMA((count,)),
-        ],
-        compiler_params=pltpu.CompilerParams(collective_id=collective_id, has_side_effects=True),
-        name="gather_weights",
-    )(*packs)
+            pltpu.VMEM((8, 16, 128), BF),
+            pltpu.VMEM((8, 96, 2 * D), BF),
+            pltpu.VMEM((2, TOK, D), BF),
+            pltpu.VMEM((2, ENC, D), BF),
+            dma((5 * 22 + 7 + 30,)),
+            dma((5, 3)),
+            dma((5, 4, 2)),
+            dma((5, 11)),
+            dma((11,)),
+            dma((7,)),
+            dma((N_CTX,)),
+            dma((N_CTX,)),
+            dma((4,)),
+        ],
+        compiler_params=pltpu.CompilerParams(
+            collective_id=collective_id, has_side_effects=True, vmem_limit_bytes=32 * MIB
+        ),
+        name="front",
+    )(*weights, small, tokens, states)
 
 
 PIECE = 48
@@ -899,37 +960,33 @@
 ):
     me = lax.axis_index("ctx")
     rows = self_query.shape[0]
-    extra = jnp.concatenate(
+    small = jnp.concatenate(
         [
-            gain_self[:, None],
-            gain_cross[:, None],
-            gain_feed[:, None],
-            jnp.zeros((rows, 5), BF),
-            jnp.pad(position_bias, ((0, rows - position_bias.shape[0]), (0, 0))),
-            jnp.zeros((rows, 236), BF),
-        ],
-        axis=1,
-    )
-    early, late, down = gather_weights(
+            jnp.pad(jnp.stack([gain_self, gain_cross, gain_feed]), ((0, 0), (0, 128 - rows))),
+            jnp.pad(position_bias, ((0, 9), (0, 128 - HEADS))),
+        ],
+        axis=0,
+    )
+    kv_one, kv_two, square, gate_up, down, small, normed_one, queries, self_kv, cross_kv = front(
         [
-            jnp.concatenate([self_query, self_key, self_value, cross_key, cross_value, extra], axis=1),
-            jnp.concatenate([self_out, cross_query, cross_out, feed_gate, feed_up], axis=1),
-            feed_down,
-        ],
-        5,
-    )
-    early = early.reshape(D, -1)
-    late = late.reshape(D, -1)
+            self_key, self_value, cross_key, cross_value,
+            self_query, self_out, cross_query, cross_out,
+            feed_gate, feed_up, feed_down,
+        ],
+        small,
+        decoder_in[0],
+        encoder_states[0],
+        0,
+    )
+    kv_one = kv_one.reshape(D, 2 * D)
+    kv_two = kv_two.reshape(D, 2 * D)
+    square = square.reshape(D, 4 * D)
+    gate_up = gate_up.reshape(D, 2 * FF)
     down = down.reshape(FF, D)
-    qkv_one = early[:, : 3 * D]
-    kv_two = early[:, 3 * D : 5 * D]
-    gains = early[:, 5 * D : 5 * D + 3].astype(F32).T
+    query_one, out_one, query_two, out_two = (square[:, k * D : k * D + D] for k in range(4))
+    gains = jnp.transpose(small[:, :3, :rows], (1, 0, 2)).reshape(3, D).astype(F32)
     norm_one, norm_two, norm_three = gains[0:1], gains[1:2], gains[2:3]
-    table = early.reshape(8, rows, -1)[:, :4, 5 * D + 8 : 5 * D + 20].reshape(32, HEADS)
-    out_one = late[:, :D]
-    query_two = late[:, D : 2 * D]
-    out_two = late[:, 2 * D : 3 * D]
-    gate_up = late[:, 3 * D :]
+    table = small[:, 3:7, :HEADS].reshape(32, HEADS)
 
     bucket_hot = (bucket_table[:, None] == jnp.arange(32, dtype=jnp.int32)[None, :]).astype(BF)
     bias_rows = transposed_right(table.T, bucket_hot)
@@ -952,22 +1009,11 @@
     tokens = decoder_in[0].astype(F32)
     states = encoder_states[0]
     upstream = out_grad[0]
-    normed_one = rms_scaled(tokens, norm_one)
-    qkv = matmul(normed_one, qkv_one).astype(BF)
-    cross_kv = matmul(states, kv_two).astype(BF)
-    queries = qkv[:, :D]
-    local = jnp.stack(
-        [
-            jnp.concatenate([qkv[:, D : 2 * D], cross_kv[:, :D]], axis=0),
-            jnp.concatenate([qkv[:, 2 * D :], cross_kv[:, D:]], axis=0),
-        ]
-    )
-    gathered = ctx_gather(local, 0)
-    attended, self_totals = attend(queries, gathered, TOK, 0, classes, tiles)
+    attended, self_totals = attend(queries, self_kv, TOK, 0, classes, tiles)
     mid_one = tokens + matmul(attended, out_one)
     normed_two = rms_scaled(mid_one, norm_two)
     cross_queries = matmul(normed_two, query_two).astype(BF)
-    cross_attended, cross_totals = attend(cross_queries, gathered, ENC, 2)
+    cross_attended, cross_totals = attend(cross_queries, cross_kv, ENC, 0)
     mid_two = mid_one + matmul(cross_attended, out_two)
     normed_three = rms_scaled(mid_two, norm_three)
     gate_up_values = matmul(normed_three, gate_up).astype(BF).astype(F32)
@@ -986,7 +1032,7 @@
     cross_branch = d_mid_two.astype(BF)
     d_cross_attended = transposed_right(cross_branch, out_two).astype(BF)
     d_cross_queries, d_cross_kv_all = attend_back(
-        cross_queries, gathered, d_cross_attended, cross_totals, ENC, 2
+        cross_queries, cross_kv, d_cross_attended, cross_totals, ENC, 0
     )
     grad_out_two = transposed_left(cross_attended, cross_branch).astype(BF)
     grad_query_two = transposed_left(normed_two, d_cross_queries).astype(BF)
@@ -996,7 +1042,7 @@
     self_branch = d_mid_one.astype(BF)
     d_attended = transposed_right(self_branch, out_one).astype(BF)
     d_queries, d_kv_all, strips = attend_back(
-        queries, gathered, d_attended, self_totals, TOK, 0, classes, near, tiles
+        queries, self_kv, d_attended, self_totals, TOK, 0, classes, near, tiles
     )
     grad_table = matmul(bias_sums(strips), bucket_hot.astype(F32)).T.reshape(8, 4, HEADS)
     grad_extra = jnp.concatenate(
@@ -1026,9 +1072,9 @@
         [
             normed_one.T.reshape(8, rows, TOK),
             states.T.reshape(8, rows, ENC),
-            qkv_one[:, D:],
+            kv_one,
             kv_two,
-            transposed_right(d_queries, qkv_one[:, :D]),
+            transposed_right(d_queries, query_one),
             d_mid_one,
             decoder_in[0],
             norm_one,

time: 423 us -> 371 us (0.88)
  Pallas kernels: 330 us -> 271 us
  local copies, waits for them, and re-layouts: 37.1 us -> 44 us
    pallas_call x2 -> x1, Pallas kernels: 145 us -> 86 us  [front(): pl.pallas_call(front_kernel, out_shape=[jax.ShapeDtypeStruct(pack, BF) fo...]
    unnamed x130 -> x131, local copies, waits for them, and re-layouts: 10.2 us -> 28.4 us
    slice x4 -> x1, local copies, waits for them, and re-layouts: 5.67 us -> 0.01 us  [body(): table = small[:, 3:7, :HEADS].reshape(32, HEADS)]
    dot_general x9 -> x7, matrix products: 9.57 us -> 11.5 us  [matmul(): return jnp.dot(left, right, preferred_element_type=F32)]
where the time goes in v2:
time: 371 us; the launch traced here: 370 us
  Pallas kernels  271 us (73%)
  local copies, waits for them, and re-layouts  44 us (12%)
  matrix products  40.3 us (11%)
  other arithmetic  12.3 us (3%)
    pallas_call x1, Pallas kernels, finish(): pl.pallas_call(finish_kernel, out_shape=[jax.ShapeDtypeStruct((8, 2 * PIE...  147 us
    pallas_call x1, Pallas kernels, front(): pl.pallas_call(front_kernel, out_shape=[jax.ShapeDtypeStruct(pack, BF) fo...  86 us
    dot_general x15, matrix products, contract(): lax.dot_general(left, right, (dims, ((), ())), preferred_element_type=F32)  28.8 us
    unnamed x131, local copies, waits for them, and re-layouts  28.4 us
    pallas_call x2, Pallas kernels, attend_back(): pl.pallas_call(functools.partial(backward_kernel, biased), grid=(PAIRS,),...  22 us
    pallas_call x2, Pallas kernels, attend(): pl.pallas_call(functools.partial(forward_kernel, biased), grid=(PAIRS,),...  15.9 us
    dot_general x7, matrix products, matmul(): return jnp.dot(left, right, preferred_element_type=F32)  11.5 us

profile of v2, /device:TPU:1, one launch (start us, length us, event | category | flops | bytes accessed | tf_op | source)
XLA Modules:
  0.0 369.9 jit_solution(6565876512259185334)
XLA Ops:
  18.3 86.0 %front.1 = (bf16[8,96,1536]{2,1,0:T(8,128)(2,1)S(1)}, bf16[8,96,1536]{2,1,0:T(8,128)(2,1)S(1)}, bf16[8,96,3072]{2,1,0:T(8,128)(2,1)S(1)}, bf16[8,96,4096]{2,1,0:...) custom-call(bf16[96,768]{1,0:T(8,128)(2,1)S(1)} %copy-done.23, ...), custom_call_target="tpu_custom_call" | custom-call | tf_op jit(solution)/shard_map/front/pallas_call | solution.py:259
  104.4 1.6 copy-done
  106.0 2.1 copy-done.2
  108.1 1.7 copy-done.4
  109.7 1.5 copy-done.6
  118.6 9.9 %attend_self.1 = (bf16[128,768]{1,0:T(8,128)(2,1)S(1)}, f32[6,8,256]{2,1,0:T(8,128)S(1)}) custom-call(s32[2,32]{1,0:T(2,128)S(1)} %compare_select_fusion.1.refs_0_, bf16[128,768]{1,0:T(8,128)(2,1)S(1)} %get-tuple-element.40.refs_1_.refs_2_, bf16[16,2,128,768]{3,2,1,0:T(8,128)(2,1)} %get-tuple-element.41.refs_2_.refs_3_.refs_4_, ...), custom_call_target="tpu_custom_call" | custom-call | flops 1000000000 | bytes 10000000 | tf_op jit(solution)/shard_map/attend_self/pallas_call | solution.py:823
  128.6 1.8 multiply_reduce_fusion.5
  131.1 1.6 convolution_convert_fusion.9.refs_0_
  132.8 1.9 copy-done.1
  134.7 6.1 %attend_cross.1 = (bf16[128,768]{1,0:T(8,128)(2,1)S(1)}, f32[6,8,256]{2,1,0:T(8,128)S(1)}) custom-call(bf16[128,768]{1,0:T(8,128)(2,1)S(1)} %convolution_convert_fusion.9.refs_0_, bf16[16,2,64,768]{3,2,1,0:T(8,128)(2,1)S(1)} %copy-done.1, bf16[16,2,64,768]{3,2,1,0:T(8,128)(2,1)S(1)} %copy-done.1), custom_call_target="tpu_custom_call" | custom-call | flops 1000000000 | bytes 10000000 | tf_op jit(solution)/shard_map/attend_cross/pallas_call | solution.py:823
  140.7 1.7 multiply_reduce_fusion.4
  142.6 4.0 %fusion.4 = f32[128,4096]{1,0:T(8,128)S(1)} fusion(bf16[768,4096]{1,0:T(8,128)(2,1)} %bitcast.115, f32[128,768]{1,0:T(8,128)S(1)} %get-tuple-element.90, f32[768]{0:T(1024)S(1)} %mul.223, f32[128]{0:T(128)S(1)} %add_rsqrt_fusion), kind=kOutput, calls=%fused_computation.11 | convolution fusion | flops 806649856 | bytes 8785408 | tf_op jit(solution)/shard_map/dot_general | solution.py:879
  146.6 1.6 fusion.14
  149.6 2.8 multiply_reduce_fusion
  152.6 2.0 convolution_convert_fusion.8.refs_3_
  154.5 8.2 %attend_cross_back.1 = (bf16[128,768]{1,0:T(8,128)(2,1)S(1)}, bf16[16,2,64,768]{3,2,1,0:T(8,128)(2,1)S(1)}) custom-call(bf16[128,768]{1,0:T(8,128)(2,1)S(1)} %convolution_convert_fusion.9.refs_0_, bf16[16,2,64,768]{3,2,1,0:T(8,128)(2,1)} %copy-done, bf16[16,2,64,768]{3,2,1,0:T(8,128)(2,1)} %copy-done, ...), custom_call_target="tpu_custom_call" | custom-call | flops 3000000000 | bytes 10000000 | tf_op jit(solution)/shard_map/attend_cross_back/pallas_call | solution.py:860
  162.8 1.6 copy-done.3
  164.7 2.6 multiply_reduce_fusion.1
  168.5 2.0 convolution_convert_fusion.7.refs_5_
  170.6 13.8 %attend_self_back.1 = (bf16[128,768]{1,0:T(8,128)(2,1)S(1)}, bf16[16,2,128,768]{3,2,1,0:T(8,128)(2,1)}, f32[12,3,64,128]{3,2,1,0:T(8,128)S(1)}) custom-call(s32[2,32]{1,0:T(2,128)S(1)} %compare_select_fusion.1.refs_0_, s32[2,3]{1,0:T(2,128)S(1)} %copy.57.refs_1_, bf16[128,768]{1,0:T(8,128)(2,1)S(1)} %copy-done.13, ...), custom_call_target="tpu_custom_call" | custom-call | flops 3000000000 | bytes 10000000 | tf_op jit(solution)/shard_map/attend_self_back/pallas_call | solution.py:860
  184.4 4.5 %convolution_convert_fusion = bf16[768,4096]{1,0:T(8,128)(2,1)} fusion(bf16[128,2048]{1,0:T(8,128)(2,1)S(1)} %copy-done.50, bf16[128,2048]{1,0:T(8,128)(2,1)S(1)} %copy-done.48, f32[128,768]{1,0:T(8,128)S(1)} %copy-done.36, f32[768]{0:T(1024)S(1)} %mul.223, f32[128]{0:T(128)S(1)} %copy-done.55), kind=kOutput, calls=%fused_computation.5 | convolution fusion | flops 810844160 | bytes 7736832 | tf_op jit(solution)/shard_map/dot_general | solution.py:687
  189.0 1.5 convolution_convert_fusion.6
  190.5 1.6 convolution_convert_fusion.5
  192.1 1.5 convolution_convert_fusion.4
  193.6 1.5 convolution_convert_fusion.3
  195.2 2.7 convolution_convert_fusion.2
  199.5 2.6 fusion.6.refs_12_
  204.1 1.4 slice_add_fusion
  205.5 1.7 reshape.249
  211.1 147.2 %finish_gradients.1 = (bf16[8,96,1664]{2,1,0:T(8,128)(2,1)}, f32[128,768]{1,0:T(8,128)}, f32[64,768]{1,0:T(8,128)}) custom-call(bf16[8,2,2,64,768]{4,3,2,1,0:T(8,128)(2,1)} %bitcast.104, bf16[8,2,2,128,768]{4,3,2,1,0:T(8,128)(2,1)} %bitcast.121, bf16[8,96,4096]{2,1,0:T(8,128)(2,1)} %bitcast.114, bf16[8,96,768]{2,1,0:T(8,128)(2,1)} %bitcast.122, ...), custom_call_target="tpu_custom_call" | custom-call | tf_op jit(solution)/shard_map/finish_gradients/pallas_call | solution.py:616
  359.8 1.5 slice_convert_fusion
  361.3 1.4 slice_bitcast_fusion
  (192 shorter events, 44.5 us)
Async XLA Ops:
  0.7 112.7 %copy-start.60 = (s32[128]{0:T(128)S(1)}, s32[128]{0:T(128)}, u32[]{:S(2)}) copy-start(s32[128]{0:T(128)} %param.24) | copy-start | bytes 1540
  113.3 5.3 %copy-start.12 = (bf16[128,768]{1,0:T(8,128)(2,1)}, bf16[128,768]{1,0:T(8,128)(2,1)S(1)}, u32[]{:S(2)}) copy-start(bf16[128,768]{1,0:T(8,128)(2,1)S(1)} %get-tuple-element.40.refs_1_.refs_2_) | copy-start | bytes 589828
  118.6 9.9 %copy-start.9 = (bf16[1,128,768]{2,1,0:T(8,128)(2,1)S(1)}, bf16[1,128,768]{2,1,0:T(8,128)(2,1)}, u32[]{:S(2)}) copy-start(bf16[1,128,768]{2,1,0:T(8,128)(2,1)} %param.20) | copy-start | bytes 589828
  130.3 10.4 %copy-start.40 = (f32[128,768]{1,0:T(8,128)}, f32[128,768]{1,0:T(8,128)S(1)}, u32[]{:S(2)}) copy-start(f32[128,768]{1,0:T(8,128)S(1)} %get-tuple-element.88) | copy-start | bytes 1179652
  131.1 36.2 %copy-start.58 = (f32[128]{0:T(128)}, f32[128]{0:T(128)S(1)}, u32[]{:S(2)}) copy-start(f32[128]{0:T(128)S(1)} %add_rsqrt_fusion.1) | copy-start | bytes 1540
  142.4 10.0 %copy-start.35 = (f32[128,768]{1,0:T(8,128)}, f32[128,768]{1,0:T(8,128)S(1)}, u32[]{:S(2)}) copy-start(f32[128,768]{1,0:T(8,128)S(1)} %get-tuple-element.90) | copy-start | bytes 1179652
  142.5 9.9 %copy-start.54 = (f32[128]{0:T(128)}, f32[128]{0:T(128)S(1)}, u32[]{:S(2)}) copy-start(f32[128]{0:T(128)S(1)} %add_rsqrt_fusion) | copy-start | bytes 1540
  142.5 4.0 %copy-start.5 = (bf16[8,256,768]{2,1,0:T(8,128)(2,1)S(1)}, bf16[8,256,768]{2,1,0:T(8,128)(2,1)}, u32[]{:S(2)}) copy-start(bf16[8,256,768]{2,1,0:T(8,128)(2,1)} %copy-done.4) | copy-start | bytes 9437188
  142.5 4.0 %copy-start.45 = (bf16[1,128,768]{2,1,0:T(8,128)(2,1)S(1)}, bf16[1,128,768]{2,1,0:T(8,128)(2,1)}, u32[]{:S(2)}) copy-start(bf16[1,128,768]{2,1,0:T(8,128)(2,1)} %param.22) | copy-start | bytes 589828
  142.6 7.0 %slice-start = ((s8[6291456]{0:T(1024)(128)(4,1)}), s8[4194304]{0:T(1024)(128)(4,1)S(1)}, s32[]{:S(2)}) async-start(s8[6291456]{0:T(1024)(128)(4,1)} %bitcast.116), calls=%async_computation | async-start | bytes 8388608
  152.6 14.8 %copy-start.38 = (f32[128,768]{1,0:T(8,128)}, f32[128,768]{1,0:T(8,128)S(1)}, u32[]{:S(2)}) copy-start(f32[128,768]{1,0:T(8,128)S(1)} %subtract_add_fusion.1) | copy-start | bytes 1179652
  164.4 6.1 %copy-start.21 = (bf16[128,768]{1,0:T(8,128)(2,1)}, bf16[128,768]{1,0:T(8,128)(2,1)S(1)}, u32[]{:S(2)}) copy-start(bf16[128,768]{1,0:T(8,128)(2,1)S(1)} %get-tuple-element.51) | copy-start | bytes 589828
  167.3 3.2 copy-start.13
  167.3 3.2 copy-start.32
  168.5 23.6 %copy-start.37 = (f32[128,768]{1,0:T(8,128)}, f32[128,768]{1,0:T(8,128)S(1)}, u32[]{:S(2)}) copy-start(f32[128,768]{1,0:T(8,128)S(1)} %subtract_add_fusion.refs_13_) | copy-start | bytes 1179652
  170.5 13.8 %copy-start.36 = (f32[128,768]{1,0:T(8,128)S(1)}, f32[128,768]{1,0:T(8,128)}, u32[]{:S(2)}) copy-start(f32[128,768]{1,0:T(8,128)} %copy-done.35) | copy-start | bytes 1179652
  170.5 13.8 %copy-start.48 = (bf16[128,2048]{1,0:T(8,128)(2,1)S(1)}, bf16[128,2048]{1,0:T(8,128)(2,1)}, u32[]{:S(2)}) copy-start(bf16[128,2048]{1,0:T(8,128)(2,1)} %copy-done.47) | copy-start | bytes 1572868
  170.5 13.8 %copy-start.50 = (bf16[128,2048]{1,0:T(8,128)(2,1)S(1)}, bf16[128,2048]{1,0:T(8,128)(2,1)}, u32[]{:S(2)}) copy-start(bf16[128,2048]{1,0:T(8,128)(2,1)} %copy-done.49) | copy-start | bytes 1572868
  170.5 13.8 %copy-start.55 = (f32[128]{0:T(128)S(1)}, f32[128]{0:T(128)}, u32[]{:S(2)}) copy-start(f32[128]{0:T(128)} %copy-done.54) | copy-start | bytes 1540
  184.4 4.6 %copy-start.39 = (f32[128,768]{1,0:T(8,128)S(1)}, f32[128,768]{1,0:T(8,128)}, u32[]{:S(2)}) copy-start(f32[128,768]{1,0:T(8,128)} %copy-done.38) | copy-start | bytes 1179652
  184.4 6.1 %copy-start.22 = (bf16[128,768]{1,0:T(8,128)(2,1)S(1)}, bf16[128,768]{1,0:T(8,128)(2,1)}, u32[]{:S(2)}) copy-start(bf16[128,768]{1,0:T(8,128)(2,1)} %copy-done.21) | copy-start | bytes 589828
  184.4 6.1 %copy-start.41 = (f32[128,768]{1,0:T(8,128)S(1)}, f32[128,768]{1,0:T(8,128)}, u32[]{:S(2)}) copy-start(f32[128,768]{1,0:T(8,128)} %copy-done.40) | copy-start | bytes 1179652
  184.4 6.1 %copy-start.59 = (f32[128]{0:T(128)S(1)}, f32[128]{0:T(128)}, u32[]{:S(2)}) copy-start(f32[128]{0:T(128)} %copy-done.58) | copy-start | bytes 1540
  188.9 3.1 copy-start.20
  190.4 3.2 copy-start.11
  192.1 3.1 copy-start.43
  192.1 3.1 copy-start.46
  195.2 3.5 copy-start.18
  197.8 4.2 %copy-start.53 = (f32[8,96]{1,0:T(8,128)S(1)}, f32[8,96]{1,0:T(8,128)}, u32[]{:S(2)}) copy-start(f32[8,96]{1,0:T(8,128)} %get-tuple-element.69) | copy-start | bytes 9220
  197.8 4.9 %copy-start.57 = (bf16[768]{0:T(1024)(128)(2,1)S(1)}, bf16[768]{0:T(1024)(128)(2,1)}, u32[]{:S(2)}) copy-start(bf16[768]{0:T(1024)(128)(2,1)} %get-tuple-element.64) | copy-start | bytes 4612
  197.8 5.2 %copy-start.56 = (bf16[768]{0:T(1024)(128)(2,1)S(1)}, bf16[768]{0:T(1024)(128)(2,1)}, u32[]{:S(2)}) copy-start(bf16[768]{0:T(1024)(128)(2,1)} %get-tuple-element.62) | copy-start | bytes 4612
  204.1 3.1 copy-start.34
  (32 other events, 44.8 us)

commit v3 on v2

--- a/solution.py
+++ b/solution.py
@@ -284,31 +284,41 @@
             dma((4,)),
         ],
         compiler_params=pltpu.CompilerParams(
-            collective_id=collective_id, has_side_effects=True, vmem_limit_bytes=32 * MIB
+            collective_id=collective_id, has_side_effects=True, vmem_limit_bytes=60 * MIB
         ),
         name="front",
     )(*weights, small, tokens, states)
 
 
-PIECE = 48
-ROOM = D + FF // 4 + FF // 8 + 128
-EARLY = (2 * FF, D, D, D, D)
-WIDTHS = EARLY + (2 * D, 2 * D, 256)
+PIECE = 96
+ROOM = D // 2 + FF // 8 + FF // 16
+WIDTHS = (FF, D // 2, D // 2, D // 2, D // 2, D, D)
 SPAN = sum(WIDTHS)
 DOWN = len(WIDTHS)
+CHUNKS = DOWN + 1
+CROSS_KV, SELF_KV = 5, 6
+LEFT = (D, FF, D, D, D, D)
+RIGHT = (FF, D // 2, D // 2, D // 2, D // 2, D // 2)
 
 
 def finish_kernel(*refs):
+    lefts = refs[:6]
+    rights = refs[6:12]
+    dkv_ref, dckv_ref = refs[12:14]
+    state_ref, kv_ref, ckv_ref, dn_ref, dmid_ref, token_ref, gain_ref, small_ref = refs[14:22]
+    decoder_ref, encoder_ref = refs[22:24]
+    square_refs = refs[24:32]
+    gate_ref, up_ref, down_ref, small_out = refs[32:36]
     (
-        dckv_ref, dkv_ref, wide_ref, two_out_ref, two_query_ref, one_out_ref, one_query_ref, down_ref,
-        normed_ref, states_ref, kv_ref, ckv_ref, dn_ref, dmid_ref, token_ref, gain_ref, extra_ref,
-        out_ref, decoder_ref, encoder_ref,
-        kept, from_core, from_z, from_x, d_kept, d_core, d_z, d_x,
-        s_kept, s_core, s_row, s_stage, s_high, c_kept, c_core, c_row, c_stage, c_high,
-        to_core, gain_cols, packed, from_ctx, total_ref,
-        s_sem, c_sem, local_sem, core_send, core_recv, z_send, z_recv, x_send, x_recv,
-        ctx_send, ctx_recv, out_send, out_recv, pass_send, pass_recv, own_sem,
-    ) = refs
+        left_all, right_all, turned, turned_one, turned_state, state_all, s_right, c_right,
+        kept, from_z, from_x, d_kept, d_z, d_x,
+        s_kept, s_core, s_row, s_via, s_stage, s_high, s_fin,
+        c_kept, c_core, c_row, c_via, c_stage, c_high, c_fin,
+        small_f32, sm_own, sm_core, sm_z, sm_x, sm_ctx, sm_total, packed, from_ctx, land,
+        s_sem, c_sem, fill_sem, act_send, act_recv, late_send, late_recv, z_send, z_recv,
+        x_send, x_recv, ctx_send, ctx_recv, out_send, out_recv, pass_send, pass_recv,
+        sm_send, sm_recv, local_sem,
+    ) = refs[36:]
     me, core, high, y, low, x = torus_place()
     shard = low * 4 + x
     rank = y * 2 + high
@@ -317,6 +327,8 @@
     outside = (slot_of(y, 0, 1 - high, core), (1 - low) * 4 + x)
     across = (slot_of(y, 0, 1 - high, core), shard)
     others = [low * 4 + (x + shift) % 4 for shift in (1, 2, 3)]
+    ahead = (slot_of(y, 1, high, core), shard)
+    behind = (slot_of(y, 3, high, core), shard)
     shifts = [(dy, dz) for dy in range(4) for dz in range(2)][1:]
     mates = [((y + dy) % 4) * 2 + (high + dz) % 2 for dy, dz in shifts]
     greet_all(
@@ -324,10 +336,6 @@
         + [(me, other) for other in others]
         + [(mate * 2 + core, shard) for mate in mates]
     )
-    mine = pl.ds(pl.multiple_of(core * PIECE, 16), PIECE)
-    theirs = pl.ds(pl.multiple_of((1 - core) * PIECE, 16), PIECE)
-    mine_down = pl.ds(pl.multiple_of(core * 128, 16), 128)
-    theirs_down = pl.ds(pl.multiple_of((1 - core) * 128, 16), 128)
     sends = []
 
     def go(src, dst, send_sem, recv_sem, device):
@@ -342,7 +350,7 @@
         return copy
 
 
-    def rows_start(source, held, arrived, sem, base):
+    def rows_start(source, held, arrived, sem):
         over = []
         local = []
         for spot, shift in enumerate((2, 1, 3, 0)):
@@ -354,105 +362,133 @@
                     sem.at[0, spot], sem.at[1, spot], sibling,
                 )
             )
-            local.append(bring(source.at[pair, core], held.at[block], local_sem.at[base + spot]))
+            local.append(bring(source.at[pair, core], held.at[block], sem.at[4, spot]))
         return over, local
 
-    def rows_send(copies, held, arrived, row, sem):
+
+    def rows_send(copies, held, arrived, via, row, sem):
         over, local = copies
         onward = []
-        for spot, shift in enumerate((2, 1, 3, 0)):
+        for spot in range(4):
             local[spot].wait()
             over[spot].wait_recv()
             for block in (2 * spot, 2 * spot + 1):
                 for part in range(2):
                     held[block, part] = held[block, part] + arrived[block, part]
-            if shift:
-                onward.append(
-                    go(
-                        held.at[pl.ds(2 * spot, 2)], row.at[spot],
-                        sem.at[2, spot], sem.at[3, spot], (others_ctx[shift - 1], shard),
-                    )
-                )
+            if spot == 0:
+                first = go(held.at[0], via.at[0], sem.at[2, 0], sem.at[3, 0], ahead)
+                second = go(held.at[1], via.at[1], sem.at[2, 1], sem.at[3, 1], behind)
+            elif spot == 1:
+                onward.append(go(held.at[3], row.at[0, 1], sem.at[2, 2], sem.at[3, 2], ahead))
+            elif spot == 2:
+                onward.append(go(held.at[4], row.at[1, 0], sem.at[2, 3], sem.at[3, 3], behind))
+        return first, second, onward
+
+    def rows_via(state, held, via, row, sem):
+        first, second, onward = state
+        first.wait_recv()
+        for part in range(2):
+            held[2, part] = held[2, part] + via[0, part]
+        onward.append(go(held.at[2], row.at[0, 0], sem.at[2, 4], sem.at[3, 4], ahead))
+        second.wait_recv()
+        for part in range(2):
+            held[5, part] = held[5, part] + via[1, part]
+        onward.append(go(held.at[5], row.at[1, 1], sem.at[2, 5], sem.at[3, 5], behind))
         return onward
 
-    others_ctx = [slot_of(y, shift, high, core) for shift in (1, 2, 3)]
-
     def rows_total(held, row, half, part):
-        result = held[6 + half, part].astype(F32)
-        for spot in range(3):
-            result = result + row[spot, half, part].astype(F32)
-        return result
+        return (
+            held[6 + half, part].astype(F32)
+            + row[0, half, part].astype(F32)
+            + row[1, half, part].astype(F32)
+        )
 
     def rows_across(onward, held, row, stage, landing, sem):
         for copy in onward:
             copy.wait_recv()
         for part in range(2):
             stage[part] = rows_total(held, row, 1 - high, part).astype(BF)
-        return go(stage, landing, sem.at[2, 3], sem.at[3, 3], across)
-
-    def rows_sum(last, held, row, landing):
+        return go(stage, landing, sem.at[2, 6], sem.at[3, 6], across)
+
+    def rows_sum(last, held, row, landing, final, right, which):
         totals = [rows_total(held, row, high, part) for part in range(2)]
         last.wait_recv()
-        return jnp.concatenate(
-            [(totals[part] + landing[part].astype(F32)).astype(BF) for part in range(2)], axis=1
+        for part in range(2):
+            final[part] = (totals[part] + landing[part].astype(F32)).astype(BF)
+        count = final.shape[1]
+        copy = go(
+            final.at[1 - core], right.at[pl.ds(count, count)],
+            late_send.at[which], late_recv.at[which], sibling,
         )
+        right[:count] = final[core]
+        return copy
 
 
     starts = [sum(WIDTHS[:k]) for k in range(len(WIDTHS))]
+    left_starts = [sum(LEFT[:k]) for k in range(6)]
+    right_starts = [sum(RIGHT[:k]) for k in range(6)]
+    acts = {}
+    over_z, over_x = {}, {}
 
     def buffers(k):
         if k == DOWN:
-            return d_kept, d_core, d_z, d_x, 0, D
-        return kept, from_core, from_z, from_x, starts[k], WIDTHS[k]
-
-    over_core, over_z, over_x, brought = {}, {}, {}, {}
-
-    def chunk_start(k, source):
-        held, arrived, _, _, start, width = buffers(k)
-        cut = pl.ds(start, width)
-        rows, far_rows = (mine_down, theirs_down) if k == DOWN else (mine, theirs)
-        over_core[k] = go(
-            source.at[:, far_rows, :], arrived.at[:, :, cut], core_send.at[k], core_recv.at[k], sibling
+            return d_kept, d_z, d_x, pl.ds(0, D // 2)
+        return kept, from_z, from_x, pl.ds(starts[k], WIDTHS[k])
+
+    def acts_start(index):
+        left = pl.ds(left_starts[index], LEFT[index])
+        right = pl.ds(right_starts[index], RIGHT[index])
+        near = pl.ds(pl.multiple_of(core * RIGHT[index], 128), RIGHT[index])
+        far = pl.ds(pl.multiple_of((1 - core) * RIGHT[index], 128), RIGHT[index])
+        mine = pl.ds(0, TOK)
+        theirs = pl.ds(TOK, TOK)
+        acts[index] = (
+            bring(lefts[index], left_all.at[mine, left], fill_sem.at[index, 0]),
+            bring(rights[index].at[:, near], right_all.at[mine, right], fill_sem.at[index, 1]),
+            go(
+                lefts[index], left_all.at[theirs, left],
+                act_send.at[index, 0], act_recv.at[index, 0], sibling,
+            ),
+            go(
+                rights[index].at[:, far], right_all.at[theirs, right],
+                act_send.at[index, 1], act_recv.at[index, 1], sibling,
+            ),
         )
-        brought[k] = bring(source.at[:, rows, :], held.at[:, :, cut], local_sem.at[8 + k])
-
-    def chunk_send(k, offset):
-        width = WIDTHS[k]
-        over_core[k] = go(
-            to_core.at[:, :, pl.ds(offset, width)],
-            from_core.at[:, :, pl.ds(starts[k], width)],
-            core_send.at[k],
-            core_recv.at[k],
-            sibling,
-        )
-
-    def step_core(k):
-        held, arrived, landing, _, start, width = buffers(k)
-        cut = pl.ds(start, width)
-        if k in brought:
-            brought[k].wait()
-        over_core[k].wait_recv()
-        for column in range(4):
-            owner = 4 * (1 - low) + column
-            held[owner, :, cut] = held[owner, :, cut] + arrived[owner, :, cut]
-        half = width // 2
-        over_z[k] = [
-            go(
-                held.at[pl.ds(4 * (1 - low), 4), :, pl.ds(start + side * half, half)],
-                landing.at[:, :, pl.ds(start + side * half, half)],
-                z_send.at[k, side],
-                z_recv.at[k, side],
-                device,
-            )
-            for side, device in enumerate((inside, outside))
-        ]
-        for column in range(4):
-            owner = 4 * low + column
-            held[owner, :, cut] = held[owner, :, cut] + arrived[owner, :, cut]
+
+    def multiply(k, left_ref, right):
+        held, landing, _, cut = buffers(k)
+        for column in range(8):
+            owner = (4 * (1 - low) + column) % 8
+            held[owner, :, cut] = contract(left_ref[owner], right, ((1,), (0,))).astype(BF)
+            if column == 3:
+                half = held.shape[1] // 2
+                away = pl.ds(4 * (1 - low), 4)
+                over_z[k] = [
+                    go(
+                        held.at[away, pl.ds(side * half, half), cut],
+                        landing.at[:, pl.ds(side * half, half), cut],
+                        z_send.at[k, side],
+                        z_recv.at[k, side],
+                        device,
+                    )
+                    for side, device in enumerate((inside, outside))
+                ]
+
+    def make(index, k):
+        near_left, near_right, far_left, far_right = acts[index]
+        near_left.wait()
+        near_right.wait()
+        far_left.wait_recv()
+        far_right.wait_recv()
+        left = left_all[:, left_starts[index] : left_starts[index] + LEFT[index]].T
+        right = right_all[:, right_starts[index] : right_starts[index] + RIGHT[index]]
+        target = turned_one if index == 5 else turned
+        rows = LEFT[index] // 8
+        target[:, :rows, :] = left.reshape(8, rows, 2 * TOK)
+        multiply(k, target.at[:, pl.ds(0, rows), :], right)
 
     def step_z(k):
-        held, _, landing, spread, start, width = buffers(k)
-        cut = pl.ds(start, width)
+        held, landing, spread, cut = buffers(k)
         for copy in over_z[k]:
             copy.wait_recv()
         for column in range(4):
@@ -468,95 +504,105 @@
             for spot in (1, 0, 2)
         ]
 
-    def step_x(k, first=None):
-        _, _, landing, spread, start, width = buffers(k)
-        cut = pl.ds(start, width)
+    def step_x(k):
+        _, landing, spread, cut = buffers(k)
         for copy in over_x[k]:
             copy.wait_recv()
         total = landing[x, :, cut].astype(F32)
         for spot in range(3):
             total = total + spread[spot, :, cut].astype(F32)
         total = total.astype(BF)
+        half = D // 2
         if k == 0:
             for piece in range(8):
-                packed[piece, :, D : D + 512] = total[:, piece * 512 : piece * 512 + 512]
+                packed[piece, :, half : half + 256] = total[:, piece * 256 : piece * 256 + 256]
         elif k == DOWN:
             for piece in range(8):
                 for part in range(3):
-                    packed[piece, part * 16 : part * 16 + 16, D + 512 : D + 768] = total[
-                        piece * 16 : piece * 16 + 16, part * 256 : part * 256 + 256
+                    packed[piece, part * 32 : part * 32 + 32, half + 256 :] = total[
+                        piece * 32 : piece * 32 + 32, part * 128 : part * 128 + 128
                     ]
-        elif k == len(WIDTHS) - 1:
-            packed[0, :, ROOM - 128 :] = total[:, :128]
-            for piece in range(1, 8):
-                packed[piece, :, ROOM - 128 :] = jnp.zeros((PIECE, 128), BF)
+        elif k == CROSS_KV or k == SELF_KV:
+            for piece in range(2):
+                packed[(4 if k == CROSS_KV else 6) + piece, :, :half] = total[
+                    :, piece * half : piece * half + half
+                ]
         else:
-            for piece in range(width // D):
-                packed[first + piece, :, :D] = total[:, piece * D : (piece + 1) * D]
-
-    def outer(left_ref, rows, right):
-        left = left_ref[:, rows, :]
-        return contract(left.reshape(8 * PIECE, left.shape[-1]), right, ((1,), (0,))).astype(BF).reshape(
-            8, PIECE, right.shape[-1]
-        )
-
-    c_copies = rows_start(dckv_ref, c_kept, c_core, c_sem, 0)
-    s_copies = rows_start(dkv_ref, s_kept, s_core, s_sem, 4)
-    for k, source in enumerate((wide_ref, two_out_ref, two_query_ref, one_out_ref, one_query_ref)):
-        chunk_start(k, source)
-        if k == 0:
-            chunk_start(DOWN, down_ref)
-    c_onward = rows_send(c_copies, c_kept, c_core, c_row, c_sem)
-    s_onward = rows_send(s_copies, s_kept, s_core, s_row, s_sem)
-    for k in (0, DOWN, 1, 2, 3, 4):
-        step_core(k)
+            packed[k - 1, :, :half] = total
+
+    s_copies = rows_start(dkv_ref, s_kept, s_core, s_sem)
+    c_copies = rows_start(dckv_ref, c_kept, c_core, c_sem)
+    for index in range(6):
+        acts_start(index)
+    state_near = bring(state_ref, state_all.at[pl.ds(0, ENC)], local_sem.at[0])
+    state_far = go(
+        state_ref, state_all.at[pl.ds(ENC, ENC)], late_send.at[2], late_recv.at[2], sibling
+    )
+    s_state = rows_send(s_copies, s_kept, s_core, s_via, s_row, s_sem)
+    c_state = rows_send(c_copies, c_kept, c_core, c_via, c_row, c_sem)
+    make(0, 0)
+    s_onward = rows_via(s_state, s_kept, s_via, s_row, s_sem)
+    make(1, DOWN)
+    c_onward = rows_via(c_state, c_kept, c_via, c_row, c_sem)
+    for index in (2, 3, 4, 5):
+        make(index, index - 1)
     step_z(0)
-    c_last = rows_across(c_onward, c_kept, c_row, c_stage, c_high, c_sem)
     step_z(DOWN)
-    d_ckv = rows_sum(c_last, c_kept, c_row, c_high)
-    to_core[:, :, : 2 * D] = outer(states_ref, theirs, d_ckv)
-    chunk_send(5, 0)
-    kept[:, :, starts[5] : starts[5] + 2 * D] = outer(states_ref, mine, d_ckv)
-    encoder_ref[...] = contract(d_ckv, ckv_ref[...], ((1,), (1,)))
+    s_last = rows_across(s_onward, s_kept, s_row, s_stage, s_high, s_sem)
     for k in (1, 2, 3, 4):
         step_z(k)
-    step_core(5)
+    state_near.wait()
+    state_far.wait_recv()
+    turned_state[...] = state_all[...].T.reshape(8, PIECE, 2 * ENC)
+    s_far = rows_sum(s_last, s_kept, s_row, s_high, s_fin, s_right, 0)
     step_x(0)
-    step_x(DOWN)
-    s_last = rows_across(s_onward, s_kept, s_row, s_stage, s_high, s_sem)
-    step_z(5)
-    for k in (1, 2, 3, 4):
-        step_x(k, k - 1)
-    d_kv = rows_sum(s_last, s_kept, s_row, s_high)
-    over_core[5].wait_send()
-    to_core[:, :, : 2 * D] = outer(normed_ref, theirs, d_kv)
-    chunk_send(6, 0)
-    kept[:, :, starts[6] : starts[6] + 2 * D] = outer(normed_ref, mine, d_kv)
+    s_far.wait_recv()
+    multiply(SELF_KV, turned_one, s_right[...])
+    c_last = rows_across(c_onward, c_kept, c_row, c_stage, c_high, c_sem)
     tokens = token_ref[...].astype(F32)
+    d_kv = jnp.concatenate([s_fin[0], s_fin[1]], axis=1)
     grad = dn_ref[...] + contract(d_kv, kv_ref[...], ((1,), (1,)))
     inverse = lax.rsqrt(jnp.mean(tokens * tokens, axis=-1, keepdims=True) + 1e-06)
-    columns = contract(
-        (tokens * inverse * grad).astype(BF), jnp.ones((TOK, 128), BF), ((0,), (0,))
-    )
-    lane = lax.broadcasted_iota(jnp.int32, (D, 128), 1)
-    gain_cols[...] = jnp.where(lane == 0, columns, 0.0).astype(BF).reshape(8, 2 * PIECE, 128)
-    to_core[:, :, 2 * D : 2 * D + 128] = gain_cols[:, theirs, :] + extra_ref[:, theirs, :128]
-    to_core[:, :, 2 * D + 128 :] = extra_ref[:, theirs, 128:]
-    chunk_send(7, 2 * D)
-    kept[:, :, starts[7] : starts[7] + 128] = gain_cols[:, mine, :] + extra_ref[:, mine, :128]
-    kept[:, :, starts[7] + 128 :] = extra_ref[:, mine, 128:]
-    step_core(6)
-    step_core(7)
-    step_x(5, 4)
-    step_z(6)
-    step_z(7)
+    small_f32[...] = small_ref[...]
+    line = jnp.sum(tokens * inverse * grad, axis=0, keepdims=True)
+    for owner in range(8):
+        small_f32[owner, 0:1, :96] = line[:, owner * 96 : owner * 96 + 96]
+    sm_own[...] = small_f32[...].astype(BF)
+    sm_over = go(sm_own, sm_core, sm_send.at[0], sm_recv.at[0], sibling)
+    c_far = rows_sum(c_last, c_kept, c_row, c_high, c_fin, c_right, 1)
+    step_x(DOWN)
+    c_far.wait_recv()
+    multiply(CROSS_KV, turned_state, c_right[...])
+    step_z(SELF_KV)
+    sm_over.wait_recv()
+    sm_own_sum = (sm_own[...].astype(F32) + sm_core[...].astype(F32)).astype(BF)
+    sm_over.wait_send()
+    sm_own[...] = sm_own_sum
+    sm_inside = go(
+        sm_own.at[pl.ds(4 * (1 - low), 4)], sm_z, sm_send.at[1], sm_recv.at[1], inside
+    )
+    for k in (1, 2, 3, 4):
+        step_x(k)
+    step_z(CROSS_KV)
+    sm_inside.wait_recv()
+    for column in range(4):
+        sm_z[column] = sm_z[column] + sm_own[4 * low + column]
+    sm_row = [
+        go(
+            sm_z.at[(x + spot + 1) % 4], sm_x.at[spot],
+            sm_send.at[2 + spot], sm_recv.at[2 + spot], (me, others[spot]),
+        )
+        for spot in range(3)
+    ]
     scaled = gain_ref[...] * grad
     mixed = jnp.mean(tokens * scaled, axis=-1, keepdims=True)
     decoder_ref[...] = (
         dmid_ref[...] + inverse * scaled - tokens * (inverse * inverse * inverse * mixed)
     )
-    step_x(6, 6)
-    step_x(7)
+    d_ckv = jnp.concatenate([c_fin[0], c_fin[1]], axis=1)
+    encoder_ref[...] = contract(d_ckv, ckv_ref[...], ((1,), (1,)))
+    step_x(SELF_KV)
+    step_x(CROSS_KV)
 
 
     over_ctx = [
@@ -569,101 +615,144 @@
         )
         for spot, mate in enumerate(mates)
     ]
+    sm_sum = sm_z[x].astype(F32)
+    for spot in range(3):
+        sm_row[spot].wait_recv()
+        sm_sum = sm_sum + sm_x[spot].astype(F32)
+    sm_total[...] = sm_sum.astype(BF)
+    sm_mates = [
+        go(
+            sm_total, sm_ctx.at[spot],
+            sm_send.at[5 + spot], sm_recv.at[5 + spot], (mate * 2 + core, shard),
+        )
+        for spot, mate in enumerate(mates)
+    ]
     total = packed[rank].astype(F32)
     for spot in range(7):
         over_ctx[spot].wait_recv()
         total = total + from_ctx[spot].astype(F32)
-    total_ref[...] = total.astype(BF)
+    land[rank, core] = total.astype(BF)
+    own = land.at[rank, core]
     for spot, mate in enumerate(mates):
-        go(
-            total_ref,
-            out_ref.at[rank, mine, :],
-            out_send.at[spot],
-            out_recv.at[rank],
-            (mate * 2 + core, shard),
-        )
-    go(total_ref, out_ref.at[rank, mine, :], pass_send.at[7], pass_recv.at[rank], sibling)
-    own = bring(total_ref, out_ref.at[rank, mine, :], own_sem)
+        go(own, own, out_send.at[spot], out_recv.at[rank], (mate * 2 + core, shard))
+    go(own, own, pass_send.at[7], pass_recv.at[rank], sibling)
 
     def landed(ref, recv_sem):
         hop(ref, ref, pass_send.at[0], recv_sem, *sibling).wait_recv()
 
+    sm_sum = sm_total[...].astype(F32)
+    for spot in range(7):
+        sm_mates[spot].wait_recv()
+        sm_sum = sm_sum + sm_ctx[spot].astype(F32)
+    small_out[...] = sm_sum
     for spot, mate in enumerate(mates):
-        block = out_ref.at[mate, mine, :]
+        block = land.at[mate, core]
         landed(block, out_recv.at[mate])
         go(block, block, pass_send.at[spot], pass_recv.at[mate], sibling)
     for mate in [rank] + mates:
-        landed(out_ref.at[mate, theirs, :], pass_recv.at[mate])
-    own.wait()
+        landed(land.at[mate, 1 - core], pass_recv.at[mate])
+    half = D // 2
+    for side in range(2):
+        for piece in range(4):
+            square_refs[piece][:, side * half : side * half + half] = land[
+                piece, side, :, :half
+            ].astype(F32)
+            square_refs[4 + 2 * (piece // 2) + side][
+                :, (piece % 2) * half : (piece % 2) * half + half
+            ] = land[4 + piece, side, :, :half].astype(F32)
+        target = up_ref if side else gate_ref
+        for piece in range(8):
+            target[:, piece * 256 : piece * 256 + 256] = land[
+                piece, side, :, half : half + 256
+            ].astype(F32)
+            for part in range(3):
+                down_ref[
+                    piece * 32 : piece * 32 + 32,
+                    side * half + part * 128 : side * half + part * 128 + 128,
+                ] = land[piece, side, part * 32 : part * 32 + 32, half + 256 :].astype(F32)
     for copy in sends:
-        if copy is not over_core[5]:
+        if copy is not sm_over:
             copy.wait_send()
 
 
 def finish(far, near, collective_id):
     dma = pltpu.SemaphoreType.DMA
-    chunks = len(WIDTHS) + 1
 
     def rows(count):
         return [
             pltpu.VMEM((8, 2, count, D), BF),
             pltpu.VMEM((8, 2, count, D), BF),
-            pltpu.VMEM((3, 2, 2, count, D), BF),
+            pltpu.VMEM((2, 2, 2, count, D), BF),
+            pltpu.VMEM((2, 2, count, D), BF),
+            pltpu.VMEM((2, count, D), BF),
             pltpu.VMEM((2, count, D), BF),
             pltpu.VMEM((2, count, D), BF),
         ]
 
+    outs = (
+        [jax.ShapeDtypeStruct((TOK, D), F32), jax.ShapeDtypeStruct((ENC, D), F32)]
+        + [jax.ShapeDtypeStruct((PIECE, D), F32)] * 8
+        + [jax.ShapeDtypeStruct((PIECE, FF), F32)] * 2
+        + [jax.ShapeDtypeStruct((FF // 8, D), F32), jax.ShapeDtypeStruct((16, 128), F32)]
+    )
     return pl.pallas_call(
         finish_kernel,
-        out_shape=[
-            jax.ShapeDtypeStruct((8, 2 * PIECE, ROOM), BF),
-            jax.ShapeDtypeStruct((TOK, D), F32),
-            jax.ShapeDtypeStruct((ENC, D), F32),
-        ],
+        out_shape=outs,
         in_specs=[pl.BlockSpec(memory_space=pl.ANY)] * len(far)
         + [pl.BlockSpec(memory_space=pltpu.VMEM)] * len(near),
-        out_specs=[
-            pl.BlockSpec(memory_space=pl.ANY),
-            pl.BlockSpec(memory_space=pltpu.VMEM),
-            pl.BlockSpec(memory_space=pltpu.VMEM),
-        ],
+        out_specs=[pl.BlockSpec(memory_space=pltpu.VMEM)] * len(outs),
         scratch_shapes=[
-            pltpu.VMEM((8, PIECE, SPAN), BF),
+            pltpu.VMEM((2 * TOK, sum(LEFT)), BF),
+            pltpu.VMEM((2 * TOK, sum(RIGHT)), BF),
+            pltpu.VMEM((8, FF // 8, 2 * TOK), BF),
+            pltpu.VMEM((8, PIECE, 2 * TOK), BF),
+            pltpu.VMEM((8, PIECE, 2 * ENC), BF),
+            pltpu.VMEM((2 * ENC, D), BF),
+            pltpu.VMEM((2 * TOK, D), BF),
+            pltpu.VMEM((2 * ENC, D), BF),
             pltpu.VMEM((8, PIECE, SPAN), BF),
             pltpu.VMEM((4, PIECE, SPAN), BF),
             pltpu.VMEM((3, PIECE, SPAN), BF),
-            pltpu.VMEM((8, 128, D), BF),
-            pltpu.VMEM((8, 128, D), BF),
-            pltpu.VMEM((4, 128, D), BF),
-            pltpu.VMEM((3, 128, D), BF),
+            pltpu.VMEM((8, FF // 8, D // 2), BF),
+            pltpu.VMEM((4, FF // 8, D // 2), BF),
+            pltpu.VMEM((3, FF // 8, D // 2), BF),
         ]
         + rows(TOK)
         + rows(ENC)
         + [
-            pltpu.VMEM((8, PIECE, 2 * D + 256), BF),
-            pltpu.VMEM((8, 2 * PIECE, 128), BF),
+            pltpu.VMEM((8, 16, 128), F32),
+            pltpu.VMEM((8, 16, 128), BF),
+            pltpu.VMEM((8, 16, 128), BF),
+            pltpu.VMEM((4, 16, 128), BF),
+            pltpu.VMEM((3, 16, 128), BF),
+            pltpu.VMEM((7, 16, 128), BF),
+            pltpu.VMEM((16, 128), BF),
             pltpu.VMEM((8, PIECE, ROOM), BF),
             pltpu.VMEM((7, PIECE, ROOM), BF),
-            pltpu.VMEM((PIECE, ROOM), BF),
-            dma((4, 4)),
-            dma((4, 4)),
-            dma((8 + chunks,)),
-            dma((chunks,)),
-            dma((chunks,)),
-            dma((chunks, 2)),
-            dma((chunks, 2)),
-            dma((chunks, 3)),
-            dma((chunks, 3)),
+            pltpu.VMEM((8, 2, PIECE, ROOM), BF),
+            dma((5, 7)),
+            dma((5, 7)),
+            dma((6, 2)),
+            dma((6, 2)),
+            dma((6, 2)),
+            dma((3,)),
+            dma((3,)),
+            dma((CHUNKS, 2)),
+            dma((CHUNKS, 2)),
+            dma((CHUNKS, 3)),
+            dma((CHUNKS, 3)),
             dma((7,)),
             dma((7,)),
             dma((7,)),
             dma((8,)),
             dma((8,)),
             dma((8,)),
-            dma,
+            dma((12,)),
+            dma((12,)),
+            dma((1,)),
         ],
         compiler_params=pltpu.CompilerParams(
-            collective_id=collective_id, has_side_effects=True, vmem_limit_bytes=60 * MIB
+            collective_id=collective_id, has_side_effects=True, vmem_limit_bytes=62 * MIB
         ),
         name="finish_gradients",
     )(*far, *near)
@@ -1024,8 +1113,6 @@
 
     d_hidden = transposed_right(upstream, down)
     d_gate_up = jnp.concatenate(pull_feed(d_hidden), axis=1).astype(BF)
-    grad_down = transposed_left(hidden, upstream).astype(BF)
-    grad_gate_up = transposed_left(normed_three, d_gate_up).astype(BF)
     d_normed_three = transposed_right(d_gate_up, gate_up)
     part_three, grad_norm_three = rms_back(mid_two, norm_three, d_normed_three)
     d_mid_two = upstream.astype(F32) + part_three
@@ -1034,8 +1121,6 @@
     d_cross_queries, d_cross_kv_all = attend_back(
         cross_queries, cross_kv, d_cross_attended, cross_totals, ENC, 0
     )
-    grad_out_two = transposed_left(cross_attended, cross_branch).astype(BF)
-    grad_query_two = transposed_left(normed_two, d_cross_queries).astype(BF)
     d_normed_two = transposed_right(d_cross_queries, query_two)
     part_two, grad_norm_two = rms_back(mid_one, norm_two, d_normed_two)
     d_mid_one = d_mid_two + part_two
@@ -1045,68 +1130,59 @@
         queries, self_kv, d_attended, self_totals, TOK, 0, classes, near, tiles
     )
     grad_table = matmul(bias_sums(strips), bucket_hot.astype(F32)).T.reshape(8, 4, HEADS)
-    grad_extra = jnp.concatenate(
+    grad_gains = jnp.stack([grad_norm_two, grad_norm_three]).reshape(2, 8, rows)
+    grad_small = jnp.concatenate(
         [
-            jnp.zeros((D, 1), F32),
-            grad_norm_two[:, None],
-            grad_norm_three[:, None],
-            jnp.zeros((D, 5), F32),
-            jnp.pad(grad_table, ((0, 0), (0, rows - 4), (0, 0))).reshape(D, HEADS),
-            jnp.zeros((D, 236), F32),
+            jnp.zeros((8, 1, 128), F32),
+            jnp.pad(jnp.transpose(grad_gains, (1, 0, 2)), ((0, 0), (0, 0), (0, 128 - rows))),
+            jnp.pad(grad_table, ((0, 0), (0, 9), (0, 128 - HEADS))),
         ],
         axis=1,
     )
-    grad_out_one = transposed_left(attended, self_branch).astype(BF)
-    grad_query_one = transposed_left(normed_one, d_queries).astype(BF)
-    summed, grad_decoder, grad_encoder = finish(
+    done = finish(
         [
+            normed_three, hidden, cross_attended, normed_two, attended, normed_one,
+            d_gate_up, upstream, cross_branch, d_cross_queries, self_branch, d_queries,
+            d_kv_all.reshape(8, 2, 2, TOK, D),
             d_cross_kv_all.reshape(8, 2, 2, ENC, D),
-            d_kv_all.reshape(8, 2, 2, TOK, D),
-            grad_gate_up.reshape(8, rows, -1),
-            grad_out_two.reshape(8, rows, D),
-            grad_query_two.reshape(8, rows, D),
-            grad_out_one.reshape(8, rows, D),
-            grad_query_one.reshape(8, rows, D),
-            grad_down.reshape(8, -1, D),
         ],
         [
-            normed_one.T.reshape(8, rows, TOK),
-            states.T.reshape(8, rows, ENC),
+            states,
             kv_one,
             kv_two,
             transposed_right(d_queries, query_one),
             d_mid_one,
             decoder_in[0],
             norm_one,
-            grad_extra.astype(BF).reshape(8, rows, 256),
+            grad_small,
         ],
         3,
     )
-    owned = summed[:, :, :D].astype(F32)
-    wide = summed[:, :, D : D + 512].astype(F32)
-    wide = jnp.transpose(wide, (1, 0, 2)).reshape(rows, 2 * FF)
-    tall = summed[:, :, D + 512 : D + 768].astype(F32).reshape(8, 2, 3, 16, 256)
-    tall = jnp.transpose(tall, (1, 0, 3, 2, 4)).reshape(256, D)
-    extras = summed[0, :, D + 768 :].astype(F32)
+    grad_decoder, grad_encoder = done[:2]
+    (
+        grad_out_two, grad_query_two, grad_out_one, grad_query_one,
+        grad_key_two, grad_value_two, grad_key_one, grad_value_one,
+        grad_gate, grad_up, grad_down, extras,
+    ) = done[2:]
     return (
         block_out[None],
         grad_decoder[None],
         grad_encoder[None],
-        extras[:, 0],
-        owned[3],
-        owned[6],
-        owned[7],
-        owned[2],
-        extras[:4, 8:20],
-        extras[:, 1],
-        owned[1],
-        owned[4],
-        owned[5],
-        owned[0],
-        extras[:, 2],
-        wide[:, :FF],
-        wide[:, FF:],
-        tall,
+        extras[0, :rows],
+        grad_query_one,
+        grad_key_one,
+        grad_value_one,
+        grad_out_one,
+        extras[3:7, :HEADS],
+        extras[1, :rows],
+        grad_query_two,
+        grad_key_two,
+        grad_value_two,
+        grad_out_two,
+        extras[2, :rows],
+        grad_gate,
+        grad_up,
+        grad_down,
     )
 
 

time: 371 us -> 378 us (1.019)
  Pallas kernels: 271 us -> 308 us
  local copies, waits for them, and re-layouts: 44 us -> 27.8 us
  matrix products: 40.3 us -> 24.2 us
    pallas_call x1, Pallas kernels: 86 us -> 130 us  [front(): pl.pallas_call(front_kernel, out_shape=[jax.ShapeDtypeStruct(pack, BF) fo...]
    dot_general x15 -> x9, matrix products: 28.8 us -> 15.6 us  [contract(): lax.dot_general(left, right, (dims, ((), ())), preferred_element_type=F32)]
    unnamed x131 -> x81, local copies, waits for them, and re-layouts: 28.4 us -> 18.2 us
    pallas_call x1, Pallas kernels: 147 us -> 140 us  [finish(): pl.pallas_call(finish_kernel, out_shape=outs, in_specs=[pl.BlockSpec(memo...]
where the time goes in v3:
time: 378 us; the launch traced here: 377 us
  Pallas kernels  308 us (81%)
  local copies, waits for them, and re-layouts  27.8 us (7%)
  matrix products  24.2 us (6%)
  other arithmetic  15.4 us (4%)
    pallas_call x1, Pallas kernels, finish(): pl.pallas_call(finish_kernel, out_shape=outs, in_specs=[pl.BlockSpec(memo...  140 us
    pallas_call x1, Pallas kernels, front(): pl.pallas_call(front_kernel, out_shape=[jax.ShapeDtypeStruct(pack, BF) fo...  130 us
    pallas_call x2, Pallas kernels, attend_back(): pl.pallas_call(functools.partial(backward_kernel, biased), grid=(PAIRS,),...  21.9 us
    unnamed x81, local copies, waits for them, and re-layouts  18.2 us
    pallas_call x2, Pallas kernels, attend(): pl.pallas_call(functools.partial(forward_kernel, biased), grid=(PAIRS,),...  16.4 us
    dot_general x9, matrix products, contract(): lax.dot_general(left, right, (dims, ((), ())), preferred_element_type=F32)  15.6 us
    dot_general x7, matrix products, matmul(): return jnp.dot(left, right, preferred_element_type=F32)  8.62 us

profile of v3, /device:TPU:1, one launch (start us, length us, event | category | flops | bytes accessed | tf_op | source)
XLA Modules:
  0.0 376.9 jit_solution(14969970449262450476)
XLA Ops:
  0.7 1.2 dynamic_slice.3
  5.8 1.3 fusion.45.refs_11_
  8.5 1.3 fusion.2
  9.8 129.6 %front.1 = (bf16[8,96,1536]{2,1,0:T(8,128)(2,1)}, bf16[8,96,1536]{2,1,0:T(8,128)(2,1)}, bf16[8,96,3072]{2,1,0:T(8,128)(2,1)}, bf16[8,96,4096]{2,1,0:T(8,128)(2,1...) custom-call(bf16[96,768]{1,0:T(8,128)(2,1)} %refs_0_.1, ...), custom_call_target="tpu_custom_call" | custom-call | tf_op jit(solution)/shard_map/front/pallas_call | solution.py:259
  146.1 10.4 %attend_self.1 = (bf16[128,768]{1,0:T(8,128)(2,1)S(1)}, f32[6,8,256]{2,1,0:T(8,128)S(1)}) custom-call(s32[2,32]{1,0:T(2,128)S(1)} %compare_select_fusion.1.refs_0_, bf16[128,768]{1,0:T(8,128)(2,1)S(1)} %copy-done.4, bf16[16,2,128,768]{3,2,1,0:T(8,128)(2,1)} %get-tuple-element.52.refs_2_.refs_3_.refs_4_, ...), custom_call_target="tpu_custom_call" | custom-call | flops 1000000000 | bytes 10000000 | tf_op jit(solution)/shard_map/attend_self/pallas_call | solution.py:912
  156.5 1.8 multiply_reduce_fusion.5
  159.2 1.6 convolution_convert_fusion.3.refs_0_
  160.8 6.1 %attend_cross.1 = (bf16[128,768]{1,0:T(8,128)(2,1)S(1)}, f32[6,8,256]{2,1,0:T(8,128)S(1)}) custom-call(bf16[128,768]{1,0:T(8,128)(2,1)S(1)} %convolution_convert_fusion.3.refs_0_, bf16[16,2,64,768]{3,2,1,0:T(8,128)(2,1)S(1)} %copy-done, bf16[16,2,64,768]{3,2,1,0:T(8,128)(2,1)S(1)} %copy-done), custom_call_target="tpu_custom_call" | custom-call | flops 1000000000 | bytes 10000000 | tf_op jit(solution)/shard_map/attend_cross/pallas_call | solution.py:912
  166.9 1.8 multiply_reduce_fusion.4
  168.9 1.0 fusion.4
  170.8 1.6 fusion.14
  172.4 1.3 fusion.5
  173.8 3.0 multiply_reduce_fusion
  176.7 1.1 pad_maximum_fusion.refs_6_
  177.9 1.1 fusion.58.refs_8_
  179.7 1.8 convolution_convert_fusion.2.refs_3_
  181.5 8.2 %attend_cross_back.1 = (bf16[128,768]{1,0:T(8,128)(2,1)S(1)}, bf16[16,2,64,768]{3,2,1,0:T(8,128)(2,1)S(1)}) custom-call(bf16[128,768]{1,0:T(8,128)(2,1)S(1)} %convolution_convert_fusion.3.refs_0_, bf16[16,2,64,768]{3,2,1,0:T(8,128)(2,1)} %get-tuple-element.56.refs_1_.refs_2_, bf16[16,2,64,768]{3,2,1,0:T(8,128)(2,1)} %get-tuple-element.56.refs_1_.refs_2_, ...), custom_call_target="tpu_custom_call" | custom-call | flops 3000000000 | bytes 10000000 | tf_op jit(solution)/shard_map/attend_cross_back/pallas_call | solution.py:949
  189.8 1.6 copy-done.1
  191.4 2.7 multiply_reduce_fusion.1
  194.2 2.1 fusion.61
  196.3 1.9 convolution_convert_fusion.1.refs_5_
  198.2 13.7 %attend_self_back.1 = (bf16[128,768]{1,0:T(8,128)(2,1)S(1)}, bf16[16,2,128,768]{3,2,1,0:T(8,128)(2,1)}, f32[12,3,64,128]{3,2,1,0:T(8,128)S(1)}) custom-call(s32[2,32]{1,0:T(2,128)S(1)} %compare_select_fusion.1.refs_0_, s32[2,3]{1,0:T(2,128)S(1)} %copy.48.refs_1_, bf16[128,768]{1,0:T(8,128)(2,1)S(1)} %copy-done.4, ...), custom_call_target="tpu_custom_call" | custom-call | flops 3000000000 | bytes 10000000 | tf_op jit(solution)/shard_map/attend_self_back/pallas_call | solution.py:949
  211.9 2.6 fusion.6.refs_17_
  214.5 1.4 slice_add_fusion
  215.9 1.7 reshape.190
  220.7 139.7 %finish_gradients.1 = (f32[128,768]{1,0:T(8,128)}, f32[64,768]{1,0:T(8,128)}, f32[96,768]{1,0:T(8,128)}, f32[96,768]{1,0:T(8,128)}, f32[96,768]{1,0:T(8,128)}, /...) custom-call(bf16[128,768]{1,0:T(8,128)(2,1)} %copy-done.10, ...), custom_call_target="tpu_custom_call" | custom-call | tf_op jit(solution)/shard_map/finish_gradients/pallas_call | solution.py:698
  360.4 1.3 slice_bitcast_fusion
  361.7 1.3 slice.80
  363.0 1.8 copy.70
  364.8 1.7 copy.71
  366.4 1.7 copy.72
  368.2 1.8 copy.73
  (126 shorter events, 24.0 us)
Async XLA Ops:
  8.5 133.1 %copy-start.30 = (s32[128]{0:T(128)S(1)}, s32[128]{0:T(128)}, u32[]{:S(2)}) copy-start(s32[128]{0:T(128)} %param.24) | copy-start | bytes 1540
  9.8 134.0 %copy-start.7 = (pred[128,12288]{1,0:T(32,128)(4,1)}, pred[128,12288]{1,0:T(32,128)(4,1)S(1)}, u32[]{:S(2)}) copy-start(pred[128,12288]{1,0:T(32,128)(4,1)S(1)} %fusion.2) | copy-start | bytes 4718596
  144.2 1.0 copy-start.15
  145.2 1.0 copy-start.4
  145.3 23.5 %slice-start = ((s8[6291456]{0:T(1024)(128)(4,1)}), s8[4194304]{0:T(1024)(128)(4,1)S(1)}, s32[]{:S(2)}) async-start(s8[6291456]{0:T(1024)(128)(4,1)} %bitcast.68), calls=%async_computation | async-start | bytes 8388608
  146.1 10.4 %copy-start.18 = (bf16[1,128,768]{2,1,0:T(8,128)(2,1)S(1)}, bf16[1,128,768]{2,1,0:T(8,128)(2,1)}, u32[]{:S(2)}) copy-start(bf16[1,128,768]{2,1,0:T(8,128)(2,1)} %param.20) | copy-start | bytes 589828
  146.1 22.7 %slice-start.1 = ((s8[6291456]{0:T(1024)(128)(4,1)}), s8[2097152]{0:T(1024)(128)(4,1)S(1)}, s32[]{:S(2)}) async-start(s8[6291456]{0:T(1024)(128)(4,1)} %bitcast.68), calls=%async_computation.1 | async-start | bytes 4194304
  156.5 4.3 %copy-start.5 = (bf16[128,768]{1,0:T(8,128)(2,1)}, bf16[128,768]{1,0:T(8,128)(2,1)S(1)}, u32[]{:S(2)}) copy-start(bf16[128,768]{1,0:T(8,128)(2,1)S(1)} %get-tuple-element.54.refs_4_) | copy-start | bytes 589828
  156.5 4.3 %copy-start = (bf16[16,2,64,768]{3,2,1,0:T(8,128)(2,1)S(1)}, bf16[16,2,64,768]{3,2,1,0:T(8,128)(2,1)}, u32[]{:S(2)}) copy-start(bf16[16,2,64,768]{3,2,1,0:T(8,128)(2,1)} %get-tuple-element.56.refs_1_.refs_2_) | copy-start | bytes 9437188
  166.9 3.0 copy-start.2
  168.8 1.0 copy-start.10
  168.8 2.0 copy-start.9
  168.9 2.0 copy-start.12
  172.4 1.4 copy-start.11
  176.7 1.2 copy-start.13
  189.8 1.6 copy-start.1
  191.4 4.9 %copy-start.6 = (bf16[128,768]{1,0:T(8,128)(2,1)}, bf16[128,768]{1,0:T(8,128)(2,1)S(1)}, u32[]{:S(2)}) copy-start(bf16[128,768]{1,0:T(8,128)(2,1)S(1)} %get-tuple-element.62.refs_9_) | copy-start | bytes 589828
  191.4 2.8 copy-start.14
  196.3 15.6 %copy-start.19 = (bf16[128,768]{1,0:T(8,128)(2,1)}, bf16[128,768]{1,0:T(8,128)(2,1)S(1)}, u32[]{:S(2)}) copy-start(bf16[128,768]{1,0:T(8,128)(2,1)S(1)} %get-tuple-element.93.refs_10_) | copy-start | bytes 589828
  211.9 4.0 %copy-start.3 = (bf16[128,768]{1,0:T(8,128)(2,1)}, bf16[128,768]{1,0:T(8,128)(2,1)S(1)}, u32[]{:S(2)}) copy-start(bf16[128,768]{1,0:T(8,128)(2,1)S(1)} %get-tuple-element.64.refs_11_) | copy-start | bytes 589828
  214.5 3.1 copy-start.8
  217.6 2.1 copy-start.31
  217.6 2.4 copy-start.29
  360.4 9.6 %copy-start.28 = (f32[96,768]{1,0:T(8,128)S(1)}, f32[96,768]{1,0:T(8,128)}, u32[]{:S(2)}) copy-start(f32[96,768]{1,0:T(8,128)} %get-tuple-element.141) | copy-start | bytes 884740
  360.4 10.3 %copy-start.27 = (f32[96,768]{1,0:T(8,128)S(1)}, f32[96,768]{1,0:T(8,128)}, u32[]{:S(2)}) copy-start(f32[96,768]{1,0:T(8,128)} %get-tuple-element.142) | copy-start | bytes 884740
  360.4 11.0 %copy-start.26 = (f32[96,768]{1,0:T(8,128)S(1)}, f32[96,768]{1,0:T(8,128)}, u32[]{:S(2)}) copy-start(f32[96,768]{1,0:T(8,128)} %get-tuple-element.145) | copy-start | bytes 884740
  360.4 11.7 %copy-start.25 = (f32[96,768]{1,0:T(8,128)S(1)}, f32[96,768]{1,0:T(8,128)}, u32[]{:S(2)}) copy-start(f32[96,768]{1,0:T(8,128)} %get-tuple-element.146) | copy-start | bytes 884740
  364.8 8.0 %copy-start.24 = (f32[96,768]{1,0:T(8,128)S(1)}, f32[96,768]{1,0:T(8,128)}, u32[]{:S(2)}) copy-start(f32[96,768]{1,0:T(8,128)} %get-tuple-element.147) | copy-start | bytes 884740
  366.4 7.1 %copy-start.23 = (f32[96,768]{1,0:T(8,128)S(1)}, f32[96,768]{1,0:T(8,128)}, u32[]{:S(2)}) copy-start(f32[96,768]{1,0:T(8,128)} %get-tuple-element.148) | copy-start | bytes 884740
  368.2 6.1 %copy-start.22 = (f32[96,2048]{1,0:T(8,128)S(1)}, f32[96,2048]{1,0:T(8,128)}, u32[]{:S(2)}) copy-start(f32[96,2048]{1,0:T(8,128)} %get-tuple-element.150) | copy-start | bytes 2359300
  371.4 3.8 copy-start.21
  372.8 3.2 copy-start.20
  (2 other events, 1.4 us)

commit v4 on v3

--- a/solution.py
+++ b/solution.py
@@ -63,12 +63,13 @@
 def front_kernel(*refs):
     sources = refs[:11]
     small_ref, token_ref, state_ref = refs[11:14]
-    targets = refs[14:19]
-    small_out, normed_out, query_out, self_out_ref, cross_out_ref = refs[19:24]
+    results = refs[14:19]
+    small_out, normed_out, query_out, self_result, cross_result = refs[19:24]
+    targets = refs[24:29]
     (
-        landing, weight_ref, self_ref, cross_ref, send_sem, x_sem, z_sem, core_sem, fill_sem,
-        small_sem, self_sem, cross_sem, local_sem,
-    ) = refs[24:]
+        self_out_ref, cross_out_ref, landing, self_ref, cross_ref, send_sem, x_sem, z_sem, core_sem,
+        fill_sem, small_sem, self_sem, cross_sem, local_sem,
+    ) = refs[29:]
     me, core, high, y, low, x = torus_place()
     shard = low * 4 + x
     sibling = (slot_of(y, 0, high, 1 - core), shard)
@@ -209,17 +210,17 @@
     pass_x(1)
     send_own(3)
     complete(0)
-    bring(targets[0], weight_ref, local_sem.at[1]).wait()
+    exits = [bring(targets[0], results[0], local_sem.at[1])]
     for half in range(2):
-        weight = weight_ref[:, :, half * D : half * D + D].reshape(D, D)
+        weight = targets[0][:, :, half * D : half * D + D].reshape(D, D)
         self_ref[half] = matmul(normed, weight).astype(BF)
     kv_start(self_ref, self_out_ref, self_sem)
     own_self = bring(self_ref, self_out_ref.at[me], local_sem.at[2])
     pass_z(1)
     complete(1)
-    bring(targets[1], weight_ref, local_sem.at[1]).wait()
+    exits.append(bring(targets[1], results[1], local_sem.at[4]))
     for half in range(2):
-        weight = weight_ref[:, :, half * D : half * D + D].reshape(D, D)
+        weight = targets[1][:, :, half * D : half * D + D].reshape(D, D)
         cross_ref[half] = matmul(state_ref[...], weight).astype(BF)
     kv_start(cross_ref, cross_out_ref, cross_sem)
     own_cross = bring(cross_ref, cross_out_ref.at[me], local_sem.at[3])
@@ -237,16 +238,22 @@
     pass_z(4)
     kv_rows(cross_out_ref, cross_sem, True)
     complete(2)
-    bring(targets[2].at[:, :, pl.ds(0, D)], weight_ref.at[:, :, pl.ds(0, D)], local_sem.at[1]).wait()
-    query_out[...] = matmul(normed, weight_ref[:, :, :D].reshape(D, D)).astype(BF)
-    complete(3)
-    complete(4)
-    kv_complete(self_out_ref, self_sem)
-    kv_complete(cross_out_ref, cross_sem)
+    exits.append(bring(targets[2], results[2], local_sem.at[5]))
+    query_out[...] = matmul(normed, targets[2][:, :, :D].reshape(D, D)).astype(BF)
     own_self.wait()
     own_cross.wait()
+    kv_complete(self_out_ref, self_sem)
+    exits.append(bring(self_out_ref, self_result, local_sem.at[6]))
+    kv_complete(cross_out_ref, cross_sem)
+    exits.append(bring(cross_out_ref, cross_result, local_sem.at[7]))
+    complete(3)
+    exits.append(bring(targets[3], results[3], local_sem.at[8]))
+    complete(4)
+    exits.append(bring(targets[4], results[4], local_sem.at[9]))
     for copy in sends:
         copy.wait_send()
+    for copy in exits:
+        copy.wait()
 
 
 def front(weights, small, tokens, states, collective_id):
@@ -268,9 +275,11 @@
         ],
         in_specs=[anywhere] * 12 + [inside] * 2,
         out_specs=[anywhere] * 5 + [inside] * 3 + [anywhere] * 2,
-        scratch_shapes=[
+        scratch_shapes=[pltpu.VMEM(pack, BF) for pack in packs]
+        + [
+            pltpu.VMEM((N_CTX, 2, TOK, D), BF),
+            pltpu.VMEM((N_CTX, 2, ENC, D), BF),
             pltpu.VMEM((8, 16, 128), BF),
-            pltpu.VMEM((8, 96, 2 * D), BF),
             pltpu.VMEM((2, TOK, D), BF),
             pltpu.VMEM((2, ENC, D), BF),
             dma((5 * 22 + 7 + 30,)),
@@ -281,7 +290,7 @@
             dma((7,)),
             dma((N_CTX,)),
             dma((N_CTX,)),
-            dma((4,)),
+            dma((10,)),
         ],
         compiler_params=pltpu.CompilerParams(
             collective_id=collective_id, has_side_effects=True, vmem_limit_bytes=60 * MIB
@@ -292,33 +301,31 @@
 
 PIECE = 96
 ROOM = D // 2 + FF // 8 + FF // 16
-WIDTHS = (FF, D // 2, D // 2, D // 2, D // 2, D, D)
+WIDTHS = (D // 2, D // 2, D // 2, D // 2, D, D, FF)
 SPAN = sum(WIDTHS)
 DOWN = len(WIDTHS)
 CHUNKS = DOWN + 1
-CROSS_KV, SELF_KV = 5, 6
-LEFT = (D, FF, D, D, D, D)
-RIGHT = (FF, D // 2, D // 2, D // 2, D // 2, D // 2)
+CROSS_KV, SELF_KV, WIDE = 4, 5, 6
+LEFT = (D,) * 4
+RIGHT = (D // 2,) * 4
 
 
 def finish_kernel(*refs):
-    lefts = refs[:6]
-    rights = refs[6:12]
-    dkv_ref, dckv_ref = refs[12:14]
-    state_ref, kv_ref, ckv_ref, dn_ref, dmid_ref, token_ref, gain_ref, small_ref = refs[14:22]
-    decoder_ref, encoder_ref = refs[22:24]
-    square_refs = refs[24:32]
-    gate_ref, up_ref, down_ref, small_out = refs[32:36]
+    lefts = refs[:4]
+    rights = refs[4:8]
+    wide_ref, down_ref, dkv_ref, dckv_ref = refs[8:12]
+    state_ref, kv_ref, ckv_ref, dn_ref, dmid_ref, token_ref, gain_ref, small_ref = refs[12:20]
+    land_out, small_out, decoder_ref, encoder_ref = refs[20:24]
     (
         left_all, right_all, turned, turned_one, turned_state, state_all, s_right, c_right,
-        kept, from_z, from_x, d_kept, d_z, d_x,
+        kept, from_z, from_x, via_x, d_z, d_x, d_via,
         s_kept, s_core, s_row, s_via, s_stage, s_high, s_fin,
         c_kept, c_core, c_row, c_via, c_stage, c_high, c_fin,
         small_f32, sm_own, sm_core, sm_z, sm_x, sm_ctx, sm_total, packed, from_ctx, land,
         s_sem, c_sem, fill_sem, act_send, act_recv, late_send, late_recv, z_send, z_recv,
         x_send, x_recv, ctx_send, ctx_recv, out_send, out_recv, pass_send, pass_recv,
         sm_send, sm_recv, local_sem,
-    ) = refs[36:]
+    ) = refs[24:]
     me, core, high, y, low, x = torus_place()
     shard = low * 4 + x
     rank = y * 2 + high
@@ -425,15 +432,17 @@
 
 
     starts = [sum(WIDTHS[:k]) for k in range(len(WIDTHS))]
-    left_starts = [sum(LEFT[:k]) for k in range(6)]
-    right_starts = [sum(RIGHT[:k]) for k in range(6)]
+    left_starts = [sum(LEFT[:k]) for k in range(4)]
+    right_starts = [sum(RIGHT[:k]) for k in range(4)]
     acts = {}
-    over_z, over_x = {}, {}
+    over_z, over_via, over_x = {}, {}, {}
+    column_ahead = (me, low * 4 + (x + 1) % 4)
+    column_behind = (me, low * 4 + (x + 3) % 4)
 
     def buffers(k):
         if k == DOWN:
-            return d_kept, d_z, d_x, pl.ds(0, D // 2)
-        return kept, from_z, from_x, pl.ds(starts[k], WIDTHS[k])
+            return d_z, d_x, d_via, pl.ds(0, D // 2)
+        return from_z, from_x, via_x, pl.ds(starts[k], WIDTHS[k])
 
     def acts_start(index):
         left = pl.ds(left_starts[index], LEFT[index])
@@ -456,16 +465,18 @@
         )
 
     def multiply(k, left_ref, right):
-        held, landing, _, cut = buffers(k)
-        for column in range(8):
-            owner = (4 * (1 - low) + column) % 8
-            held[owner, :, cut] = contract(left_ref[owner], right, ((1,), (0,))).astype(BF)
-            if column == 3:
-                half = held.shape[1] // 2
-                away = pl.ds(4 * (1 - low), 4)
+        landing, _, _, cut = buffers(k)
+        for group in range(2):
+            owners = pl.ds(4 * ((1 - low + group) % 2), 4)
+            left = left_ref[owners].reshape(4 * PIECE, right.shape[0])
+            kept[owners, :, cut] = (
+                contract(left, right, ((1,), (0,))).astype(BF).reshape(4, PIECE, WIDTHS[k])
+            )
+            if group == 0:
+                half = PIECE // 2
                 over_z[k] = [
                     go(
-                        held.at[away, pl.ds(side * half, half), cut],
+                        kept.at[owners, pl.ds(side * half, half), cut],
                         landing.at[:, pl.ds(side * half, half), cut],
                         z_send.at[k, side],
                         z_recv.at[k, side],
@@ -474,7 +485,7 @@
                     for side, device in enumerate((inside, outside))
                 ]
 
-    def make(index, k):
+    def make(index):
         near_left, near_right, far_left, far_right = acts[index]
         near_left.wait()
         near_right.wait()
@@ -482,38 +493,77 @@
         far_right.wait_recv()
         left = left_all[:, left_starts[index] : left_starts[index] + LEFT[index]].T
         right = right_all[:, right_starts[index] : right_starts[index] + RIGHT[index]]
-        target = turned_one if index == 5 else turned
-        rows = LEFT[index] // 8
-        target[:, :rows, :] = left.reshape(8, rows, 2 * TOK)
-        multiply(k, target.at[:, pl.ds(0, rows), :], right)
+        target = turned_one if index == 3 else turned
+        target[...] = left.reshape(8, PIECE, 2 * TOK)
+        multiply(index, target, right)
 
     def step_z(k):
-        held, landing, spread, cut = buffers(k)
+        landing, _, _, cut = buffers(k)
         for copy in over_z[k]:
             copy.wait_recv()
         for column in range(4):
-            landing[column, :, cut] = landing[column, :, cut] + held[4 * low + column, :, cut]
+            landing[column, :, cut] = landing[column, :, cut] + kept[4 * low + column, :, cut]
+        send_x(k)
+
+
+    def send_x(k):
+        landing, spread, via, cut = buffers(k)
+        half = landing.shape[1] // 2
+        upper, lower = pl.ds(0, half), pl.ds(half, half)
+        away, front_column, back_column = (x + 2) % 4, (x + 1) % 4, (x + 3) % 4
+        over_via[k] = (
+            go(
+                landing.at[away, upper, cut], via.at[0, :, cut],
+                x_send.at[k, 0], x_recv.at[k, 0], column_ahead,
+            ),
+            go(
+                landing.at[away, lower, cut], via.at[1, :, cut],
+                x_send.at[k, 1], x_recv.at[k, 1], column_behind,
+            ),
+        )
         over_x[k] = [
             go(
-                landing.at[(x + spot + 1) % 4, :, cut],
-                spread.at[spot, :, cut],
-                x_send.at[k, spot],
-                x_recv.at[k, spot],
-                (me, others[spot]),
+                landing.at[front_column, lower, cut], spread.at[0, lower, cut],
+                x_send.at[k, 2], x_recv.at[k, 2], column_ahead,
+            ),
+            go(
+                landing.at[back_column, upper, cut], spread.at[1, upper, cut],
+                x_send.at[k, 3], x_recv.at[k, 3], column_behind,
+            ),
+        ]
+
+    def step_via(k):
+        landing, spread, via, cut = buffers(k)
+        half = landing.shape[1] // 2
+        upper, lower = pl.ds(0, half), pl.ds(half, half)
+        front_column, back_column = (x + 1) % 4, (x + 3) % 4
+        over_via[k][0].wait_recv()
+        landing[front_column, upper, cut] = landing[front_column, upper, cut] + via[0, :, cut]
+        over_x[k].append(
+            go(
+                landing.at[front_column, upper, cut], spread.at[0, upper, cut],
+                x_send.at[k, 4], x_recv.at[k, 4], column_ahead,
             )
-            for spot in (1, 0, 2)
-        ]
+        )
+        over_via[k][1].wait_recv()
+        landing[back_column, lower, cut] = landing[back_column, lower, cut] + via[1, :, cut]
+        over_x[k].append(
+            go(
+                landing.at[back_column, lower, cut], spread.at[1, lower, cut],
+                x_send.at[k, 5], x_recv.at[k, 5], column_behind,
+            )
+        )
 
     def step_x(k):
-        _, landing, spread, cut = buffers(k)
+        landing, spread, _, cut = buffers(k)
         for copy in over_x[k]:
             copy.wait_recv()
         total = landing[x, :, cut].astype(F32)
-        for spot in range(3):
+        for spot in range(2):
             total = total + spread[spot, :, cut].astype(F32)
         total = total.astype(BF)
         half = D // 2
-        if k == 0:
+        if k == WIDE:
             for piece in range(8):
                 packed[piece, :, half : half + 256] = total[:, piece * 256 : piece * 256 + 256]
         elif k == DOWN:
@@ -524,41 +574,51 @@
                     ]
         elif k == CROSS_KV or k == SELF_KV:
             for piece in range(2):
-                packed[(4 if k == CROSS_KV else 6) + piece, :, :half] = total[
+                packed[k + (0 if k == CROSS_KV else 1) + piece, :, :half] = total[
                     :, piece * half : piece * half + half
                 ]
         else:
-            packed[k - 1, :, :half] = total
-
+            packed[k, :, :half] = total
+
+    wide_copy = bring(wide_ref, from_z.at[:, :, pl.ds(starts[WIDE], FF)], local_sem.at[1])
+    down_copy = bring(down_ref, d_z, local_sem.at[2])
     s_copies = rows_start(dkv_ref, s_kept, s_core, s_sem)
     c_copies = rows_start(dckv_ref, c_kept, c_core, c_sem)
-    for index in range(6):
+    for index in range(4):
         acts_start(index)
     state_near = bring(state_ref, state_all.at[pl.ds(0, ENC)], local_sem.at[0])
     state_far = go(
         state_ref, state_all.at[pl.ds(ENC, ENC)], late_send.at[2], late_recv.at[2], sibling
     )
+    down_copy.wait()
+    send_x(DOWN)
+    wide_copy.wait()
+    send_x(WIDE)
     s_state = rows_send(s_copies, s_kept, s_core, s_via, s_row, s_sem)
     c_state = rows_send(c_copies, c_kept, c_core, c_via, c_row, c_sem)
-    make(0, 0)
+    make(0)
+    step_via(DOWN)
+    make(1)
     s_onward = rows_via(s_state, s_kept, s_via, s_row, s_sem)
-    make(1, DOWN)
+    make(2)
+    make(3)
+    step_via(WIDE)
     c_onward = rows_via(c_state, c_kept, c_via, c_row, c_sem)
-    for index in (2, 3, 4, 5):
-        make(index, index - 1)
-    step_z(0)
-    step_z(DOWN)
-    s_last = rows_across(s_onward, s_kept, s_row, s_stage, s_high, s_sem)
-    for k in (1, 2, 3, 4):
+    for k in range(4):
         step_z(k)
     state_near.wait()
     state_far.wait_recv()
     turned_state[...] = state_all[...].T.reshape(8, PIECE, 2 * ENC)
+    s_last = rows_across(s_onward, s_kept, s_row, s_stage, s_high, s_sem)
+    step_x(DOWN)
+    step_via(0)
     s_far = rows_sum(s_last, s_kept, s_row, s_high, s_fin, s_right, 0)
-    step_x(0)
+    step_via(1)
     s_far.wait_recv()
     multiply(SELF_KV, turned_one, s_right[...])
     c_last = rows_across(c_onward, c_kept, c_row, c_stage, c_high, c_sem)
+    step_via(2)
+    step_via(3)
     tokens = token_ref[...].astype(F32)
     d_kv = jnp.concatenate([s_fin[0], s_fin[1]], axis=1)
     grad = dn_ref[...] + contract(d_kv, kv_ref[...], ((1,), (1,)))
@@ -570,7 +630,7 @@
     sm_own[...] = small_f32[...].astype(BF)
     sm_over = go(sm_own, sm_core, sm_send.at[0], sm_recv.at[0], sibling)
     c_far = rows_sum(c_last, c_kept, c_row, c_high, c_fin, c_right, 1)
-    step_x(DOWN)
+    step_x(WIDE)
     c_far.wait_recv()
     multiply(CROSS_KV, turned_state, c_right[...])
     step_z(SELF_KV)
@@ -581,7 +641,7 @@
     sm_inside = go(
         sm_own.at[pl.ds(4 * (1 - low), 4)], sm_z, sm_send.at[1], sm_recv.at[1], inside
     )
-    for k in (1, 2, 3, 4):
+    for k in range(4):
         step_x(k)
     step_z(CROSS_KV)
     sm_inside.wait_recv()
@@ -594,6 +654,8 @@
         )
         for spot in range(3)
     ]
+    step_via(SELF_KV)
+    step_via(CROSS_KV)
     scaled = gain_ref[...] * grad
     mixed = jnp.mean(tokens * scaled, axis=-1, keepdims=True)
     decoder_ref[...] = (
@@ -651,6 +713,15 @@
         go(block, block, pass_send.at[spot], pass_recv.at[mate], sibling)
     for mate in [rank] + mates:
         landed(land.at[mate, 1 - core], pass_recv.at[mate])
+    land_out[...] = land[...]
+    for copy in sends:
+        if copy is not sm_over:
+            copy.wait_send()
+
+
+def unpack_kernel(land, *refs):
+    square_refs = refs[:8]
+    gate_ref, up_ref, down_ref = refs[8:]
     half = D // 2
     for side in range(2):
         for piece in range(4):
@@ -670,9 +741,22 @@
                     piece * 32 : piece * 32 + 32,
                     side * half + part * 128 : side * half + part * 128 + 128,
                 ] = land[piece, side, part * 32 : part * 32 + 32, half + 256 :].astype(F32)
-    for copy in sends:
-        if copy is not sm_over:
-            copy.wait_send()
+
+
+def unpack(land):
+    outs = (
+        [jax.ShapeDtypeStruct((PIECE, D), F32)] * 8
+        + [jax.ShapeDtypeStruct((PIECE, FF), F32)] * 2
+        + [jax.ShapeDtypeStruct((FF // 8, D), F32)]
+    )
+    return pl.pallas_call(
+        unpack_kernel,
+        out_shape=outs,
+        in_specs=[pl.BlockSpec(memory_space=pltpu.VMEM)],
+        out_specs=[pl.BlockSpec(memory_space=pltpu.VMEM)] * len(outs),
+        compiler_params=pltpu.CompilerParams(vmem_limit_bytes=24 * MIB),
+        name="unpack",
+    )(land)
 
 
 def finish(far, near, collective_id):
@@ -689,12 +773,12 @@
             pltpu.VMEM((2, count, D), BF),
         ]
 
-    outs = (
-        [jax.ShapeDtypeStruct((TOK, D), F32), jax.ShapeDtypeStruct((ENC, D), F32)]
-        + [jax.ShapeDtypeStruct((PIECE, D), F32)] * 8
-        + [jax.ShapeDtypeStruct((PIECE, FF), F32)] * 2
-        + [jax.ShapeDtypeStruct((FF // 8, D), F32), jax.ShapeDtypeStruct((16, 128), F32)]
-    )
+    outs = [
+        jax.ShapeDtypeStruct((8, 2, PIECE, ROOM), BF),
+        jax.ShapeDtypeStruct((16, 128), F32),
+        jax.ShapeDtypeStruct((TOK, D), F32),
+        jax.ShapeDtypeStruct((ENC, D), F32),
+    ]
     return pl.pallas_call(
         finish_kernel,
         out_shape=outs,
@@ -704,18 +788,19 @@
         scratch_shapes=[
             pltpu.VMEM((2 * TOK, sum(LEFT)), BF),
             pltpu.VMEM((2 * TOK, sum(RIGHT)), BF),
-            pltpu.VMEM((8, FF // 8, 2 * TOK), BF),
+            pltpu.VMEM((8, PIECE, 2 * TOK), BF),
             pltpu.VMEM((8, PIECE, 2 * TOK), BF),
             pltpu.VMEM((8, PIECE, 2 * ENC), BF),
             pltpu.VMEM((2 * ENC, D), BF),
             pltpu.VMEM((2 * TOK, D), BF),
             pltpu.VMEM((2 * ENC, D), BF),
-            pltpu.VMEM((8, PIECE, SPAN), BF),
+            pltpu.VMEM((8, PIECE, SPAN - FF), BF),
             pltpu.VMEM((4, PIECE, SPAN), BF),
-            pltpu.VMEM((3, PIECE, SPAN), BF),
-            pltpu.VMEM((8, FF // 8, D // 2), BF),
+            pltpu.VMEM((2, PIECE, SPAN), BF),
+            pltpu.VMEM((2, PIECE // 2, SPAN), BF),
             pltpu.VMEM((4, FF // 8, D // 2), BF),
-            pltpu.VMEM((3, FF // 8, D // 2), BF),
+            pltpu.VMEM((2, FF // 8, D // 2), BF),
+            pltpu.VMEM((2, FF // 16, D // 2), BF),
         ]
         + rows(TOK)
         + rows(ENC)
@@ -732,15 +817,15 @@
             pltpu.VMEM((8, 2, PIECE, ROOM), BF),
             dma((5, 7)),
             dma((5, 7)),
-            dma((6, 2)),
-            dma((6, 2)),
-            dma((6, 2)),
+            dma((4, 2)),
+            dma((4, 2)),
+            dma((4, 2)),
             dma((3,)),
             dma((3,)),
             dma((CHUNKS, 2)),
             dma((CHUNKS, 2)),
-            dma((CHUNKS, 3)),
-            dma((CHUNKS, 3)),
+            dma((CHUNKS, 6)),
+            dma((CHUNKS, 6)),
             dma((7,)),
             dma((7,)),
             dma((7,)),
@@ -749,7 +834,7 @@
             dma((8,)),
             dma((12,)),
             dma((12,)),
-            dma((1,)),
+            dma((3,)),
         ],
         compiler_params=pltpu.CompilerParams(
             collective_id=collective_id, has_side_effects=True, vmem_limit_bytes=62 * MIB
@@ -1025,6 +1110,44 @@
     return jnp.concatenate([sums[:, :-1], far], axis=1)
 
 
+def feed_gradients(normed, hidden, d_gate, d_up, upstream):
+    first = lax.axis_index("ctx") % 2 == 0
+    low = lax.axis_index("fsdp") // 4
+    half = D // 2
+
+    def swap(values, move):
+        perm = []
+        for ctx in range(N_CTX):
+            for shard in range(8):
+                there, owner = move(ctx, shard)
+                perm.append((ctx * 8 + shard, there * 8 + owner))
+        return lax.ppermute(values, ("ctx", "fsdp"), perm)
+
+    near = jnp.where(first, d_gate, d_up)
+    far = jnp.where(first, d_up, d_gate)
+    near_grad = jnp.where(first, upstream[:, :half], upstream[:, half:])
+    far_grad = jnp.where(first, upstream[:, half:], upstream[:, :half])
+    other = swap(
+        jnp.concatenate([normed, hidden, far, far_grad], axis=1), lambda ctx, shard: (ctx ^ 1, shard)
+    )
+    lefts = jnp.concatenate([normed, other[:, :D]], axis=0)
+    rights = jnp.concatenate([near, other[:, D + FF : D + 2 * FF]], axis=0)
+    wide = transposed_left(lefts, rights).astype(BF).reshape(8, PIECE, FF)
+    lefts = jnp.concatenate([hidden, other[:, D : D + FF]], axis=0)
+    rights = jnp.concatenate([near_grad, other[:, D + 2 * FF :]], axis=0)
+    tall = transposed_left(lefts, rights).astype(BF).reshape(8, FF // 8, half)
+
+    def over_z(part):
+        middle = part.shape[1] // 2
+        away = lax.dynamic_slice_in_dim(part, 4 * (1 - low), 4, 0)
+        mine = lax.dynamic_slice_in_dim(part, 4 * low, 4, 0)
+        inner = swap(away[:, :middle], lambda ctx, shard: (ctx, (shard + 4) % 8))
+        outer = swap(away[:, middle:], lambda ctx, shard: (ctx ^ 2, (shard + 4) % 8))
+        return mine + jnp.concatenate([inner, outer], axis=1)
+
+    return over_z(wide), over_z(tall)
+
+
 def body(
     decoder_in,
     encoder_states,
@@ -1112,7 +1235,9 @@
     block_out = mid_two + matmul(hidden, down)
 
     d_hidden = transposed_right(upstream, down)
-    d_gate_up = jnp.concatenate(pull_feed(d_hidden), axis=1).astype(BF)
+    d_gate, d_up = (part.astype(BF) for part in pull_feed(d_hidden))
+    d_gate_up = jnp.concatenate([d_gate, d_up], axis=1)
+    wide, tall = feed_gradients(normed_three, hidden, d_gate, d_up, upstream)
     d_normed_three = transposed_right(d_gate_up, gate_up)
     part_three, grad_norm_three = rms_back(mid_two, norm_three, d_normed_three)
     d_mid_two = upstream.astype(F32) + part_three
@@ -1141,8 +1266,9 @@
     )
     done = finish(
         [
-            normed_three, hidden, cross_attended, normed_two, attended, normed_one,
-            d_gate_up, upstream, cross_branch, d_cross_queries, self_branch, d_queries,
+            cross_attended, normed_two, attended, normed_one,
+            cross_branch, d_cross_queries, self_branch, d_queries,
+            wide, tall,
             d_kv_all.reshape(8, 2, 2, TOK, D),
             d_cross_kv_all.reshape(8, 2, 2, ENC, D),
         ],
@@ -1158,12 +1284,12 @@
         ],
         3,
     )
-    grad_decoder, grad_encoder = done[:2]
+    land, extras, grad_decoder, grad_encoder = done
     (
         grad_out_two, grad_query_two, grad_out_one, grad_query_one,
         grad_key_two, grad_value_two, grad_key_one, grad_value_one,
-        grad_gate, grad_up, grad_down, extras,
-    ) = done[2:]
+        grad_gate, grad_up, grad_down,
+    ) = unpack(land)
     return (
         block_out[None],
         grad_decoder[None],

time: 378 us -> 352 us (0.931)
  Pallas kernels: 308 us -> 263 us
  waiting for transfers between devices: 0 us -> 17 us
  local copies, waits for them, and re-layouts: 27.8 us -> 20.2 us
  starting transfers between devices: 0 us -> 5.03 us
    pallas_call x1, Pallas kernels: 130 us -> 94 us  [front(): pl.pallas_call(front_kernel, out_shape=[jax.ShapeDtypeStruct(pack, BF) fo...]
    ppermute x0 -> x5, waiting for transfers between devices: none -> 17 us  [swap(): return lax.ppermute(values, ('ctx', 'fsdp'), perm)]
    unnamed x81 -> x72, local copies, waits for them, and re-layouts: 18.2 us -> 7.14 us
    pallas_call x1, Pallas kernels: 140 us -> 130 us  [finish(): pl.pallas_call(finish_kernel, out_shape=outs, in_specs=[pl.BlockSpec(memo...]
    slice x0 -> x5, local copies, waits for them, and re-layouts: none -> 5.32 us  [the longest x2 2.21 us: over_z(): inner = swap(away[:, :middle], lambda ctx, shard: (ctx, (shard + 4) % 8))]
    add x0 -> x2, other arithmetic: none -> 5.32 us  [over_z(): return mine + jnp.concatenate([inner, outer], axis=1)]
    ppermute x0 -> x5, starting transfers between devices: none -> 5.03 us  [swap(): return lax.ppermute(values, ('ctx', 'fsdp'), perm)]
    dot_general x9 -> x11, matrix products: 15.6 us -> 15 us  [contract(): lax.dot_general(left, right, (dims, ((), ())), preferred_element_type=F32)]
  transfers between devices with their start and end apart: 0 -> 5, of which waited for: 0 -> 2; matrix products, arithmetic and copies ran while one was open for 0% -> 8% of each run, Pallas kernels for 0% -> 6%
where the time goes in v4:
time: 352 us; the launch traced here: 351 us
  Pallas kernels  263 us (75%)
  matrix products  25.8 us (7%)
  local copies, waits for them, and re-layouts  20.2 us (6%)
  other arithmetic  18.1 us (5%)
  waiting for transfers between devices  17 us (5%)
  starting transfers between devices  5.03 us (1%)
    pallas_call x1, Pallas kernels, finish(): pl.pallas_call(finish_kernel, out_shape=outs, in_specs=[pl.BlockSpec(memo...  130 us
    pallas_call x1, Pallas kernels, front(): pl.pallas_call(front_kernel, out_shape=[jax.ShapeDtypeStruct(pack, BF) fo...  94 us
    pallas_call x2, Pallas kernels, attend_back(): pl.pallas_call(functools.partial(backward_kernel, biased), grid=(PAIRS,),...  21.7 us
    ppermute x5, waiting for transfers between devices, swap(): return lax.ppermute(values, ('ctx', 'fsdp'), perm)  17 us
    pallas_call x2, Pallas kernels, attend(): pl.pallas_call(functools.partial(forward_kernel, biased), grid=(PAIRS,),...  15.9 us
    dot_general x11, matrix products, contract(): lax.dot_general(left, right, (dims, ((), ())), preferred_element_type=F32)  15 us
    dot_general x7, matrix products, matmul(): return jnp.dot(left, right, preferred_element_type=F32)  10.8 us
    unnamed x72, local copies, waits for them, and re-layouts  7.14 us
  transfers between devices with their start and end apart: 5, of which 2 were waited for; matrix products, arithmetic and copies ran while one was open for 8% of the time, Pallas kernels for 6%

profile of v4, /device:TPU:1, one launch (start us, length us, event | category | flops | bytes accessed | tf_op | source)
XLA Modules:
  0.0 351.4 jit_solution(18008058103935707431)
XLA Ops:
  1.5 1.3 fusion.61.refs_11_
  2.8 94.0 %front.1 = (bf16[8,96,1536]{2,1,0:T(8,128)(2,1)}, bf16[8,96,1536]{2,1,0:T(8,128)(2,1)}, bf16[8,96,3072]{2,1,0:T(8,128)(2,1)}, bf16[8,96,4096]{2,1,0:T(8,128)(2,1...) custom-call(bf16[96,768]{1,0:T(8,128)(2,1)} %refs_0_.1, ...), custom_call_target="tpu_custom_call" | custom-call | tf_op jit(solution)/shard_map/front/pallas_call | solution.py:266
  101.0 1.3 fusion.2
  102.3 1.2 copy-done.8
  106.1 10.0 %attend_self.1 = (bf16[128,768]{1,0:T(8,128)(2,1)S(1)}, f32[6,8,256]{2,1,0:T(8,128)S(1)}) custom-call(s32[2,32]{1,0:T(2,128)S(1)} %compare_select_fusion.1.refs_0_, bf16[128,768]{1,0:T(8,128)(2,1)S(1)} %copy-done.5, bf16[16,2,128,768]{3,2,1,0:T(8,128)(2,1)} %get-tuple-element.53.refs_2_.refs_3_.refs_4_, ...), custom_call_target="tpu_custom_call" | custom-call | flops 1000000000 | bytes 10000000 | tf_op jit(solution)/shard_map/attend_self/pallas_call | solution.py:997
  116.2 1.8 multiply_reduce_fusion.5
  118.1 1.7 convolution_convert_fusion.5.refs_0_
  119.9 5.9 %attend_cross.1 = (bf16[128,768]{1,0:T(8,128)(2,1)S(1)}, f32[6,8,256]{2,1,0:T(8,128)S(1)}) custom-call(bf16[128,768]{1,0:T(8,128)(2,1)S(1)} %convolution_convert_fusion.5.refs_0_, bf16[16,2,64,768]{3,2,1,0:T(8,128)(2,1)S(1)} %copy-done, bf16[16,2,64,768]{3,2,1,0:T(8,128)(2,1)S(1)} %copy-done), custom_call_target="tpu_custom_call" | custom-call | flops 1000000000 | bytes 10000000 | tf_op jit(solution)/shard_map/attend_cross/pallas_call | solution.py:997
  125.8 1.8 multiply_reduce_fusion.4
  130.3 2.4 broadcast_select_fusion.1
  134.0 1.5 collective-permute-start
  135.5 3.0 multiply_reduce_fusion
  140.0 2.0 convolution_convert_fusion.4.refs_3_
  142.0 8.3 %attend_cross_back.1 = (bf16[128,768]{1,0:T(8,128)(2,1)S(1)}, bf16[16,2,64,768]{3,2,1,0:T(8,128)(2,1)S(1)}) custom-call(bf16[128,768]{1,0:T(8,128)(2,1)S(1)} %convolution_convert_fusion.5.refs_0_, bf16[16,2,64,768]{3,2,1,0:T(8,128)(2,1)} %get-tuple-element.57.refs_1_.refs_2_, bf16[16,2,64,768]{3,2,1,0:T(8,128)(2,1)} %get-tuple-element.57.refs_1_.refs_2_, ...), custom_call_target="tpu_custom_call" | custom-call | flops 3000000000 | bytes 10000000 | tf_op jit(solution)/shard_map/attend_cross_back/pallas_call | solution.py:1034
  153.3 13.3 %attend_self_back.1 = (bf16[128,768]{1,0:T(8,128)(2,1)S(1)}, bf16[16,2,128,768]{3,2,1,0:T(8,128)(2,1)}, f32[12,3,64,128]{3,2,1,0:T(8,128)S(1)}) custom-call(s32[2,32]{1,0:T(2,128)S(1)} %compare_select_fusion.1.refs_0_, s32[2,3]{1,0:T(2,128)S(1)} %copy.48.refs_1_, bf16[128,768]{1,0:T(8,128)(2,1)S(1)} %copy-done.5, ...), custom_call_target="tpu_custom_call" | custom-call | flops 3000000000 | bytes 10000000 | tf_op jit(solution)/shard_map/attend_self_back/pallas_call | solution.py:1034
  166.6 1.4 slice_add_fusion
  168.0 1.7 reshape.198
  172.2 2.7 fusion.6.refs_15_
  175.8 1.3 fusion.81
  178.2 1.2 constant_dynamic-slice_fusion.1
  179.4 1.5 collective-permute-start.2
  184.7 2.1 collective-permute-start.4
  188.1 3.5 fusion.5
  191.6 15.7 %collective-permute-done.3 = bf16[4,128,384]{2,1,0:T(8,128)(2,1)} collective-permute-done((bf16[4,128,384]{2,1,0:T(8,128)(2,1)}, bf16[4,128,384]{2,1,0:T(8,128)(2,1)}, u32[]{:S(2)}, u32[]{:S(2)}) %collective-permute-start.3) | collective-permute-done | bytes 393248 | tf_op jit(solution)/shard_map/ppermute | solution.py:1124
  207.3 1.2 collective-permute-done.4
  208.6 2.2 maximum_add_fusion.1.refs_9_
  210.8 3.1 maximum_add_fusion.refs_8_
  213.9 129.6 %finish_gradients.1 = (bf16[8,2,96,768]{3,2,1,0:T(8,128)(2,1)}, f32[16,128]{1,0:T(8,128)}, f32[128,768]{1,0:T(8,128)}, f32[64,768]{1,0:T(8,128)}) custom-call(bf16[128,768]{1,0:T(8,128)(2,1)} %copy-done.3, bf16[128,768]{1,0:T(8,128)(2,1)} %copy-done.21, bf16[128,768]{1,0:T(8,128)(2,1)} %copy-done.6, bf16[128,768]{1,0:T(8,128)(2,1)} %get-tuple-element.61.refs_3_, ...), custom_call_target="tpu_custom_call" | custom-call | tf_op jit(solution)/shard_map/finish_gradients/pallas_call | solution.py:782
  343.5 1.3 slice_bitcast_fusion
  344.8 1.3 slice.122
  346.1 1.7 copy-done.2
  347.8 2.2 unpack.1
  (141 shorter events, 26.4 us)
Async XLA Ops:
  0.7 97.6 %copy-start.29 = (s32[16]{0:T(128)S(1)}, s32[16]{0:T(128)}, u32[]{:S(2)}) copy-start(s32[16]{0:T(128)} %param.23) | copy-start | bytes 196
  0.7 99.8 %copy-start.30 = (s32[128]{0:T(128)S(1)}, s32[128]{0:T(128)}, u32[]{:S(2)}) copy-start(s32[128]{0:T(128)} %param.24) | copy-start | bytes 1540
  105.2 22.5 %slice-start = ((s8[6291456]{0:T(1024)(128)(4,1)}), s8[4194304]{0:T(1024)(128)(4,1)S(1)}, s32[]{:S(2)}) async-start(s8[6291456]{0:T(1024)(128)(4,1)} %bitcast.72), calls=%async_computation | async-start | bytes 8388608
  106.1 10.1 %copy-start.23 = (bf16[1,128,768]{2,1,0:T(8,128)(2,1)S(1)}, bf16[1,128,768]{2,1,0:T(8,128)(2,1)}, u32[]{:S(2)}) copy-start(bf16[1,128,768]{2,1,0:T(8,128)(2,1)} %param.20) | copy-start | bytes 589828
  106.1 21.6 %slice-start.1 = ((s8[6291456]{0:T(1024)(128)(4,1)}), s8[2097152]{0:T(1024)(128)(4,1)S(1)}, s32[]{:S(2)}) async-start(s8[6291456]{0:T(1024)(128)(4,1)} %bitcast.72), calls=%async_computation.1 | async-start | bytes 4194304
  116.1 3.7 %copy-start.6 = (bf16[128,768]{1,0:T(8,128)(2,1)}, bf16[128,768]{1,0:T(8,128)(2,1)S(1)}, u32[]{:S(2)}) copy-start(bf16[128,768]{1,0:T(8,128)(2,1)S(1)} %get-tuple-element.55.refs_2_) | copy-start | bytes 589828
  116.1 3.7 %copy-start = (bf16[16,2,64,768]{3,2,1,0:T(8,128)(2,1)S(1)}, bf16[16,2,64,768]{3,2,1,0:T(8,128)(2,1)}, u32[]{:S(2)}) copy-start(bf16[16,2,64,768]{3,2,1,0:T(8,128)(2,1)} %get-tuple-element.57.refs_1_.refs_2_) | copy-start | bytes 9437188
  118.0 7.8 %copy-start.14 = (f32[128,768]{1,0:T(8,128)}, f32[128,768]{1,0:T(8,128)S(1)}, u32[]{:S(2)}) copy-start(f32[128,768]{1,0:T(8,128)S(1)} %get-tuple-element.112) | copy-start | bytes 1179652
  125.8 3.0 copy-start.3
  127.7 5.1 %copy-start.12 = (bf16[128,768]{1,0:T(8,128)(2,1)}, bf16[128,768]{1,0:T(8,128)(2,1)S(1)}, u32[]{:S(2)}) copy-start(bf16[128,768]{1,0:T(8,128)(2,1)S(1)} %multiply_convert_fusion.2) | copy-start | bytes 589828
  127.7 2.6 copy-start.16
  129.1 3.7 %copy-start.10 = (bf16[128,2048]{1,0:T(8,128)(2,1)}, bf16[128,2048]{1,0:T(8,128)(2,1)S(1)}, u32[]{:S(2)}) copy-start(bf16[128,2048]{1,0:T(8,128)(2,1)S(1)} %multiply_convert_fusion.1) | copy-start | bytes 1572868
  134.0 40.9 %collective-permute-start = (bf16[128,5248]{1,0:T(8,128)(2,1)}, bf16[128,5248]{1,0:T(8,128)(2,1)}, u32[]{:S(2)}, u32[]{:S(2)}) collective-permute-start(bf16[128,5248]{1,0:T(8,128)(2,1)} %pad_maximum_fusion), channel_id=1, source_target_pairs={{0,8},{1,9},{2,10},{3,11},{4,12},{5,13},{6,14},{7,15},{8,0},{9,1},... | collective-permute-start | bytes 4030472 | tf_op jit(solution)/shard_map/ppermute | solution.py:1124
  139.9 2.0 copy-start.22
  140.0 10.4 %slice-start.2 = ((s8[4718592]{0:T(1024)(128)(4,1)}), s8[4194304]{0:T(1024)(128)(4,1)S(1)}, s32[]{:S(2)}) async-start(s8[4718592]{0:T(1024)(128)(4,1)} %bitcast.89), calls=%async_computation.2 | async-start | bytes 8388608
  141.9 8.4 %copy-start.15 = (f32[128,768]{1,0:T(8,128)S(1)}, f32[128,768]{1,0:T(8,128)}, u32[]{:S(2)}) copy-start(f32[128,768]{1,0:T(8,128)} %copy-done.14) | copy-start | bytes 1179652
  142.0 8.4 %slice-start.3 = ((s8[4718592]{0:T(1024)(128)(4,1)}), s8[524288]{0:T(1024)(128)(4,1)S(1)}, s32[]{:S(2)}) async-start(s8[4718592]{0:T(1024)(128)(4,1)} %bitcast.89), calls=%async_computation.3 | async-start | bytes 1048576
  150.3 2.3 copy-start.1
  150.3 2.3 copy-start.7
  166.6 5.6 %copy-start.4 = (bf16[128,768]{1,0:T(8,128)(2,1)}, bf16[128,768]{1,0:T(8,128)(2,1)S(1)}, u32[]{:S(2)}) copy-start(bf16[128,768]{1,0:T(8,128)(2,1)S(1)} %get-tuple-element.65.refs_7_) | copy-start | bytes 589828
  166.6 3.1 copy-start.9
  172.2 4.9 %copy-start.13 = (bf16[128,768]{1,0:T(8,128)(2,1)S(1)}, bf16[128,768]{1,0:T(8,128)(2,1)}, u32[]{:S(2)}) copy-start(bf16[128,768]{1,0:T(8,128)(2,1)} %copy-done.12) | copy-start | bytes 589828
  172.2 4.9 %copy-start.25 = (bf16[128,2048]{1,0:T(8,128)(2,1)S(1)}, bf16[128,2048]{1,0:T(8,128)(2,1)}, u32[]{:S(2)}) copy-start(bf16[128,2048]{1,0:T(8,128)(2,1)} %get-tuple-element.95) | copy-start | bytes 1572868
  178.1 3.6 %copy-start.11 = (bf16[128,2048]{1,0:T(8,128)(2,1)S(1)}, bf16[128,2048]{1,0:T(8,128)(2,1)}, u32[]{:S(2)}) copy-start(bf16[128,2048]{1,0:T(8,128)(2,1)} %copy-done.10) | copy-start | bytes 1572868
  178.2 3.6 %copy-start.28 = (bf16[128,384]{1,0:T(8,128)(2,1)S(1)}, bf16[128,384]{1,0:T(8,128)(2,1)}, u32[]{:S(2)}) copy-start(bf16[128,384]{1,0:T(8,128)(2,1)} %get-tuple-element.106) | copy-start | bytes 294916
  179.4 31.3 %collective-permute-start.1 = (bf16[4,48,2048]{2,1,0:T(8,128)(2,1)}, bf16[4,48,2048]{2,1,0:T(8,128)(2,1)}, u32[]{:S(2)}, u32[]{:S(2)}) collective-permute-start(bf16[4,48,2048]{2,1,0:T(8,128)(2,1)} %get-tuple-element.100), channel_id=1, source_target_pairs={{0,4},{1,5},{2,6},{3,7},{4,0},{5,1},{6,2},{7,3},{8,12},{9,13},{10,... | collective-permute-start | bytes 2359304 | tf_op jit(solution)/shard_map/ppermute | solution.py:1124
  179.4 31.3 %collective-permute-start.2 = (bf16[4,48,2048]{2,1,0:T(8,128)(2,1)}, bf16[4,48,2048]{2,1,0:T(8,128)(2,1)}, u32[]{:S(2)}, u32[]{:S(2)}) collective-permute-start(bf16[4,48,2048]{2,1,0:T(8,128)(2,1)} %get-tuple-element.101), channel_id=1, source_target_pairs={{0,20},{1,21},{2,22},{3,23},{4,16},{5,17},{6,18},{7,19},{8,28},{9,... | collective-permute-start | bytes 2359304 | tf_op jit(solution)/shard_map/ppermute | solution.py:1124
  184.7 22.7 %collective-permute-start.3 = (bf16[4,128,384]{2,1,0:T(8,128)(2,1)}, bf16[4,128,384]{2,1,0:T(8,128)(2,1)}, u32[]{:S(2)}, u32[]{:S(2)}) collective-permute-start(bf16[4,128,384]{2,1,0:T(8,128)(2,1)} %get-tuple-element.102), channel_id=1, source_target_pairs={{0,4},{1,5},{2,6},{3,7},{4,0},{5,1},{6,2},{7,3},{8,12},{9,13},{10,... | collective-permute-start | bytes 1179656 | tf_op jit(solution)/shard_map/ppermute | solution.py:1124
  184.7 23.9 %collective-permute-start.4 = (bf16[4,128,384]{2,1,0:T(8,128)(2,1)}, bf16[4,128,384]{2,1,0:T(8,128)(2,1)}, u32[]{:S(2)}, u32[]{:S(2)}) collective-permute-start(bf16[4,128,384]{2,1,0:T(8,128)(2,1)} %get-tuple-element.103), channel_id=1, source_target_pairs={{0,20},{1,21},{2,22},{3,23},{4,16},{5,17},{6,18},{7,19},{8,28},{9,... | collective-permute-start | bytes 1179656 | tf_op jit(solution)/shard_map/ppermute | solution.py:1124
  188.1 20.5 %copy-start.19 = (bf16[2048,384]{1,0:T(8,128)(2,1)S(1)}, bf16[2048,384]{1,0:T(8,128)(2,1)}, u32[]{:S(2)}) copy-start(bf16[2048,384]{1,0:T(8,128)(2,1)} %copy-done.18) | copy-start | bytes 4718596
  347.8 2.2 copy-start.26
  347.8 3.0 copy-start.27
  (8 other events, 9.6 us)

commit v5 on v4

--- a/solution.py
+++ b/solution.py
@@ -300,7 +300,6 @@
 
 
 PIECE = 96
-ROOM = D // 2 + FF // 8 + FF // 16
 WIDTHS = (D // 2, D // 2, D // 2, D // 2, D, D, FF)
 SPAN = sum(WIDTHS)
 DOWN = len(WIDTHS)
@@ -315,17 +314,17 @@
     rights = refs[4:8]
     wide_ref, down_ref, dkv_ref, dckv_ref = refs[8:12]
     state_ref, kv_ref, ckv_ref, dn_ref, dmid_ref, token_ref, gain_ref, small_ref = refs[12:20]
-    land_out, small_out, decoder_ref, encoder_ref = refs[20:24]
+    early_out, late_out, small_out, decoder_ref, encoder_ref = refs[20:25]
     (
         left_all, right_all, turned, turned_one, turned_state, state_all, s_right, c_right,
         kept, from_z, from_x, via_x, d_z, d_x, d_via,
         s_kept, s_core, s_row, s_via, s_stage, s_high, s_fin,
         c_kept, c_core, c_row, c_via, c_stage, c_high, c_fin,
-        small_f32, sm_own, sm_core, sm_z, sm_x, sm_ctx, sm_total, packed, from_ctx, land,
+        small_f32, sm_own, sm_core, sm_z, sm_x, sm_ctx, sm_total,
+        packed, from_ctx, land, late_packed, late_from, late_land,
         s_sem, c_sem, fill_sem, act_send, act_recv, late_send, late_recv, z_send, z_recv,
-        x_send, x_recv, ctx_send, ctx_recv, out_send, out_recv, pass_send, pass_recv,
-        sm_send, sm_recv, local_sem,
-    ) = refs[24:]
+        x_send, x_recv, ctx_send, ctx_recv, pass_send, pass_recv, sm_send, sm_recv, local_sem,
+    ) = refs[25:]
     me, core, high, y, low, x = torus_place()
     shard = low * 4 + x
     rank = y * 2 + high
@@ -565,20 +564,61 @@
         half = D // 2
         if k == WIDE:
             for piece in range(8):
-                packed[piece, :, half : half + 256] = total[:, piece * 256 : piece * 256 + 256]
+                packed[piece, :PIECE, :256] = total[:, piece * 256 : piece * 256 + 256]
         elif k == DOWN:
             for piece in range(8):
                 for part in range(3):
-                    packed[piece, part * 32 : part * 32 + 32, half + 256 :] = total[
+                    packed[piece, part * 32 : part * 32 + 32, 256:] = total[
                         piece * 32 : piece * 32 + 32, part * 128 : part * 128 + 128
                     ]
-        elif k == CROSS_KV or k == SELF_KV:
-            for piece in range(2):
-                packed[k + (0 if k == CROSS_KV else 1) + piece, :, :half] = total[
-                    :, piece * half : piece * half + half
-                ]
         else:
-            packed[k, :, :half] = total
+            middle = PIECE // 2
+            for upper in range(2):
+                rows = total[upper * middle : upper * middle + middle, :]
+                if k == CROSS_KV or k == SELF_KV:
+                    for piece in range(2):
+                        late_packed[(0 if k == CROSS_KV else 4) + 2 * piece + upper] = rows[
+                            :, piece * half : piece * half + half
+                        ]
+                else:
+                    packed[2 * k + upper, PIECE:, :] = rows
+
+
+    def mate_device(mate):
+        return (mate * 2 + core, shard)
+
+    def ctx_start(which, source, landing):
+        return [
+            go(
+                source.at[mate], landing.at[spot],
+                ctx_send.at[which, spot], ctx_recv.at[which, spot], mate_device(mate),
+            )
+            for spot, mate in enumerate(mates)
+        ]
+
+    def ctx_sum(which, over, source, landing, final):
+        total = source[rank].astype(F32)
+        for spot in range(7):
+            over[spot].wait_recv()
+            total = total + landing[spot].astype(F32)
+        final[rank, core] = total.astype(BF)
+        own = final.at[rank, core]
+        for spot, mate in enumerate(mates):
+            go(own, own, ctx_send.at[which, 7 + spot], ctx_recv.at[which, 7 + rank], mate_device(mate))
+        go(own, own, pass_send.at[which, 7], pass_recv.at[which, rank], sibling)
+
+    def landed(ref, recv_sem):
+        hop(ref, ref, pass_send.at[0, 0], recv_sem, *sibling).wait_recv()
+
+    def ctx_pass(which, final):
+        for spot, mate in enumerate(mates):
+            block = final.at[mate, core]
+            landed(block, ctx_recv.at[which, 7 + mate])
+            go(block, block, pass_send.at[which, spot], pass_recv.at[which, mate], sibling)
+
+    def ctx_done(which, final):
+        for mate in [rank] + mates:
+            landed(final.at[mate, 1 - core], pass_recv.at[which, mate])
 
     wide_copy = bring(wide_ref, from_z.at[:, :, pl.ds(starts[WIDE], FF)], local_sem.at[1])
     down_copy = bring(down_ref, d_z, local_sem.at[2])
@@ -595,30 +635,32 @@
     wide_copy.wait()
     send_x(WIDE)
     s_state = rows_send(s_copies, s_kept, s_core, s_via, s_row, s_sem)
-    c_state = rows_send(c_copies, c_kept, c_core, c_via, c_row, c_sem)
     make(0)
-    step_via(DOWN)
     make(1)
     s_onward = rows_via(s_state, s_kept, s_via, s_row, s_sem)
+    c_state = rows_send(c_copies, c_kept, c_core, c_via, c_row, c_sem)
     make(2)
     make(3)
+    step_via(DOWN)
     step_via(WIDE)
-    c_onward = rows_via(c_state, c_kept, c_via, c_row, c_sem)
     for k in range(4):
         step_z(k)
     state_near.wait()
     state_far.wait_recv()
     turned_state[...] = state_all[...].T.reshape(8, PIECE, 2 * ENC)
     s_last = rows_across(s_onward, s_kept, s_row, s_stage, s_high, s_sem)
+    c_onward = rows_via(c_state, c_kept, c_via, c_row, c_sem)
+    for k in range(4):
+        step_via(k)
     step_x(DOWN)
-    step_via(0)
+    step_x(WIDE)
     s_far = rows_sum(s_last, s_kept, s_row, s_high, s_fin, s_right, 0)
-    step_via(1)
+    for k in range(4):
+        step_x(k)
+    early = ctx_start(0, packed, from_ctx)
     s_far.wait_recv()
     multiply(SELF_KV, turned_one, s_right[...])
     c_last = rows_across(c_onward, c_kept, c_row, c_stage, c_high, c_sem)
-    step_via(2)
-    step_via(3)
     tokens = token_ref[...].astype(F32)
     d_kv = jnp.concatenate([s_fin[0], s_fin[1]], axis=1)
     grad = dn_ref[...] + contract(d_kv, kv_ref[...], ((1,), (1,)))
@@ -630,7 +672,6 @@
     sm_own[...] = small_f32[...].astype(BF)
     sm_over = go(sm_own, sm_core, sm_send.at[0], sm_recv.at[0], sibling)
     c_far = rows_sum(c_last, c_kept, c_row, c_high, c_fin, c_right, 1)
-    step_x(WIDE)
     c_far.wait_recv()
     multiply(CROSS_KV, turned_state, c_right[...])
     step_z(SELF_KV)
@@ -641,9 +682,9 @@
     sm_inside = go(
         sm_own.at[pl.ds(4 * (1 - low), 4)], sm_z, sm_send.at[1], sm_recv.at[1], inside
     )
-    for k in range(4):
-        step_x(k)
+    ctx_sum(0, early, packed, from_ctx, land)
     step_z(CROSS_KV)
+    step_via(SELF_KV)
     sm_inside.wait_recv()
     for column in range(4):
         sm_z[column] = sm_z[column] + sm_own[4 * low + column]
@@ -654,96 +695,70 @@
         )
         for spot in range(3)
     ]
-    step_via(SELF_KV)
     step_via(CROSS_KV)
     scaled = gain_ref[...] * grad
     mixed = jnp.mean(tokens * scaled, axis=-1, keepdims=True)
     decoder_ref[...] = (
         dmid_ref[...] + inverse * scaled - tokens * (inverse * inverse * inverse * mixed)
     )
-    d_ckv = jnp.concatenate([c_fin[0], c_fin[1]], axis=1)
-    encoder_ref[...] = contract(d_ckv, ckv_ref[...], ((1,), (1,)))
     step_x(SELF_KV)
     step_x(CROSS_KV)
-
-
-    over_ctx = [
-        go(
-            packed.at[mate],
-            from_ctx.at[spot],
-            ctx_send.at[spot],
-            ctx_recv.at[spot],
-            (mate * 2 + core, shard),
-        )
-        for spot, mate in enumerate(mates)
-    ]
+    late = ctx_start(1, late_packed, late_from)
     sm_sum = sm_z[x].astype(F32)
     for spot in range(3):
         sm_row[spot].wait_recv()
         sm_sum = sm_sum + sm_x[spot].astype(F32)
     sm_total[...] = sm_sum.astype(BF)
     sm_mates = [
-        go(
-            sm_total, sm_ctx.at[spot],
-            sm_send.at[5 + spot], sm_recv.at[5 + spot], (mate * 2 + core, shard),
-        )
+        go(sm_total, sm_ctx.at[spot], sm_send.at[5 + spot], sm_recv.at[5 + spot], mate_device(mate))
         for spot, mate in enumerate(mates)
     ]
-    total = packed[rank].astype(F32)
-    for spot in range(7):
-        over_ctx[spot].wait_recv()
-        total = total + from_ctx[spot].astype(F32)
-    land[rank, core] = total.astype(BF)
-    own = land.at[rank, core]
-    for spot, mate in enumerate(mates):
-        go(own, own, out_send.at[spot], out_recv.at[rank], (mate * 2 + core, shard))
-    go(own, own, pass_send.at[7], pass_recv.at[rank], sibling)
-
-    def landed(ref, recv_sem):
-        hop(ref, ref, pass_send.at[0], recv_sem, *sibling).wait_recv()
-
+    ctx_pass(0, land)
+    ctx_sum(1, late, late_packed, late_from, late_land)
+    d_ckv = jnp.concatenate([c_fin[0], c_fin[1]], axis=1)
+    encoder_ref[...] = contract(d_ckv, ckv_ref[...], ((1,), (1,)))
     sm_sum = sm_total[...].astype(F32)
     for spot in range(7):
         sm_mates[spot].wait_recv()
         sm_sum = sm_sum + sm_ctx[spot].astype(F32)
     small_out[...] = sm_sum
-    for spot, mate in enumerate(mates):
-        block = land.at[mate, core]
-        landed(block, out_recv.at[mate])
-        go(block, block, pass_send.at[spot], pass_recv.at[mate], sibling)
-    for mate in [rank] + mates:
-        landed(land.at[mate, 1 - core], pass_recv.at[mate])
-    land_out[...] = land[...]
+    ctx_done(0, land)
+    early_out[...] = land[...]
+    ctx_pass(1, late_land)
+    ctx_done(1, late_land)
+    late_out[...] = late_land[...]
     for copy in sends:
         if copy is not sm_over:
             copy.wait_send()
 
 
-def unpack_kernel(land, *refs):
+def unpack_kernel(early, late, *refs):
     square_refs = refs[:8]
     gate_ref, up_ref, down_ref = refs[8:]
     half = D // 2
+    middle = PIECE // 2
     for side in range(2):
-        for piece in range(4):
-            square_refs[piece][:, side * half : side * half + half] = land[
-                piece, side, :, :half
-            ].astype(F32)
-            square_refs[4 + 2 * (piece // 2) + side][
-                :, (piece % 2) * half : (piece % 2) * half + half
-            ] = land[4 + piece, side, :, :half].astype(F32)
+        columns = slice(side * half, side * half + half)
+        for upper in range(2):
+            rows = slice(upper * middle, upper * middle + middle)
+            for k in range(4):
+                square_refs[k][rows, columns] = early[2 * k + upper, side, PIECE:, :].astype(F32)
+            for k in range(2):
+                for piece in range(2):
+                    square_refs[4 + 2 * k + side][rows, piece * half : piece * half + half] = late[
+                        4 * k + 2 * piece + upper, side
+                    ].astype(F32)
         target = up_ref if side else gate_ref
         for piece in range(8):
-            target[:, piece * 256 : piece * 256 + 256] = land[
-                piece, side, :, half : half + 256
-            ].astype(F32)
+            target[:, piece * 256 : piece * 256 + 256] = early[piece, side, :PIECE, :256].astype(F32)
             for part in range(3):
                 down_ref[
                     piece * 32 : piece * 32 + 32,
                     side * half + part * 128 : side * half + part * 128 + 128,
-                ] = land[piece, side, part * 32 : part * 32 + 32, half + 256 :].astype(F32)
-
-
-def unpack(land):
+                ] = early[piece, side, part * 32 : part * 32 + 32, 256:].astype(F32)
+
+
+def unpack(early, late):
     outs = (
         [jax.ShapeDtypeStruct((PIECE, D), F32)] * 8
         + [jax.ShapeDtypeStruct((PIECE, FF), F32)] * 2
@@ -752,11 +767,11 @@
     return pl.pallas_call(
         unpack_kernel,
         out_shape=outs,
-        in_specs=[pl.BlockSpec(memory_space=pltpu.VMEM)],
+        in_specs=[pl.BlockSpec(memory_space=pltpu.VMEM)] * 2,
         out_specs=[pl.BlockSpec(memory_space=pltpu.VMEM)] * len(outs),
         compiler_params=pltpu.CompilerParams(vmem_limit_bytes=24 * MIB),
         name="unpack",
-    )(land)
+    )(early, late)
 
 
 def finish(far, near, collective_id):
@@ -774,7 +789,8 @@
         ]
 
     outs = [
-        jax.ShapeDtypeStruct((8, 2, PIECE, ROOM), BF),
+        jax.ShapeDtypeStruct((8, 2, 3 * PIECE // 2, D // 2), BF),
+        jax.ShapeDtypeStruct((8, 2, PIECE // 2, D // 2), BF),
         jax.ShapeDtypeStruct((16, 128), F32),
         jax.ShapeDtypeStruct((TOK, D), F32),
         jax.ShapeDtypeStruct((ENC, D), F32),
@@ -812,9 +828,12 @@
             pltpu.VMEM((3, 16, 128), BF),
             pltpu.VMEM((7, 16, 128), BF),
             pltpu.VMEM((16, 128), BF),
-            pltpu.VMEM((8, PIECE, ROOM), BF),
-            pltpu.VMEM((7, PIECE, ROOM), BF),
-            pltpu.VMEM((8, 2, PIECE, ROOM), BF),
+            pltpu.VMEM((8, 3 * PIECE // 2, D // 2), BF),
+            pltpu.VMEM((7, 3 * PIECE // 2, D // 2), BF),
+            pltpu.VMEM((8, 2, 3 * PIECE // 2, D // 2), BF),
+            pltpu.VMEM((8, PIECE // 2, D // 2), BF),
+            pltpu.VMEM((7, PIECE // 2, D // 2), BF),
+            pltpu.VMEM((8, 2, PIECE // 2, D // 2), BF),
             dma((5, 7)),
             dma((5, 7)),
             dma((4, 2)),
@@ -826,12 +845,10 @@
             dma((CHUNKS, 2)),
             dma((CHUNKS, 6)),
             dma((CHUNKS, 6)),
-            dma((7,)),
-            dma((7,)),
-            dma((7,)),
-            dma((8,)),
-            dma((8,)),
-            dma((8,)),
+            dma((2, 14)),
+            dma((2, 15)),
+            dma((2, 8)),
+            dma((2, 8)),
             dma((12,)),
             dma((12,)),
             dma((3,)),
@@ -1044,7 +1061,7 @@
             pltpu.VMEM((chunks, TOK, 2 * TOK), BF),
         ],
         compiler_params=LOCAL,
-        cost_estimate=pl.CostEstimate(flops=3 * 10**9, bytes_accessed=10**7, transcendentals=10**6),
+        cost_estimate=pl.CostEstimate(flops=1000, bytes_accessed=1000, transcendentals=0),
         name="attend_self_back" if biased else "attend_cross_back",
     )(*operands)
 
@@ -1110,19 +1127,19 @@
     return jnp.concatenate([sums[:, :-1], far], axis=1)
 
 
+def swap(values, move):
+    perm = []
+    for ctx in range(N_CTX):
+        for shard in range(8):
+            there, owner = move(ctx, shard)
+            perm.append((ctx * 8 + shard, there * 8 + owner))
+    return lax.ppermute(values, ("ctx", "fsdp"), perm)
+
+
 def feed_gradients(normed, hidden, d_gate, d_up, upstream):
     first = lax.axis_index("ctx") % 2 == 0
     low = lax.axis_index("fsdp") // 4
     half = D // 2
-
-    def swap(values, move):
-        perm = []
-        for ctx in range(N_CTX):
-            for shard in range(8):
-                there, owner = move(ctx, shard)
-                perm.append((ctx * 8 + shard, there * 8 + owner))
-        return lax.ppermute(values, ("ctx", "fsdp"), perm)
-
     near = jnp.where(first, d_gate, d_up)
     far = jnp.where(first, d_up, d_gate)
     near_grad = jnp.where(first, upstream[:, :half], upstream[:, half:])
@@ -1137,15 +1154,19 @@
     rights = jnp.concatenate([near_grad, other[:, D + 2 * FF :]], axis=0)
     tall = transposed_left(lefts, rights).astype(BF).reshape(8, FF // 8, half)
 
-    def over_z(part):
+    def cut(part):
         middle = part.shape[1] // 2
         away = lax.dynamic_slice_in_dim(part, 4 * (1 - low), 4, 0)
         mine = lax.dynamic_slice_in_dim(part, 4 * low, 4, 0)
-        inner = swap(away[:, :middle], lambda ctx, shard: (ctx, (shard + 4) % 8))
-        outer = swap(away[:, middle:], lambda ctx, shard: (ctx ^ 2, (shard + 4) % 8))
-        return mine + jnp.concatenate([inner, outer], axis=1)
-
-    return over_z(wide), over_z(tall)
+        return mine, away[:, :middle], away[:, middle:]
+
+    return cut(wide), cut(tall)
+
+
+def over_z(mine, upper, lower):
+    inner = swap(upper, lambda ctx, shard: (ctx, (shard + 4) % 8))
+    outer = swap(lower, lambda ctx, shard: (ctx ^ 2, (shard + 4) % 8))
+    return mine, inner, outer
 
 
 def body(
@@ -1237,12 +1258,14 @@
     d_hidden = transposed_right(upstream, down)
     d_gate, d_up = (part.astype(BF) for part in pull_feed(d_hidden))
     d_gate_up = jnp.concatenate([d_gate, d_up], axis=1)
-    wide, tall = feed_gradients(normed_three, hidden, d_gate, d_up, upstream)
+    feed_parts = feed_gradients(normed_three, hidden, d_gate, d_up, upstream)
     d_normed_three = transposed_right(d_gate_up, gate_up)
     part_three, grad_norm_three = rms_back(mid_two, norm_three, d_normed_three)
     d_mid_two = upstream.astype(F32) + part_three
     cross_branch = d_mid_two.astype(BF)
     d_cross_attended = transposed_right(cross_branch, out_two).astype(BF)
+    feed_parts, d_cross_attended = lax.optimization_barrier((feed_parts, d_cross_attended))
+    feed_parts = [over_z(*parts) for parts in feed_parts]
     d_cross_queries, d_cross_kv_all = attend_back(
         cross_queries, cross_kv, d_cross_attended, cross_totals, ENC, 0
     )
@@ -1251,8 +1274,15 @@
     d_mid_one = d_mid_two + part_two
     self_branch = d_mid_one.astype(BF)
     d_attended = transposed_right(self_branch, out_one).astype(BF)
+    feed_parts[1], d_attended = lax.optimization_barrier((feed_parts[1], d_attended))
     d_queries, d_kv_all, strips = attend_back(
         queries, self_kv, d_attended, self_totals, TOK, 0, classes, near, tiles
+    )
+    feed_parts, d_queries, d_kv_all, strips = lax.optimization_barrier(
+        (feed_parts, d_queries, d_kv_all, strips)
+    )
+    wide, tall = (
+        mine + jnp.concatenate([inner, outer], axis=1) for mine, inner, outer in feed_parts
     )
     grad_table = matmul(bias_sums(strips), bucket_hot.astype(F32)).T.reshape(8, 4, HEADS)
     grad_gains = jnp.stack([grad_norm_two, grad_norm_three]).reshape(2, 8, rows)
@@ -1284,12 +1314,12 @@
         ],
         3,
     )
-    land, extras, grad_decoder, grad_encoder = done
+    early, late, extras, grad_decoder, grad_encoder = done
     (
         grad_out_two, grad_query_two, grad_out_one, grad_query_one,
         grad_key_two, grad_value_two, grad_key_one, grad_value_one,
         grad_gate, grad_up, grad_down,
-    ) = unpack(land)
+    ) = unpack(early, late)
     return (
         block_out[None],
         grad_decoder[None],

time: 352 us -> 339 us (0.963)
  Pallas kernels: 263 us -> 253 us
  waiting for transfers between devices: 17 us -> 9.01 us
  matrix products: 25.8 us -> 30.8 us
    pallas_call x1, Pallas kernels: 130 us -> 118 us  [finish(): pl.pallas_call(finish_kernel, out_shape=outs, in_specs=[pl.BlockSpec(memo...]
    ppermute x5, waiting for transfers between devices: 17 us -> 9.01 us  [swap(): return lax.ppermute(values, ('ctx', 'fsdp'), perm)]
    dot_general x11, matrix products: 15 us -> 20.1 us  [contract(): lax.dot_general(left, right, (dims, ((), ())), preferred_element_type=F32)]
    unnamed x72 -> x74, local copies, waits for them, and re-layouts: 7.14 us -> 6.08 us
  transfers between devices with their start and end apart: 5 -> 5, of which waited for: 2 -> 4; matrix products, arithmetic and copies ran while one was open for 8% -> 4% of each run, Pallas kernels for 6% -> 4%
where the time goes in v5:
time: 339 us; the launch traced here: 338 us
  Pallas kernels  253 us (75%)
  matrix products  30.8 us (9%)
  local copies, waits for them, and re-layouts  21.5 us (6%)
  other arithmetic  16.7 us (5%)
  waiting for transfers between devices  9.01 us (3%)
  starting transfers between devices  5.1 us (2%)
    pallas_call x1, Pallas kernels, finish(): pl.pallas_call(finish_kernel, out_shape=outs, in_specs=[pl.BlockSpec(memo...  118 us
    pallas_call x1, Pallas kernels, front(): pl.pallas_call(front_kernel, out_shape=[jax.ShapeDtypeStruct(pack, BF) fo...  93.9 us
    pallas_call x2, Pallas kernels, attend_back(): pl.pallas_call(functools.partial(backward_kernel, biased), grid=(PAIRS,),...  21.9 us
    dot_general x11, matrix products, contract(): lax.dot_general(left, right, (dims, ((), ())), preferred_element_type=F32)  20.1 us
    pallas_call x2, Pallas kernels, attend(): pl.pallas_call(functools.partial(forward_kernel, biased), grid=(PAIRS,),...  16.6 us
    dot_general x7, matrix products, matmul(): return jnp.dot(left, right, preferred_element_type=F32)  10.7 us
    ppermute x5, waiting for transfers between devices, swap(): return lax.ppermute(values, ('ctx', 'fsdp'), perm)  9.01 us
  transfers between devices with their start and end apart: 5, of which 4 were waited for; matrix products, arithmetic and copies ran while one was open for 4% of the time, Pallas kernels for 4%

profile of v5, /device:TPU:1, one launch (start us, length us, event | category | flops | bytes accessed | tf_op | source)
XLA Modules:
  0.0 338.1 jit_solution(16733083485445080047)
XLA Ops:
  2.8 93.9 %front.1 = (bf16[8,96,1536]{2,1,0:T(8,128)(2,1)}, bf16[8,96,1536]{2,1,0:T(8,128)(2,1)}, bf16[8,96,3072]{2,1,0:T(8,128)(2,1)}, bf16[8,96,4096]{2,1,0:T(8,128)(2,1...) custom-call(bf16[96,768]{1,0:T(8,128)(2,1)} %refs_0_.1, ...), custom_call_target="tpu_custom_call" | custom-call | tf_op jit(solution)/shard_map/front/pallas_call | solution.py:266
  105.9 10.7 %attend_self.1 = (bf16[128,768]{1,0:T(8,128)(2,1)S(1)}, f32[6,8,256]{2,1,0:T(8,128)S(1)}) custom-call(s32[2,32]{1,0:T(2,128)S(1)} %compare_select_fusion.1.refs_0_, bf16[128,768]{1,0:T(8,128)(2,1)S(1)} %copy-done.7, bf16[16,2,128,768]{3,2,1,0:T(8,128)(2,1)} %get-tuple-element.74.refs_2_.refs_3_.refs_4_, ...), custom_call_target="tpu_custom_call" | custom-call | flops 1000000000 | bytes 10000000 | tf_op jit(solution)/shard_map/attend_self/pallas_call | solution.py:1014
  116.7 1.8 multiply_reduce_fusion.5
  118.7 1.7 convolution_convert_fusion.5.refs_0_
  120.4 5.9 %attend_cross.1 = (bf16[128,768]{1,0:T(8,128)(2,1)S(1)}, f32[6,8,256]{2,1,0:T(8,128)S(1)}) custom-call(bf16[128,768]{1,0:T(8,128)(2,1)S(1)} %convolution_convert_fusion.5.refs_0_, bf16[16,2,64,768]{3,2,1,0:T(8,128)(2,1)S(1)} %copy-done, bf16[16,2,64,768]{3,2,1,0:T(8,128)(2,1)S(1)} %copy-done), custom_call_target="tpu_custom_call" | custom-call | flops 1000000000 | bytes 10000000 | tf_op jit(solution)/shard_map/attend_cross/pallas_call | solution.py:1014
  126.4 1.8 multiply_reduce_fusion.4
  130.4 1.6 broadcast_select_fusion.1
  132.1 1.3 pad_maximum_fusion
  133.4 1.5 collective-permute-start
  135.9 5.4 %multiply_reduce_fusion = (f32[768]{0:T(1024)S(1)}, f32[128]{0:T(128)S(1)}, f32[128,768]{1,0:T(8,128)S(1)}) fusion(f32[128,768]{1,0:T(8,128)S(1)} %get-tuple-element.156, f32[128]{0:T(128)S(1)} %add_rsqrt_fusion, f32[768]{0:T(1024)S(1)} %mul.231, bf16[768,4096]{1,0:T(8,128)(2,1)} %bitcast.72, bf16[128,2048]{1,0:T(8,128)(2,1)} %copy-done.29, ...), kind=kOutput, calls=%fused_computation.65 | convolution fusion | flops 807992448 | bytes 8133632 | tf_op jit(solution)/shard_map/dot_general | solution.py:878
  141.6 1.9 convolution_convert_fusion.4.refs_3_
  143.4 3.2 fusion.5
  152.6 1.4 constant_dynamic-slice_fusion.5
  154.9 1.3 constant_dynamic-slice_fusion.4
  156.2 8.2 %attend_cross_back.1 = (bf16[128,768]{1,0:T(8,128)(2,1)S(1)}, bf16[16,2,64,768]{3,2,1,0:T(8,128)(2,1)S(1)}) custom-call(bf16[128,768]{1,0:T(8,128)(2,1)S(1)} %convolution_convert_fusion.5.refs_0_, bf16[16,2,64,768]{3,2,1,0:T(8,128)(2,1)} %get-tuple-element.78.refs_1_.refs_2_, bf16[16,2,64,768]{3,2,1,0:T(8,128)(2,1)} %get-tuple-element.78.refs_1_.refs_2_, ...), custom_call_target="tpu_custom_call" | custom-call | flops 1000 | bytes 1000 | tf_op jit(solution)/shard_map/attend_cross_back/pallas_call | solution.py:1051
  164.5 2.9 multiply_reduce_fusion.1
  167.5 1.5 collective-permute-start.4
  169.0 2.1 collective-permute-start.2
  172.2 1.8 convolution_convert_fusion.3.refs_5_
  174.0 4.6 %collective-permute-done.3 = bf16[4,128,384]{2,1,0:T(8,128)(2,1)} collective-permute-done((bf16[4,128,384]{2,1,0:T(8,128)(2,1)}, bf16[4,128,384]{2,1,0:T(8,128)(2,1)}, u32[]{:S(2)}, u32[]{:S(2)}) %collective-permute-start.3) | collective-permute-done | bytes 393248 | tf_op jit(solution)/shard_map/ppermute | solution.py:1136
  178.6 1.3 collective-permute-done.4
  179.9 13.7 %attend_self_back.1 = (bf16[128,768]{1,0:T(8,128)(2,1)S(1)}, bf16[16,2,128,768]{3,2,1,0:T(8,128)(2,1)}, f32[12,3,64,128]{3,2,1,0:T(8,128)S(1)}) custom-call(s32[2,32]{1,0:T(2,128)S(1)} %compare_select_fusion.1.refs_0_, s32[2,3]{1,0:T(2,128)S(1)} %copy.48.refs_1_, bf16[128,768]{1,0:T(8,128)(2,1)S(1)} %copy-done.8, ...), custom_call_target="tpu_custom_call" | custom-call | flops 1000 | bytes 1000 | tf_op jit(solution)/shard_map/attend_self_back/pallas_call | solution.py:1051
  193.6 1.8 collective-permute-done.1
  196.7 1.4 slice_add_fusion
  198.1 1.7 reshape.198
  201.7 2.7 fusion.6.refs_15_
  204.8 3.2 maximum_add_fusion.refs_8_
  208.1 2.2 maximum_add_fusion.1.refs_9_
  211.0 118.3 %finish_gradients.1 = (bf16[8,2,144,384]{3,2,1,0:T(8,128)(2,1)}, bf16[8,2,48,384]{3,2,1,0:T(8,128)(2,1)}, f32[16,128]{1,0:T(8,128)}, f32[128,768]{1,0:T(8,128)}, f32[64,768]{1,0:T(8,128)}) custom-call(bf16[128,768]{1,0:T(8,128)(2,1)} %copy-done.5, bf16[128,768]{1,0:T(8,128)(2,1)} %copy-done.24, bf16[128,768]{1,0:T(8,128)(2,1)} %copy-done.10, ...), custom_call_target="tpu_custom_call" | custom-call | tf_op jit(solution)/shard_map/finish_gradients/pallas_call | solution.py:798
  329.3 1.3 slice_bitcast_fusion
  331.9 1.5 copy-done.4
  334.4 2.2 unpack.1
  (144 shorter events, 30.3 us)
Async XLA Ops:
  0.7 97.5 %copy-start.32 = (s32[16]{0:T(128)S(1)}, s32[16]{0:T(128)}, u32[]{:S(2)}) copy-start(s32[16]{0:T(128)} %param.23) | copy-start | bytes 196
  0.7 99.7 %copy-start.33 = (s32[128]{0:T(128)S(1)}, s32[128]{0:T(128)}, u32[]{:S(2)}) copy-start(s32[128]{0:T(128)} %param.24) | copy-start | bytes 1540
  105.1 23.2 %slice-start = ((s8[6291456]{0:T(1024)(128)(4,1)}), s8[4194304]{0:T(1024)(128)(4,1)S(1)}, s32[]{:S(2)}) async-start(s8[6291456]{0:T(1024)(128)(4,1)} %bitcast.73), calls=%async_computation | async-start | bytes 8388608
  105.6 11.0 %copy-start.1 = (f32[12,5,64,128]{3,2,1,0:T(8,128)}, f32[12,5,64,128]{3,2,1,0:T(8,128)S(1)}, u32[]{:S(2)}) copy-start(f32[12,5,64,128]{3,2,1,0:T(8,128)S(1)} %maximum_maximum_fusion.refs_4_.refs_7_) | copy-start | bytes 5898244
  105.9 10.8 %copy-start.26 = (bf16[1,128,768]{2,1,0:T(8,128)(2,1)S(1)}, bf16[1,128,768]{2,1,0:T(8,128)(2,1)}, u32[]{:S(2)}) copy-start(bf16[1,128,768]{2,1,0:T(8,128)(2,1)} %param.20) | copy-start | bytes 589828
  105.9 22.4 %slice-start.1 = ((s8[6291456]{0:T(1024)(128)(4,1)}), s8[2097152]{0:T(1024)(128)(4,1)S(1)}, s32[]{:S(2)}) async-start(s8[6291456]{0:T(1024)(128)(4,1)} %bitcast.73), calls=%async_computation.1 | async-start | bytes 4194304
  116.7 3.7 %copy-start.10 = (bf16[128,768]{1,0:T(8,128)(2,1)}, bf16[128,768]{1,0:T(8,128)(2,1)S(1)}, u32[]{:S(2)}) copy-start(bf16[128,768]{1,0:T(8,128)(2,1)S(1)} %get-tuple-element.76.refs_2_) | copy-start | bytes 589828
  116.7 3.7 %copy-start.12 = (f32[6,8,256]{2,1,0:T(8,128)}, f32[6,8,256]{2,1,0:T(8,128)S(1)}, u32[]{:S(2)}) copy-start(f32[6,8,256]{2,1,0:T(8,128)S(1)} %get-tuple-element.96.refs_6_) | copy-start | bytes 147460
  116.7 3.7 %copy-start = (bf16[16,2,64,768]{3,2,1,0:T(8,128)(2,1)S(1)}, bf16[16,2,64,768]{3,2,1,0:T(8,128)(2,1)}, u32[]{:S(2)}) copy-start(bf16[16,2,64,768]{3,2,1,0:T(8,128)(2,1)} %get-tuple-element.78.refs_1_.refs_2_) | copy-start | bytes 9437188
  118.7 7.6 %copy-start.24 = (bf16[128,768]{1,0:T(8,128)(2,1)}, bf16[128,768]{1,0:T(8,128)(2,1)S(1)}, u32[]{:S(2)}) copy-start(bf16[128,768]{1,0:T(8,128)(2,1)S(1)} %multiply_convert_fusion.3.refs_1_) | copy-start | bytes 589828
  126.4 3.0 copy-start.5
  126.4 3.0 copy-start.14
  133.4 13.3 %collective-permute-start = (bf16[128,5248]{1,0:T(8,128)(2,1)}, bf16[128,5248]{1,0:T(8,128)(2,1)}, u32[]{:S(2)}, u32[]{:S(2)}) collective-permute-start(bf16[128,5248]{1,0:T(8,128)(2,1)} %pad_maximum_fusion), channel_id=1, source_target_pairs={{0,8},{1,9},{2,10},{3,11},{4,12},{5,13},{6,14},{7,15},{8,0},{9,1},... | collective-permute-start | bytes 4030472 | tf_op jit(solution)/shard_map/ppermute | solution.py:1136
  141.3 5.4 %copy-start.22 = (f32[128,768]{1,0:T(8,128)}, f32[128,768]{1,0:T(8,128)S(1)}, u32[]{:S(2)}) copy-start(f32[128,768]{1,0:T(8,128)S(1)} %get-tuple-element.157) | copy-start | bytes 1179652
  141.5 5.1 %copy-start.25 = (bf16[128,768]{1,0:T(8,128)(2,1)}, bf16[128,768]{1,0:T(8,128)(2,1)S(1)}, u32[]{:S(2)}) copy-start(bf16[128,768]{1,0:T(8,128)(2,1)S(1)} %fusion.77.refs_4_) | copy-start | bytes 589828
  153.9 2.3 copy-start.15
  164.4 7.6 %copy-start.3 = (bf16[16,2,64,768]{3,2,1,0:T(8,128)(2,1)}, bf16[16,2,64,768]{3,2,1,0:T(8,128)(2,1)S(1)}, u32[]{:S(2)}) copy-start(bf16[16,2,64,768]{3,2,1,0:T(8,128)(2,1)S(1)} %get-tuple-element.108) | copy-start | bytes 9437188
  164.5 7.6 %copy-start.11 = (bf16[128,768]{1,0:T(8,128)(2,1)}, bf16[128,768]{1,0:T(8,128)(2,1)S(1)}, u32[]{:S(2)}) copy-start(bf16[128,768]{1,0:T(8,128)(2,1)S(1)} %get-tuple-element.85.refs_5_) | copy-start | bytes 589828
  164.5 6.6 %copy-start.23 = (f32[128,768]{1,0:T(8,128)S(1)}, f32[128,768]{1,0:T(8,128)}, u32[]{:S(2)}) copy-start(f32[128,768]{1,0:T(8,128)} %copy-done.22) | copy-start | bytes 1179652
  167.4 12.5 %copy-start.2 = (f32[12,5,64,128]{3,2,1,0:T(8,128)S(1)}, f32[12,5,64,128]{3,2,1,0:T(8,128)}, u32[]{:S(2)}) copy-start(f32[12,5,64,128]{3,2,1,0:T(8,128)} %copy-done.1) | copy-start | bytes 5898244
  167.4 12.5 %copy-start.8 = (bf16[128,768]{1,0:T(8,128)(2,1)S(1)}, bf16[128,768]{1,0:T(8,128)(2,1)}, u32[]{:S(2)}) copy-start(bf16[128,768]{1,0:T(8,128)(2,1)} %get-tuple-element.73.refs_1_.refs_2_) | copy-start | bytes 589828
  167.4 12.5 %copy-start.13 = (f32[6,8,256]{2,1,0:T(8,128)S(1)}, f32[6,8,256]{2,1,0:T(8,128)}, u32[]{:S(2)}) copy-start(f32[6,8,256]{2,1,0:T(8,128)} %copy-done.12) | copy-start | bytes 147460
  167.4 11.1 %collective-permute-start.3 = (bf16[4,128,384]{2,1,0:T(8,128)(2,1)}, bf16[4,128,384]{2,1,0:T(8,128)(2,1)}, u32[]{:S(2)}, u32[]{:S(2)}) collective-permute-start(bf16[4,128,384]{2,1,0:T(8,128)(2,1)} %get-tuple-element.90), channel_id=1, source_target_pairs={{0,4},{1,5},{2,6},{3,7},{4,0},{5,1},{6,2},{7,3},{8,12},{9,13},{10,... | collective-permute-start | bytes 1179656 | tf_op jit(solution)/shard_map/ppermute | solution.py:1136
  167.5 12.3 %collective-permute-start.4 = (bf16[4,128,384]{2,1,0:T(8,128)(2,1)}, bf16[4,128,384]{2,1,0:T(8,128)(2,1)}, u32[]{:S(2)}, u32[]{:S(2)}) collective-permute-start(bf16[4,128,384]{2,1,0:T(8,128)(2,1)} %get-tuple-element.91), channel_id=1, source_target_pairs={{0,20},{1,21},{2,22},{3,23},{4,16},{5,17},{6,18},{7,19},{8,28},{9,... | collective-permute-start | bytes 1179656 | tf_op jit(solution)/shard_map/ppermute | solution.py:1136
  169.0 26.4 %collective-permute-start.1 = (bf16[4,48,2048]{2,1,0:T(8,128)(2,1)}, bf16[4,48,2048]{2,1,0:T(8,128)(2,1)}, u32[]{:S(2)}, u32[]{:S(2)}) collective-permute-start(bf16[4,48,2048]{2,1,0:T(8,128)(2,1)} %get-tuple-element.87), channel_id=1, source_target_pairs={{0,4},{1,5},{2,6},{3,7},{4,0},{5,1},{6,2},{7,3},{8,12},{9,13},{10,... | collective-permute-start | bytes 2359304 | tf_op jit(solution)/shard_map/ppermute | solution.py:1136
  169.0 27.7 %collective-permute-start.2 = (bf16[4,48,2048]{2,1,0:T(8,128)(2,1)}, bf16[4,48,2048]{2,1,0:T(8,128)(2,1)}, u32[]{:S(2)}, u32[]{:S(2)}) collective-permute-start(bf16[4,48,2048]{2,1,0:T(8,128)(2,1)} %get-tuple-element.88), channel_id=1, source_target_pairs={{0,20},{1,21},{2,22},{3,23},{4,16},{5,17},{6,18},{7,19},{8,28},{9,... | collective-permute-start | bytes 2359304 | tf_op jit(solution)/shard_map/ppermute | solution.py:1136
  172.1 21.5 %copy-start.27 = (bf16[128,768]{1,0:T(8,128)(2,1)}, bf16[128,768]{1,0:T(8,128)(2,1)S(1)}, u32[]{:S(2)}) copy-start(bf16[128,768]{1,0:T(8,128)(2,1)S(1)} %get-tuple-element.137.refs_6_) | copy-start | bytes 589828
  193.6 8.1 %copy-start.6 = (bf16[128,768]{1,0:T(8,128)(2,1)}, bf16[128,768]{1,0:T(8,128)(2,1)S(1)}, u32[]{:S(2)}) copy-start(bf16[128,768]{1,0:T(8,128)(2,1)S(1)} %get-tuple-element.100.refs_7_) | copy-start | bytes 589828
  196.7 3.1 copy-start.17
  201.7 3.2 copy-start.18
  204.8 3.2 copy-start.20
  334.4 3.0 copy-start.31
  (9 other events, 12.6 us)
